TPU v7x, 256 devices: a whole 4x4x8 slice. The times are simulated.
256 devices in a mesh: section: 16 (over z_lo, y), dp: 16 (over z_hi, x, core).
Axes of the slice: x: 4, y: 4, z: 8 (z_hi: 2, z_lo: 4; z = z_hi * 4 + z_lo), core: 2. Of those that a mesh axis runs over, the one named last changes fastest.
Arguments:
- inputs: bfloat16 [2048, 4096], P('dp', 'section'), may hold values from -0.3125 to 0.3125
- norm_gain: float32 [4096], P('section'), may hold values from 0.25 to 1.75
- router: bfloat16 [4096, 8], P('section'), may hold values from -0.09375 to 0.09375
- w_in: bfloat16 [16, 4096, 2, 6144], P('dp', None, None, 'section'), may hold values from -0.09375 to 0.09375
- w_out: bfloat16 [16, 6144, 4096], P('dp', 'section'), may hold values from -0.0546875 to 0.0546875
- routes: int32 [2048, 2], P('dp'), may hold values from 0 to 7, all different within a row; in each aligned block of 128 rows (0 to 127, 128 to 255, ...) at most 40 rows name the same one
Outputs:
- hiddens: bfloat16 [2048, 4096], P('dp', 'section')
Inputs may be any that keep to these rules, and one draw needn't show every extreme that they name: `routes`: among the tokens of one index of dp (aligned blocks of 128 rows), no expert is named more than 40 times, a bound that some block reaches; a token's two experts differ.
All inputs are finite; a program needn't handle non-finite values.
Results may differ from a plain program's by a relative error of at most 0.0067.
Values may be sent and summed in bfloat16 or wider, within the bound.
No kernel may reach another device: no remote copies, remote signals or barrier semaphores. Data moves between devices by JAX's collectives and lax.ppermute only.
A program may use at most 128 MiB of HBM per device.

v0:
```python
import jax
import jax.numpy as jnp
from jax import lax
from jax.sharding import PartitionSpec as P


def slots_of(id_table, experts):
    flat_ids = id_table.reshape(-1)
    onehot = (flat_ids[:, None] == jnp.arange(experts, dtype=jnp.int32)[None, :]).astype(jnp.int32)
    ranked = jnp.cumsum(onehot, axis=0) - onehot
    return (flat_ids, jnp.sum(ranked * onehot, axis=1))


def local(inputs, norm_gain, router, w_in, w_out, routes):
    sections = lax.axis_size("section")
    tokens = inputs.shape[0]
    local_width = inputs.shape[1]
    experts = router.shape[1]
    capacity = min(tokens, 5 * tokens // (2 * experts))
    half_units = w_out.shape[1]
    w_rows = w_in[0].reshape(w_in.shape[1], 2 * half_units)
    w_down = w_out[0]
    acts_f32 = inputs.astype(jnp.float32)
    square_sum = lax.psum(jnp.sum(acts_f32 * acts_f32, axis=1), "section")
    mean_square = square_sum[:, None] / (local_width * sections)
    normed = (acts_f32 * lax.rsqrt(mean_square + 1e-05) * norm_gain).astype(jnp.bfloat16)
    logits = lax.psum(jnp.dot(normed, router, preferred_element_type=jnp.float32), "section")
    gate_probs = jax.nn.softmax(jnp.take_along_axis(logits, routes, axis=1), axis=1)
    expert_ids, slot_ids = slots_of(routes, experts)
    dup_rows = jnp.repeat(normed, 2, axis=0)
    buffer = (
        jnp.zeros((experts, capacity, local_width), jnp.bfloat16)
        .at[expert_ids, slot_ids]
        .set(dup_rows)
    )
    outgoing = jnp.repeat(buffer, 2, axis=0)
    received = lax.all_to_all(outgoing, "dp", split_axis=0, concat_axis=0, tiled=True)
    row_count = received.shape[0] * received.shape[1]
    shaped = received.reshape(row_count, local_width)
    projection = jnp.dot(
        lax.all_gather(shaped, "section", axis=1, tiled=True),
        w_rows,
        preferred_element_type=jnp.float32,
    )
    hidden_act = (jax.nn.silu(projection[:, :half_units]) * projection[:, half_units:]).astype(
        jnp.bfloat16
    )
    summed = lax.psum_scatter(
        lax.dot_general(
            w_down, hidden_act, (((0,), (1,)), ((), ())), preferred_element_type=jnp.float32
        ),
        "section",
        scatter_dimension=0,
        tiled=True,
    )
    answered = summed.T.reshape(received.shape[0], received.shape[1], local_width)
    returned = lax.all_to_all(answered, "dp", split_axis=0, concat_axis=0, tiled=True)
    summed_pairs = returned.reshape(experts, 2, capacity, local_width).sum(axis=1)
    picked = summed_pairs[expert_ids, slot_ids].reshape(tokens, 2, local_width)
    mixed_out = jnp.sum(gate_probs[..., None] * picked, axis=1)
    return (acts_f32 + mixed_out).astype(jnp.bfloat16)


def solution(mesh):
    return jax.shard_map(
        local,
        mesh=mesh,
        in_specs=(
            P("dp", "section"),
            P("section"),
            P("section", None),
            P("dp", None, None, "section"),
            P("dp", "section", None),
            P("dp", None),
        ),
        out_specs=P("dp", "section"),
        check_vma=False,
    )
```

profile of v0, /device:TPU:4, one launch (start us, length us, event | category | flops | bytes accessed | tf_op | source)
XLA Modules:
  0.0 390.3 jit_solution(3629799733325090047)
XLA Ops:
  6.5 0.0 copy-start
  6.5 0.0 all-gather.2.cloned.1.call-start
  6.5 0.9 copy.19
  7.5 0.1 eq.29
  7.6 0.1 eq.25
  7.8 0.1 reshape.114
  7.9 0.9 fusion.4
  8.8 44.9 %psum.14 = f32[128]{0:T(128)S(1)} all-reduce(f32[128]{0:T(128)S(1)} %fusion.4), channel_id=1, replica_groups=mesh['section'=16,'dp'=16] {'section'}, use_global_device_ids=true, to_apply=%region_1.0 | all-reduce | flops 128 | bytes 1024 | tf_op jit(solution)/shard_map/psum | solution.py:24
  53.7 0.6 reduce-window.6
  54.3 0.2 slice_reduce_fusion
  54.6 0.9 fusion.6
  55.5 0.1 broadcast_in_dim.12
  55.6 0.1 reshape.136
  55.7 0.1 fusion.9
  55.8 13.2 %scatter_fusion = bf16[8,40,256]{2,1,0:T(8,128)(2,1)S(1)} fusion(bf16[8,40,256]{2,1,0:T(8,128)(2,1)S(1)} %broadcast_in_dim.11, s32[256]{0:T(256)S(1)} %bitcast.36, bf16[256,256]{1,0:T(8,128)(2,1)S(1)} %reshape.136), kind=kCustom, calls=%fused_computation.2 | custom fusion | bytes 395264 | tf_op jit(solution)/shard_map/scatter | solution.py:34
  69.1 18.0 %all_to_all.10 = bf16[16,40,256]{2,1,0:T(8,128)(2,1)} all-to-all(bf16[16,40,256]{2,1,0:T(8,128)(2,1)S(1)} %bitcast.40), channel_id=1, replica_groups=mesh['section'=16,'dp'=16] {'dp'}, dimensions={0} | all-to-all | bytes 655360 | tf_op jit(solution)/shard_map/all_to_all | solution.py:37
  87.1 0.0 all-gather.2.cloned.1.call-update
  87.1 0.0 reduce-scatter.2.cloned.1.call-start
  87.1 6.5 %copy.22 = bf16[512,8,2,384]{3,1,2,0:T(8,128)(2,1)} copy(bf16[512,8,2,384]{3,2,1,0:T(2,128)(2,1)} %bitcast.37) | data formatting | bytes 12582912
  93.7 87.4 %all-gather.2.cloned.1.call-done = bf16[640,4096]{1,0:T(8,128)(2,1)} async-done(((bf16[640,256]{1,0:T(8,128)(2,1)}), bf16[640,4096]{1,0:T(8,128)(2,1)}) %all-gather.2.cloned.1.call-update) | async-done | bytes 5242896 | tf_op jit(solution)/shard_map/all_gather | solution.py:41
  181.0 8.0 %fusion.18 = f32[640,768]{1,0:T(8,128)S(1)} fusion(bf16[640,4096]{1,0:T(8,128)(2,1)} %all-gather.2.cloned.1.call-done, bf16[4096,768]{1,0:T(8,128)(2,1)} %bitcast.38), kind=kOutput, calls=%fused_computation.40 | convolution fusion | flops 4026531840 | bytes 13500416 | tf_op jit(solution)/shard_map/dot_general | solution.py:40
  189.0 0.0 copy-done
  189.0 5.5 %convolution_bitcast_fusion = f32[4096,640]{0,1:T(8,128)} fusion(bf16[1,384,4096]{2,1,0:T(8,128)(2,1)S(1)} %copy-done, f32[640,768]{1,0:T(8,128)S(1)} %fusion.18), kind=kOutput, calls=%fused_computation.3 | convolution fusion | flops 2014740480 | bytes 15597568 | tf_op jit(solution)/shard_map/dot_general | solution.py:49
  194.6 0.0 copy-start.2
  194.6 0.0 copy-start.3
  194.6 0.0 reduce-scatter.2.cloned.1.call-update
  194.6 126.0 %reduce-scatter.2.cloned.1.call-done = f32[256,640]{0,1:T(8,128)} async-done(((f32[4096,640]{0,1:T(8,128)}), f32[256,640]{0,1:T(8,128)}) %reduce-scatter.2.cloned.1.call-update) | async-done | bytes 655376 | tf_op jit(solution)/shard_map/reduce_scatter | solution.py:48
  320.6 7.3 %all-to-all-start.1 = ((f32[16,40,256]{2,1,0:T(8,128)}), f32[16,40,256]{2,1,0:T(8,128)}, u32[]{:S(2)}, u32[]{:S(2)}) async-start(f32[16,40,256]{2,1,0:T(8,128)} %bitcast.41), calls=%async_computation.2 | async-start | bytes 1310720 | tf_op jit(solution)/shard_map/all_to_all | solution.py:57
  327.9 0.0 copy-done.2
  327.9 0.1 copy.16
  328.0 0.1 reshape.128
  328.1 0.0 copy-done.3
  328.2 0.1 fusion.17
  328.3 45.9 %psum.15 = f32[128,8]{0,1:T(8,128)S(1)} all-reduce(f32[128,8]{0,1:T(8,128)S(1)} %fusion.17), channel_id=1, replica_groups=mesh['section'=16,'dp'=16] {'section'}, use_global_device_ids=true, to_apply=%region_2.0 | all-reduce | flops 1024 | bytes 8192 | tf_op jit(solution)/shard_map/psum | solution.py:27
  374.2 0.0 copy-start.1
  374.2 1.4 gather_fusion.1
  375.6 0.1 reshape.131
  375.7 0.1 copy.17
  375.9 0.8 copy.18
  376.6 0.0 all-to-all-done.1
  376.6 1.2 bitcast_reduce_fusion
  377.8 2.7 gather_fusion
  380.5 1.1 reshape.121
  381.6 1.2 multiply_reduce_fusion
  382.8 0.0 copy-done.1
  382.8 0.6 fusion.7
  (11 shorter events, 0.2 us)
Async XLA Ops:
  6.5 182.5 %copy-start = (bf16[1,384,4096]{2,1,0:T(8,128)(2,1)S(1)}, bf16[1,384,4096]{2,1,0:T(8,128)(2,1)}, u32[]{:S(2)}) copy-start(bf16[1,384,4096]{2,1,0:T(8,128)(2,1)} %param.10) | copy-start | bytes 9437188
  6.5 174.5 %all-gather.2.cloned.1.call-start = ((), (), s32[]{:S(2)}) async-start(), calls=%async_computation.3 | async-start | bytes 5570560 | tf_op jit(solution)/shard_map/all_gather | solution.py:41
  87.1 233.5 %reduce-scatter.2.cloned.1.call-start = ((), (), s32[]{:S(2)}) async-start(), calls=%async_computation.4 | async-start | bytes 11141120 | tf_op jit(solution)/shard_map/reduce_scatter | solution.py:48
  194.6 133.3 %copy-start.2 = (s32[128,2]{0,1:T(2,128)S(1)}, s32[128,2]{0,1:T(2,128)}, u32[]{:S(2)}) copy-start(s32[128,2]{0,1:T(2,128)} %param.11) | copy-start | bytes 3076
  194.6 133.6 %copy-start.3 = (bf16[256,8]{0,1:T(8,128)(2,1)S(1)}, bf16[256,8]{0,1:T(8,128)(2,1)}, u32[]{:S(2)}) copy-start(bf16[256,8]{0,1:T(8,128)(2,1)} %param.8) | copy-start | bytes 12292
  320.6 56.0 %all-to-all-start.1 = ((f32[16,40,256]{2,1,0:T(8,128)}), f32[16,40,256]{2,1,0:T(8,128)}, u32[]{:S(2)}, u32[]{:S(2)}) async-start(f32[16,40,256]{2,1,0:T(8,128)} %bitcast.41), calls=%async_computation.2 | async-start | bytes 1310720 | tf_op jit(solution)/shard_map/all_to_all | solution.py:57
  374.2 8.6 %copy-start.1 = (bf16[128,256]{1,0:T(8,128)(2,1)S(1)}, bf16[128,256]{1,0:T(8,128)(2,1)}, u32[]{:S(2)}) copy-start(bf16[128,256]{1,0:T(8,128)(2,1)} %param.6) | copy-start | bytes 196612
Sparse Core Ops, SparseCore 0:
  87.2 93.7 all-gather.1
  194.7 125.8 reduce-scatter.1
where the time goes:
time: 392 us; the launch traced here: 390 us
  waiting for transfers between devices  213 us (54%)
  blocking collectives  109 us (28%)
  local copies, waits for them, and re-layouts  27.9 us (7%)
  matrix products  13.6 us (3%)
  between operations  13.6 us (3%)
  starting transfers between devices  7.34 us (2%)
  other arithmetic  5.73 us (1%)
    reduce_scatter x1, waiting for transfers between devices, local(): lax.psum_scatter(lax.dot_general(w_down, hidden_act, (((0,), (1,)), ((),...  126 us
    all_gather x1, waiting for transfers between devices, local(): lax.all_gather(shaped, 'section', axis=1, tiled=True)  87.4 us
    psum x1, blocking collectives, local(): lax.psum(jnp.dot(normed, router, preferred_element_type=jnp.float32), 'se...  45.9 us
    psum x1, blocking collectives, local(): square_sum = lax.psum(jnp.sum(acts_f32 * acts_f32, axis=1), 'section')  44.9 us
    all_to_all x1, blocking collectives, local(): lax.all_to_all(outgoing, 'dp', split_axis=0, concat_axis=0, tiled=True)  18 us
    scatter x1, local copies, waits for them, and re-layouts, local(): buffer = jnp.zeros((experts, capacity, local_width), jnp.bfloat16).at[exp...  13.2 us
    dot_general x1, matrix products, local(): jnp.dot(lax.all_gather(shaped, 'section', axis=1, tiled=True), w_rows, pr...  7.99 us
  transfers between devices with their start and end apart: 3, of which 2 were waited for; matrix products, arithmetic and copies ran while one was open for 2% of the time, Pallas kernels for 0%

commit v1 on v0

v1 whole, which is shorter than its diff:
```python
import functools

import jax
import jax.numpy as jnp
from jax import lax
from jax.experimental import pallas as pl
from jax.experimental.pallas import tpu as pltpu
from jax.sharding import PartitionSpec as P

BF16 = jnp.bfloat16
F32 = jnp.float32

NZ, NY, NH, NX = 4, 4, 2, 4


def shift_y(value, step):
    pairs = [(z * NY + y, z * NY + (y + step) % NY) for z in range(NZ) for y in range(NY)]
    return lax.ppermute(value, "section", pairs)


def shift_z(value, step):
    pairs = [(z * NY + y, (z + step) % NZ * NY + y) for z in range(NZ) for y in range(NY)]
    return lax.ppermute(value, "section", pairs)


def xor_section(value, mask):
    return lax.ppermute(value, "section", [(s, s ^ mask) for s in range(NZ * NY)])


def shift_x(value, step):
    pairs = [
        ((h * NX + x) * 2 + c, (h * NX + (x + step) % NX) * 2 + c)
        for h in range(NH)
        for x in range(NX)
        for c in range(2)
    ]
    return lax.ppermute(value, "dp", pairs)


def swap_h(value):
    return lax.ppermute(value, "dp", [(d, d ^ (2 * NX)) for d in range(2 * NX * NH)])


def swap_core(value):
    return lax.ppermute(value, "dp", [(d, d ^ 1) for d in range(2 * NX * NH)])


def expert_kernel(
    place, g0, g1, g2a, g2b, g3, h0, h1, h2a, h2b, h3, w_up, w_down, own, other, rows, total
):
    zl, y = place[0], place[1]
    count = g0.shape[1]
    half = count // 2
    units = w_down.shape[0]
    width = g0.shape[2]
    for base, (p0, p1, p2a, p2b, p3) in ((0, (g0, g1, g2a, g2b, g3)), (count, (h0, h1, h2a, h2b, h3))):
        for d in range(NZ):
            z = (zl + d) % NZ
            for j, piece in ((0, p0), (1, p1), (3, p3)):
                rows[z * NY + (y + j) % NY, base : base + count] = piece[d]
            far = z * NY + (y + 2) % NY
            rows[far, base : base + half] = p2a[d]
            rows[far, base + half : base + count] = p2b[d]
    span = NY * width
    total[...] = jnp.zeros_like(total)

    def project(z, carry):
        left = jnp.concatenate([rows[z * NY + k] for k in range(NY)], axis=1)
        total[...] += jnp.dot(left, w_up[pl.ds(z * span, span), :], preferred_element_type=F32)
        return carry

    lax.fori_loop(0, NZ, project, 0)
    act = (jax.nn.silu(total[:, :units]) * total[:, units:]).astype(BF16)

    def expand(d, carry):
        z = (zl + d) % NZ
        for k in range(NY):
            start = pl.multiple_of(z * span + k * width, width)
            result = jnp.dot(act, w_down[:, pl.ds(start, width)], preferred_element_type=F32)
            j = (k - y + NY) % NY
            own[d, j] = result[:count]
            other[d, j] = result[count:].astype(BF16)
        return carry

    lax.fori_loop(0, NZ, expand, 0)


def expert(place, own_rows, other_rows, w_up, w_down):
    count, width = own_rows[0].shape[1:]
    shape = (NZ, NY, count, width)
    vmem = pl.BlockSpec(memory_space=pltpu.VMEM)
    return pl.pallas_call(
        expert_kernel,
        out_shape=(jax.ShapeDtypeStruct(shape, F32), jax.ShapeDtypeStruct(shape, BF16)),
        in_specs=[pl.BlockSpec(memory_space=pltpu.SMEM)] + [vmem] * 12,
        out_specs=(vmem, vmem),
        scratch_shapes=[
            pltpu.VMEM((NZ * NY, 2 * count, width), BF16),
            pltpu.VMEM((2 * count, w_up.shape[1]), F32),
        ],
        compiler_params=pltpu.CompilerParams(vmem_limit_bytes=48 * 1024 * 1024),
        cost_estimate=pl.CostEstimate(
            flops=6 * 2 * count * w_down.shape[0] * w_down.shape[1],
            bytes_accessed=16 * 1024 * 1024,
            transcendentals=2 * count * w_down.shape[0],
        ),
    )(place, *own_rows, *other_rows, w_up, w_down)


def gather_y(block):
    up = shift_y(block, -1)
    down = shift_y(block, 1)
    half = block.shape[1] // 2
    far_a = shift_y(down[:, :half], 1)
    far_b = shift_y(up[:, half:], -1)
    return block, up, far_a, far_b, down


def scatter_y(parts):
    half = parts.shape[2] // 2
    far_a = shift_y(parts[:, 2, :half].astype(BF16), 1)
    far_b = shift_y(parts[:, 2, half:].astype(BF16), -1)
    to_up = jnp.concatenate([parts[:, 1, :half] + far_a, parts[:, 1, half:]], axis=1).astype(BF16)
    to_down = jnp.concatenate([parts[:, 3, :half], parts[:, 3, half:] + far_b], axis=1).astype(BF16)
    return parts[:, 0] + shift_y(to_up, 1).astype(F32) + shift_y(to_down, -1).astype(F32)


def local(inputs, norm_gain, router, w_in, w_out, routes):
    sections = lax.axis_size("section")
    tokens, width = inputs.shape
    experts = router.shape[1]
    capacity = min(tokens, 5 * tokens // (2 * experts))
    units = w_out.shape[1]
    model = w_in.shape[1]
    section = lax.axis_index("section")
    dp = lax.axis_index("dp")
    zl, y = section // NY, section % NY
    zh, x = dp // (2 * NX), dp // 2 % NX
    w_up = w_in[0].reshape(model, 2 * units)
    w_down = w_out[0]

    acts = inputs.astype(F32)
    scaled = (acts * norm_gain).astype(BF16)
    partial_logits = lax.dot_general(
        router, scaled, (((0,), (1,)), ((), ())), preferred_element_type=F32
    )
    square = jnp.sum(acts * acts, axis=1)[None, :]
    sums = jnp.concatenate([square, partial_logits, jnp.zeros((7, tokens), F32)], axis=0)
    for mask in (1, 2, NY, 2 * NY):
        sums = sums + xor_section(sums, mask)
    inv = lax.rsqrt(sums[0] / model + 1e-05)
    logits = (sums[1 : 1 + experts] * inv[None, :]).T
    normed = (acts * inv[:, None] * norm_gain).astype(BF16)

    near = jnp.arange(experts, dtype=jnp.int32)
    names = (zh ^ (near // NX)) * NX + (x + near % NX) % NX
    hits = (routes[:, :, None] == names[None, None, :]).astype(F32)
    chosen = jnp.sum(hits, axis=1)
    earlier = (jnp.arange(tokens)[:, None] > jnp.arange(tokens)[None, :]).astype(F32)
    rank = jnp.dot(earlier, chosen, preferred_element_type=F32)
    slots = jnp.arange(capacity, dtype=F32)
    picks = chosen.T[:, None, :] * (rank.T[:, None, :] == slots[None, :, None]).astype(F32)
    picks = picks.reshape(experts * capacity, tokens)
    sent = jnp.dot(picks.astype(BF16), normed, preferred_element_type=F32).astype(BF16)
    sent = sent.reshape(NH, NX, capacity, width)

    crossed = jnp.stack([sent[0], swap_h(sent[1])], axis=1)
    arrived = [crossed[0]] + [shift_x(crossed[k], k) for k in range(1, NX)]
    mine = jnp.stack(arrived).reshape(experts * capacity, width)
    blocks = jnp.stack([mine] + [shift_z(mine, -d) for d in range(1, NZ)])
    own_rows = gather_y(blocks)
    other_rows = [swap_core(piece) for piece in own_rows]
    own, other = expert(jnp.stack([zl, y]).astype(jnp.int32), own_rows, other_rows, w_up, w_down)

    parts = own + swap_core(other).astype(F32)
    column = scatter_y(parts)
    full = column[0]
    for d in range(1, NZ):
        full = full + shift_z(column[d].astype(BF16), d).astype(F32)
    full = full.astype(BF16).reshape(NX, NH, capacity, width)
    back = jnp.stack([full[0]] + [shift_x(full[k], -k) for k in range(1, NX)])
    back = jnp.stack([back[:, 0], swap_h(back[:, 1])]).reshape(experts * capacity, width)

    named = (routes[:, :, None] == near[None, None, :]).astype(F32)
    pair = jnp.sum(named * logits[:, None, :], axis=2)
    gates = jax.nn.softmax(pair, axis=1)
    gate_of = jnp.sum(hits * gates[:, :, None], axis=1)
    weight = jnp.repeat(gate_of.T, capacity, axis=0) * picks
    high = weight.astype(BF16)
    low = (weight - high.astype(F32)).astype(BF16)
    mix = lambda w: lax.dot_general(w, back, (((0,), (0,)), ((), ())), preferred_element_type=F32)
    return (acts + (mix(high) + mix(low))).astype(BF16)


def solution(mesh):
    return jax.shard_map(
        local,
        mesh=mesh,
        in_specs=(
            P("dp", "section"),
            P("section"),
            P("section", None),
            P("dp", None, None, "section"),
            P("dp", "section", None),
            P("dp", None),
        ),
        out_specs=P("dp", "section"),
        check_vma=False,
    )
```

time: 392 us -> 172 us (0.44)
  waiting for transfers between devices: 213 us -> 82.4 us
  blocking collectives: 109 us -> 0 us
  starting transfers between devices: 7.34 us -> 54.2 us
  local copies, waits for them, and re-layouts: 27.9 us -> 6.99 us
  Pallas kernels: 0 us -> 16.5 us
  between operations: 13.6 us -> 0.24 us
  matrix products: 13.6 us -> 3.29 us
    reduce_scatter x1 -> x0, waiting for transfers between devices: 126 us -> none  [local(): lax.psum_scatter(lax.dot_general(w_down, hidden_act, (((0,), (1,)), ((),...]
    psum x2 -> x0, blocking collectives: 90.8 us -> none  [the longest x1 45.9 us: local(): lax.psum(jnp.dot(normed, router, preferred_element_type=jnp.float32), 'se...]
    all_gather x1 -> x0, waiting for transfers between devices: 87.4 us -> none  [local(): lax.all_gather(shaped, 'section', axis=1, tiled=True)]
    ppermute x0 -> x32, waiting for transfers between devices: none -> 82.4 us  [the longest x8 38.5 us: shift_y(): return lax.ppermute(value, 'section', pairs)]
    ppermute x0 -> x32, starting transfers between devices: none -> 54.2 us  [the longest x8 13.4 us: shift_y(): return lax.ppermute(value, 'section', pairs)]
    all_to_all x1 -> x0, blocking collectives: 18 us -> none  [local(): lax.all_to_all(outgoing, 'dp', split_axis=0, concat_axis=0, tiled=True)]
    pallas_call x0 -> x1, Pallas kernels: none -> 16.5 us  [expert(): pl.pallas_call(expert_kernel, out_shape=(jax.ShapeDtypeStruct(shape, F32)...]
    scatter x1 -> x0, local copies, waits for them, and re-layouts: 13.2 us -> none  [local(): buffer = jnp.zeros((experts, capacity, local_width), jnp.bfloat16).at[exp...]
  transfers between devices with their start and end apart: 3 -> 32, of which waited for: 2 -> 19; matrix products, arithmetic and copies ran while one was open for 2% -> 4% of each run, Pallas kernels for 0% -> 0%
where the time goes in v1:
time: 172 us; the launch traced here: 170 us
  waiting for transfers between devices  82.4 us (48%)
  starting transfers between devices  54.2 us (32%)
  Pallas kernels  16.5 us (10%)
  local copies, waits for them, and re-layouts  6.99 us (4%)
  other arithmetic  6.85 us (4%)
  matrix products  3.29 us (2%)
    ppermute x8, waiting for transfers between devices, shift_y(): return lax.ppermute(value, 'section', pairs)  38.5 us
    ppermute x6, waiting for transfers between devices, shift_z(): return lax.ppermute(value, 'section', pairs)  17.1 us
    pallas_call x1, Pallas kernels, expert(): pl.pallas_call(expert_kernel, out_shape=(jax.ShapeDtypeStruct(shape, F32)...  16.5 us
    ppermute x8, starting transfers between devices, shift_y(): return lax.ppermute(value, 'section', pairs)  13.4 us
    ppermute x2, starting transfers between devices, swap_h(): lax.ppermute(value, 'dp', [(d, d ^ 2 * NX) for d in range(2 * NX * NH)])  11.5 us
    ppermute x4, starting transfers between devices, xor_section(): lax.ppermute(value, 'section', [(s, s ^ mask) for s in range(NZ * NY)])  9.99 us
    ppermute x6, starting transfers between devices, shift_z(): return lax.ppermute(value, 'section', pairs)  9.8 us
    ppermute x6, starting transfers between devices, shift_x(): return lax.ppermute(value, 'dp', pairs)  8.4 us
  transfers between devices with their start and end apart: 32, of which 19 were waited for; matrix products, arithmetic and copies ran while one was open for 4% of the time, Pallas kernels for 0%

profile of v1, /device:TPU:4, one launch (start us, length us, event | category | flops | bytes accessed | tf_op | source)
XLA Modules:
  0.0 170.4 jit_solution(9984713682007523915)
XLA Ops:
  0.0 1.0 fusion.14
  1.0 1.0 convolution_bitcast_fusion
  2.0 0.1 pad.24.clone
  2.1 1.6 collective-permute-start
  3.7 2.1 %collective-permute-done = f32[16,128]{1,0:T(8,128)S(1)} collective-permute-done((f32[16,128]{1,0:T(8,128)S(1)}, f32[16,128]{1,0:T(8,128)S(1)}, u32[]{:S(2)}, u32[]{:S(2)}) %collective-permute-start) | collective-permute-done | bytes 8224 | tf_op jit(solution)/shard_map/ppermute | solution.py:27
  5.8 3.2 %collective-permute-start.1 = (f32[16,128]{1,0:T(8,128)S(1)}, f32[16,128]{1,0:T(8,128)S(1)}, u32[]{:S(2)}, u32[]{:S(2)}) collective-permute-start(f32[16,128]{1,0:T(8,128)S(1)} %fusion.43), channel_id=1, source_target_pairs={{0,32},{16,48},{32,0},{48,16},{64,96},{80,112},{96,64},{112,80},{1... | collective-permute-start | bytes 24584 | tf_op jit(solution)/shard_map/ppermute | solution.py:27
  9.1 2.0 %collective-permute-done.1 = f32[16,128]{1,0:T(8,128)S(1)} collective-permute-done((f32[16,128]{1,0:T(8,128)S(1)}, f32[16,128]{1,0:T(8,128)S(1)}, u32[]{:S(2)}, u32[]{:S(2)}) %collective-permute-start.1) | collective-permute-done | bytes 8224 | tf_op jit(solution)/shard_map/ppermute | solution.py:27
  11.0 1.9 %collective-permute-start.2 = (f32[16,128]{1,0:T(8,128)S(1)}, f32[16,128]{1,0:T(8,128)S(1)}, u32[]{:S(2)}, u32[]{:S(2)}) collective-permute-start(f32[16,128]{1,0:T(8,128)S(1)} %add.111), channel_id=1, source_target_pairs={{0,64},{16,80},{32,96},{48,112},{64,0},{80,16},{96,32},{112,48},{1... | collective-permute-start | bytes 24584 | tf_op jit(solution)/shard_map/ppermute | solution.py:27
  13.0 1.7 %collective-permute-done.2 = f32[16,128]{1,0:T(8,128)S(1)} collective-permute-done((f32[16,128]{1,0:T(8,128)S(1)}, f32[16,128]{1,0:T(8,128)S(1)}, u32[]{:S(2)}, u32[]{:S(2)}) %collective-permute-start.2) | collective-permute-done | bytes 8224 | tf_op jit(solution)/shard_map/ppermute | solution.py:27
  14.7 3.3 %collective-permute-start.3 = (f32[16,128]{1,0:T(8,128)S(1)}, f32[16,128]{1,0:T(8,128)S(1)}, u32[]{:S(2)}, u32[]{:S(2)}) collective-permute-start(f32[16,128]{1,0:T(8,128)S(1)} %add.112), channel_id=1, source_target_pairs={{0,128},{16,144},{32,160},{48,176},{64,192},{80,208},{96,224},{112... | collective-permute-start | bytes 24584 | tf_op jit(solution)/shard_map/ppermute | solution.py:27
  18.0 0.1 eq.78
  18.1 1.5 collective-permute-done.3
  19.6 0.7 select_reduce_fusion
  20.4 0.8 fusion.30
  21.1 0.1 fusion.23
  21.3 0.1 fusion.12
  21.4 1.1 convolution_convert_fusion
  22.5 6.9 %collective-permute-start.4 = (bf16[4,40,256]{2,1,0:T(8,128)(2,1)S(1)}, bf16[4,40,256]{2,1,0:T(8,128)(2,1)S(1)}, u32[]{:S(2)}, u32[]{:S(2)}) collective-permute-start(bf16[4,40,256]{2,1,0:T(8,128)(2,1)S(1)} %bitcast.126), channel_id=1, source_target_pairs={{0,8},{1,9},{2,10},{3,11},{4,12},{5,13},{6,14},{7,15},{8,0},{9,1},... | collective-permute-start | bytes 245768 | tf_op jit(solution)/shard_map/ppermute | solution.py:41
  29.5 2.5 %collective-permute-done.4 = bf16[4,40,256]{2,1,0:T(8,128)(2,1)S(1)} collective-permute-done((bf16[4,40,256]{2,1,0:T(8,128)(2,1)S(1)}, bf16[4,40,256]{2,1,0:T(8,128)(2,1)S(1)}, u32[]{:S(2)}, u32[]{:S(2)}) %collective-permute-start.4) | collective-permute-done | bytes 81952 | tf_op jit(solution)/shard_map/ppermute | solution.py:41
  32.0 1.3 collective-permute-start.5
  33.3 0.8 collective-permute-start.6
  34.1 1.6 collective-permute-start.7
  35.6 0.4 collective-permute-done.5
  36.1 2.7 %collective-permute-done.6 = bf16[2,40,256]{2,1,0:T(8,128)(2,1)S(1)} collective-permute-done((bf16[2,40,256]{2,1,0:T(8,128)(2,1)S(1)}, bf16[2,40,256]{2,1,0:T(8,128)(2,1)S(1)}, u32[]{:S(2)}, u32[]{:S(2)}) %collective-permute-start.6) | collective-permute-done | bytes 40992 | tf_op jit(solution)/shard_map/ppermute | solution.py:37
  38.8 3.3 %collective-permute-start.8 = (bf16[320,256]{1,0:T(8,128)(2,1)S(1)}, bf16[320,256]{1,0:T(8,128)(2,1)S(1)}, u32[]{:S(2)}, u32[]{:S(2)}) collective-permute-start(bf16[320,256]{1,0:T(8,128)(2,1)S(1)} %bitcast.113), channel_id=1, source_target_pairs={{0,192},{16,208},{32,224},{48,240},{64,0},{80,16},{96,32},{112,48}... | collective-permute-start | bytes 491528 | tf_op jit(solution)/shard_map/ppermute | solution.py:23
  42.1 1.6 collective-permute-start.10
  43.8 1.6 collective-permute-done.8
  45.4 6.3 %collective-permute-done.9 = bf16[320,256]{1,0:T(8,128)(2,1)S(1)} collective-permute-done((bf16[320,256]{1,0:T(8,128)(2,1)S(1)}, bf16[320,256]{1,0:T(8,128)(2,1)S(1)}, u32[]{:S(2)}, u32[]{:S(2)}) %collective-permute-start.9) | collective-permute-done | bytes 163872 | tf_op jit(solution)/shard_map/ppermute | solution.py:23
  51.8 0.1 pad_maximum_fusion.g0
  51.9 1.7 collective-permute-start.12
  53.5 1.7 collective-permute-start.11
  55.2 12.1 %collective-permute-done.12.g3 = bf16[4,320,256]{2,1,0:T(8,128)(2,1)S(1)} collective-permute-done((bf16[4,320,256]{2,1,0:T(8,128)(2,1)S(1)}, bf16[4,320,256]{2,1,0:T(8,128)(2,1)S(1)}, u32[]{:S(2)}, u32[]{:S(2)}) %collective-permute-start.12) | collective-permute-done | bytes 655392 | tf_op jit(solution)/shard_map/ppermute | solution.py:18
  67.3 0.4 collective-permute-start.13
  67.8 2.9 %collective-permute-start.14 = (bf16[4,160,256]{2,1,0:T(8,128)(2,1)S(1)}, bf16[4,160,256]{2,1,0:T(8,128)(2,1)}, u32[]{:S(2)}, u32[]{:S(2)}) collective-permute-start(bf16[4,160,256]{2,1,0:T(8,128)(2,1)S(1)} %slice.135), channel_id=1, source_target_pairs={{0,48},{16,0},{32,16},{48,32},{64,112},{80,64},{96,80},{112,96},{1... | collective-permute-start | bytes 983048 | tf_op jit(solution)/shard_map/ppermute | solution.py:18
  70.7 0.5 collective-permute-start.19
  71.2 4.5 %collective-permute-done.13.g2a = bf16[4,160,256]{2,1,0:T(8,128)(2,1)} collective-permute-done((bf16[4,160,256]{2,1,0:T(8,128)(2,1)S(1)}, bf16[4,160,256]{2,1,0:T(8,128)(2,1)}, u32[]{:S(2)}, u32[]{:S(2)}) %collective-permute-start.13) | collective-permute-done | bytes 327712 | tf_op jit(solution)/shard_map/ppermute | solution.py:18
  75.8 0.5 collective-permute-start.18
  76.3 6.5 %copy.21 = bf16[512,8,2,384]{3,1,2,0:T(8,128)(2,1)} copy(bf16[512,8,2,384]{3,2,1,0:T(2,128)(2,1)} %bitcast.109) | data formatting | bytes 12582912
  82.9 16.5 %shard_map.64 = (f32[4,4,320,256]{3,2,1,0:T(8,128)}, bf16[4,4,320,256]{3,2,1,0:T(8,128)(2,1)}) custom-call(s32[2]{0:T(128)S(1)} %pad_add_fusion.place, bf16[4,320,256]{2,1,0:T(8,128)(2,1)S(1)} %pad_maximum_fusion.g0, bf16[4,320,256]{2,1,0:T(8,128)(2,1)S(1)} %collective-permute-done.11.g1, bf16[4,160,256]{2,1,0:T(8,128)(2,1)} %collective-permute-done.13.g2a, ...), custom_call_target="tpu_custom_call" | custom-call | flops 6039797760 | bytes 16777216 | tf_op jit(solution)/shard_map/pallas_call | solution.py:92
  99.4 5.1 %collective-permute-done.20 = bf16[4,4,320,256]{3,2,1,0:T(8,128)(2,1)S(1)} collective-permute-done((bf16[4,4,320,256]{3,2,1,0:T(8,128)(2,1)}, bf16[4,4,320,256]{3,2,1,0:T(8,128)(2,1)S(1)}, u32[]{:S(2)}, u32[]{:S(2)}) %collective-permute-start.20) | collective-permute-done | bytes 2621472 | tf_op jit(solution)/shard_map/ppermute | solution.py:45
  104.5 3.1 %convert_add_fusion = f32[4,4,320,256]{3,2,1,0:T(8,128)S(1)} fusion(f32[4,4,320,256]{3,2,1,0:T(8,128)} %get-tuple-element.7, bf16[4,4,320,256]{3,2,1,0:T(8,128)(2,1)S(1)} %collective-permute-done.20), kind=kLoop, calls=%fused_computation | loop fusion | flops 2621440 | bytes 13107200 | tf_op jit(solution)/shard_map/add | solution.py:175
  107.7 0.2 slice_bitcast_fusion.7
  107.8 0.5 collective-permute-start.21
  108.4 2.8 %collective-permute-start.23 = (bf16[4,160,256]{2,1,0:T(8,128)(2,1)S(1)}, bf16[4,160,256]{2,1,0:T(8,128)(2,1)S(1)}, u32[]{:S(2)}, u32[]{:S(2)}) collective-permute-start(bf16[4,160,256]{2,1,0:T(8,128)(2,1)S(1)} %get-tuple-element.14), channel_id=1, source_target_pairs={{0,48},{16,0},{32,16},{48,32},{64,112},{80,64},{96,80},{112,96},{1... | collective-permute-start | bytes 983048 | tf_op jit(solution)/shard_map/ppermute | solution.py:18
  111.2 8.0 %collective-permute-done.21 = bf16[4,160,256]{2,1,0:T(8,128)(2,1)S(1)} collective-permute-done((bf16[4,160,256]{2,1,0:T(8,128)(2,1)S(1)}, bf16[4,160,256]{2,1,0:T(8,128)(2,1)S(1)}, u32[]{:S(2)}, u32[]{:S(2)}) %collective-permute-start.21) | collective-permute-done | bytes 327712 | tf_op jit(solution)/shard_map/ppermute | solution.py:18
  119.1 0.1 fusion.7
  119.3 0.1 collective-permute-start.22
  119.4 0.1 fusion.5
  119.6 3.3 %collective-permute-start.24 = (bf16[4,320,256]{2,1,0:T(8,128)(2,1)S(1)}, bf16[4,320,256]{2,1,0:T(8,128)(2,1)S(1)}, u32[]{:S(2)}, u32[]{:S(2)}) collective-permute-start(bf16[4,320,256]{2,1,0:T(8,128)(2,1)S(1)} %pad_maximum_fusion.2), channel_id=1, source_target_pairs={{0,48},{16,0},{32,16},{48,32},{64,112},{80,64},{96,80},{112,96},{1... | collective-permute-start | bytes 1966088 | tf_op jit(solution)/shard_map/ppermute | solution.py:18
  122.9 13.9 %collective-permute-done.22 = bf16[4,320,256]{2,1,0:T(8,128)(2,1)S(1)} collective-permute-done((bf16[4,320,256]{2,1,0:T(8,128)(2,1)S(1)}, bf16[4,320,256]{2,1,0:T(8,128)(2,1)S(1)}, u32[]{:S(2)}, u32[]{:S(2)}) %collective-permute-start.22) | collective-permute-done | bytes 655392 | tf_op jit(solution)/shard_map/ppermute | solution.py:18
  136.8 0.3 fusion.44
  137.1 0.1 collective-permute-start.25
  137.2 1.9 %collective-permute-start.26 = (bf16[320,256]{1,0:T(8,128)(2,1)S(1)}, bf16[320,256]{1,0:T(8,128)(2,1)S(1)}, u32[]{:S(2)}, u32[]{:S(2)}) collective-permute-start(bf16[320,256]{1,0:T(8,128)(2,1)S(1)} %get-tuple-element.19), channel_id=1, source_target_pairs={{0,128},{16,144},{32,160},{48,176},{64,192},{80,208},{96,224},{112... | collective-permute-start | bytes 491528 | tf_op jit(solution)/shard_map/ppermute | solution.py:23
  139.1 2.8 %collective-permute-start.27 = (bf16[320,256]{1,0:T(8,128)(2,1)S(1)}, bf16[320,256]{1,0:T(8,128)(2,1)S(1)}, u32[]{:S(2)}, u32[]{:S(2)}) collective-permute-start(bf16[320,256]{1,0:T(8,128)(2,1)S(1)} %get-tuple-element.18), channel_id=1, source_target_pairs={{0,192},{16,208},{32,224},{48,240},{64,0},{80,16},{96,32},{112,48}... | collective-permute-start | bytes 491528 | tf_op jit(solution)/shard_map/ppermute | solution.py:23
  142.0 4.3 %collective-permute-done.25 = bf16[320,256]{1,0:T(8,128)(2,1)S(1)} collective-permute-done((bf16[320,256]{1,0:T(8,128)(2,1)S(1)}, bf16[320,256]{1,0:T(8,128)(2,1)S(1)}, u32[]{:S(2)}, u32[]{:S(2)}) %collective-permute-start.25) | collective-permute-done | bytes 163872 | tf_op jit(solution)/shard_map/ppermute | solution.py:23
  146.2 4.8 %collective-permute-done.26 = bf16[320,256]{1,0:T(8,128)(2,1)S(1)} collective-permute-done((bf16[320,256]{1,0:T(8,128)(2,1)S(1)}, bf16[320,256]{1,0:T(8,128)(2,1)S(1)}, u32[]{:S(2)}, u32[]{:S(2)}) %collective-permute-start.26) | collective-permute-done | bytes 163872 | tf_op jit(solution)/shard_map/ppermute | solution.py:23
  151.1 0.9 collective-permute-start.28
  152.1 3.9 %collective-permute-start.29 = (bf16[2,40,256]{2,1,0:T(8,128)(2,1)S(1)}, bf16[2,40,256]{2,1,0:T(8,128)(2,1)S(1)}, u32[]{:S(2)}, u32[]{:S(2)}) collective-permute-start(bf16[2,40,256]{2,1,0:T(8,128)(2,1)S(1)} %bitcast.131), channel_id=1, source_target_pairs={{0,4},{1,5},{2,6},{3,7},{4,0},{5,1},{6,2},{7,3},{8,12},{9,13},{10,... | collective-permute-start | bytes 122888 | tf_op jit(solution)/shard_map/ppermute | solution.py:37
  155.9 2.0 %collective-permute-done.29 = bf16[2,40,256]{2,1,0:T(8,128)(2,1)S(1)} collective-permute-done((bf16[2,40,256]{2,1,0:T(8,128)(2,1)S(1)}, bf16[2,40,256]{2,1,0:T(8,128)(2,1)S(1)}, u32[]{:S(2)}, u32[]{:S(2)}) %collective-permute-start.29) | collective-permute-done | bytes 40992 | tf_op jit(solution)/shard_map/ppermute | solution.py:37
  157.9 2.0 %collective-permute-done.30 = bf16[2,40,256]{2,1,0:T(8,128)(2,1)S(1)} collective-permute-done((bf16[2,40,256]{2,1,0:T(8,128)(2,1)S(1)}, bf16[2,40,256]{2,1,0:T(8,128)(2,1)S(1)}, u32[]{:S(2)}, u32[]{:S(2)}) %collective-permute-start.30) | collective-permute-done | bytes 40992 | tf_op jit(solution)/shard_map/ppermute | solution.py:37
  160.0 4.6 %collective-permute-start.31 = (bf16[4,40,256]{2,1,0:T(8,128)(2,1)S(1)}, bf16[4,40,256]{2,1,0:T(8,128)(2,1)S(1)}, u32[]{:S(2)}, u32[]{:S(2)}) collective-permute-start(bf16[4,40,256]{2,1,0:T(8,128)(2,1)S(1)} %get-tuple-element.21), channel_id=1, source_target_pairs={{0,8},{1,9},{2,10},{3,11},{4,12},{5,13},{6,14},{7,15},{8,0},{9,1},... | collective-permute-start | bytes 245768 | tf_op jit(solution)/shard_map/ppermute | solution.py:41
  164.6 4.7 %collective-permute-done.31 = bf16[4,40,256]{2,1,0:T(8,128)(2,1)S(1)} collective-permute-done((bf16[4,40,256]{2,1,0:T(8,128)(2,1)S(1)}, bf16[4,40,256]{2,1,0:T(8,128)(2,1)S(1)}, u32[]{:S(2)}, u32[]{:S(2)}) %collective-permute-start.31) | collective-permute-done | bytes 81952 | tf_op jit(solution)/shard_map/ppermute | solution.py:41
  169.3 0.2 fusion.48
  169.5 0.9 fusion.3
  (51 shorter events, 0.8 us)
Async XLA Ops:
  0.0 1.0 copy-start
  2.1 3.7 %collective-permute-start = (f32[16,128]{1,0:T(8,128)S(1)}, f32[16,128]{1,0:T(8,128)S(1)}, u32[]{:S(2)}, u32[]{:S(2)}) collective-permute-start(f32[16,128]{1,0:T(8,128)S(1)} %maximum_maximum_fusion), channel_id=1, source_target_pairs={{0,16},{16,0},{32,48},{48,32},{64,80},{80,64},{96,112},{112,96},{1... | collective-permute-start | bytes 24584 | tf_op jit(solution)/shard_map/ppermute | solution.py:27
  5.8 5.2 %collective-permute-start.1 = (f32[16,128]{1,0:T(8,128)S(1)}, f32[16,128]{1,0:T(8,128)S(1)}, u32[]{:S(2)}, u32[]{:S(2)}) collective-permute-start(f32[16,128]{1,0:T(8,128)S(1)} %fusion.43), channel_id=1, source_target_pairs={{0,32},{16,48},{32,0},{48,16},{64,96},{80,112},{96,64},{112,80},{1... | collective-permute-start | bytes 24584 | tf_op jit(solution)/shard_map/ppermute | solution.py:27
  11.0 3.7 %collective-permute-start.2 = (f32[16,128]{1,0:T(8,128)S(1)}, f32[16,128]{1,0:T(8,128)S(1)}, u32[]{:S(2)}, u32[]{:S(2)}) collective-permute-start(f32[16,128]{1,0:T(8,128)S(1)} %add.111), channel_id=1, source_target_pairs={{0,64},{16,80},{32,96},{48,112},{64,0},{80,16},{96,32},{112,48},{1... | collective-permute-start | bytes 24584 | tf_op jit(solution)/shard_map/ppermute | solution.py:27
  14.7 4.9 %collective-permute-start.3 = (f32[16,128]{1,0:T(8,128)S(1)}, f32[16,128]{1,0:T(8,128)S(1)}, u32[]{:S(2)}, u32[]{:S(2)}) collective-permute-start(f32[16,128]{1,0:T(8,128)S(1)} %add.112), channel_id=1, source_target_pairs={{0,128},{16,144},{32,160},{48,176},{64,192},{80,208},{96,224},{112... | collective-permute-start | bytes 24584 | tf_op jit(solution)/shard_map/ppermute | solution.py:27
  22.5 9.5 %collective-permute-start.4 = (bf16[4,40,256]{2,1,0:T(8,128)(2,1)S(1)}, bf16[4,40,256]{2,1,0:T(8,128)(2,1)S(1)}, u32[]{:S(2)}, u32[]{:S(2)}) collective-permute-start(bf16[4,40,256]{2,1,0:T(8,128)(2,1)S(1)} %bitcast.126), channel_id=1, source_target_pairs={{0,8},{1,9},{2,10},{3,11},{4,12},{5,13},{6,14},{7,15},{8,0},{9,1},... | collective-permute-start | bytes 245768 | tf_op jit(solution)/shard_map/ppermute | solution.py:41
  32.0 4.1 %collective-permute-start.5 = (bf16[2,40,256]{2,1,0:T(8,128)(2,1)S(1)}, bf16[2,40,256]{2,1,0:T(8,128)(2,1)S(1)}, u32[]{:S(2)}, u32[]{:S(2)}) collective-permute-start(bf16[2,40,256]{2,1,0:T(8,128)(2,1)S(1)} %get-tuple-element.27), channel_id=1, source_target_pairs={{0,2},{1,3},{2,4},{3,5},{4,6},{5,7},{6,0},{7,1},{8,10},{9,11},{10,... | collective-permute-start | bytes 122888 | tf_op jit(solution)/shard_map/ppermute | solution.py:37
  33.3 5.5 %collective-permute-start.6 = (bf16[2,40,256]{2,1,0:T(8,128)(2,1)S(1)}, bf16[2,40,256]{2,1,0:T(8,128)(2,1)S(1)}, u32[]{:S(2)}, u32[]{:S(2)}) collective-permute-start(bf16[2,40,256]{2,1,0:T(8,128)(2,1)S(1)} %get-tuple-element.29), channel_id=1, source_target_pairs={{0,4},{1,5},{2,6},{3,7},{4,0},{5,1},{6,2},{7,3},{8,12},{9,13},{10,... | collective-permute-start | bytes 122888 | tf_op jit(solution)/shard_map/ppermute | solution.py:37
  34.1 4.7 %collective-permute-start.7 = (bf16[2,40,256]{2,1,0:T(8,128)(2,1)S(1)}, bf16[2,40,256]{2,1,0:T(8,128)(2,1)S(1)}, u32[]{:S(2)}, u32[]{:S(2)}) collective-permute-start(bf16[2,40,256]{2,1,0:T(8,128)(2,1)S(1)} %get-tuple-element.28), channel_id=1, source_target_pairs={{0,6},{1,7},{2,0},{3,1},{4,2},{5,3},{6,4},{7,5},{8,14},{9,15},{10,... | collective-permute-start | bytes 122888 | tf_op jit(solution)/shard_map/ppermute | solution.py:37
  38.8 6.6 %collective-permute-start.8 = (bf16[320,256]{1,0:T(8,128)(2,1)S(1)}, bf16[320,256]{1,0:T(8,128)(2,1)S(1)}, u32[]{:S(2)}, u32[]{:S(2)}) collective-permute-start(bf16[320,256]{1,0:T(8,128)(2,1)S(1)} %bitcast.113), channel_id=1, source_target_pairs={{0,192},{16,208},{32,224},{48,240},{64,0},{80,16},{96,32},{112,48}... | collective-permute-start | bytes 491528 | tf_op jit(solution)/shard_map/ppermute | solution.py:23
  42.1 9.6 %collective-permute-start.9 = (bf16[320,256]{1,0:T(8,128)(2,1)S(1)}, bf16[320,256]{1,0:T(8,128)(2,1)S(1)}, u32[]{:S(2)}, u32[]{:S(2)}) collective-permute-start(bf16[320,256]{1,0:T(8,128)(2,1)S(1)} %bitcast.114), channel_id=1, source_target_pairs={{0,128},{16,144},{32,160},{48,176},{64,192},{80,208},{96,224},{112... | collective-permute-start | bytes 491528 | tf_op jit(solution)/shard_map/ppermute | solution.py:23
  42.1 9.6 %collective-permute-start.10 = (bf16[320,256]{1,0:T(8,128)(2,1)S(1)}, bf16[320,256]{1,0:T(8,128)(2,1)S(1)}, u32[]{:S(2)}, u32[]{:S(2)}) collective-permute-start(bf16[320,256]{1,0:T(8,128)(2,1)S(1)} %bitcast.115), channel_id=1, source_target_pairs={{0,64},{16,80},{32,96},{48,112},{64,128},{80,144},{96,160},{112,17... | collective-permute-start | bytes 491528 | tf_op jit(solution)/shard_map/ppermute | solution.py:23
  51.9 15.4 %collective-permute-start.12 = (bf16[4,320,256]{2,1,0:T(8,128)(2,1)S(1)}, bf16[4,320,256]{2,1,0:T(8,128)(2,1)S(1)}, u32[]{:S(2)}, u32[]{:S(2)}) collective-permute-start(bf16[4,320,256]{2,1,0:T(8,128)(2,1)S(1)} %pad_maximum_fusion.g0), channel_id=1, source_target_pairs={{0,16},{16,32},{32,48},{48,0},{64,80},{80,96},{96,112},{112,64},{1... | collective-permute-start | bytes 1966088 | tf_op jit(solution)/shard_map/ppermute | solution.py:18
  53.5 14.2 %collective-permute-start.11 = (bf16[4,320,256]{2,1,0:T(8,128)(2,1)S(1)}, bf16[4,320,256]{2,1,0:T(8,128)(2,1)S(1)}, u32[]{:S(2)}, u32[]{:S(2)}) collective-permute-start(bf16[4,320,256]{2,1,0:T(8,128)(2,1)S(1)} %pad_maximum_fusion.g0), channel_id=1, source_target_pairs={{0,48},{16,0},{32,16},{48,32},{64,112},{80,64},{96,80},{112,96},{1... | collective-permute-start | bytes 1966088 | tf_op jit(solution)/shard_map/ppermute | solution.py:18
  55.2 27.7 %collective-permute-start.15 = (bf16[4,320,256]{2,1,0:T(8,128)(2,1)S(1)}, bf16[4,320,256]{2,1,0:T(8,128)(2,1)S(1)}, u32[]{:S(2)}, u32[]{:S(2)}) collective-permute-start(bf16[4,320,256]{2,1,0:T(8,128)(2,1)S(1)} %pad_maximum_fusion.g0), channel_id=1, source_target_pairs={{0,1},{1,0},{2,3},{3,2},{4,5},{5,4},{6,7},{7,6},{8,9},{9,8},{10,11... | collective-permute-start | bytes 1966088 | tf_op jit(solution)/shard_map/ppermute | solution.py:45
  67.3 8.5 %collective-permute-start.13 = (bf16[4,160,256]{2,1,0:T(8,128)(2,1)S(1)}, bf16[4,160,256]{2,1,0:T(8,128)(2,1)}, u32[]{:S(2)}, u32[]{:S(2)}) collective-permute-start(bf16[4,160,256]{2,1,0:T(8,128)(2,1)S(1)} %slice.134), channel_id=1, source_target_pairs={{0,16},{16,32},{32,48},{48,0},{64,80},{80,96},{96,112},{112,64},{1... | collective-permute-start | bytes 983048 | tf_op jit(solution)/shard_map/ppermute | solution.py:18
  67.8 8.0 %collective-permute-start.14 = (bf16[4,160,256]{2,1,0:T(8,128)(2,1)S(1)}, bf16[4,160,256]{2,1,0:T(8,128)(2,1)}, u32[]{:S(2)}, u32[]{:S(2)}) collective-permute-start(bf16[4,160,256]{2,1,0:T(8,128)(2,1)S(1)} %slice.135), channel_id=1, source_target_pairs={{0,48},{16,0},{32,16},{48,32},{64,112},{80,64},{96,80},{112,96},{1... | collective-permute-start | bytes 983048 | tf_op jit(solution)/shard_map/ppermute | solution.py:18
  70.7 12.2 %collective-permute-start.16 = (bf16[4,320,256]{2,1,0:T(8,128)(2,1)S(1)}, bf16[4,320,256]{2,1,0:T(8,128)(2,1)S(1)}, u32[]{:S(2)}, u32[]{:S(2)}) collective-permute-start(bf16[4,320,256]{2,1,0:T(8,128)(2,1)S(1)} %collective-permute-done.11.g1), channel_id=1, source_target_pairs={{0,1},{1,0},{2,3},{3,2},{4,5},{5,4},{6,7},{7,6},{8,9},{9,8},{10,11... | collective-permute-start | bytes 1966088 | tf_op jit(solution)/shard_map/ppermute | solution.py:45
  70.7 12.2 %collective-permute-start.19 = (bf16[4,320,256]{2,1,0:T(8,128)(2,1)S(1)}, bf16[4,320,256]{2,1,0:T(8,128)(2,1)}, u32[]{:S(2)}, u32[]{:S(2)}) collective-permute-start(bf16[4,320,256]{2,1,0:T(8,128)(2,1)S(1)} %collective-permute-done.12.g3), channel_id=1, source_target_pairs={{0,1},{1,0},{2,3},{3,2},{4,5},{5,4},{6,7},{7,6},{8,9},{9,8},{10,11... | collective-permute-start | bytes 1966088 | tf_op jit(solution)/shard_map/ppermute | solution.py:45
  75.8 7.1 %collective-permute-start.17 = (bf16[4,160,256]{2,1,0:T(8,128)(2,1)}, bf16[4,160,256]{2,1,0:T(8,128)(2,1)}, u32[]{:S(2)}, u32[]{:S(2)}) collective-permute-start(bf16[4,160,256]{2,1,0:T(8,128)(2,1)} %collective-permute-done.13.g2a), channel_id=1, source_target_pairs={{0,1},{1,0},{2,3},{3,2},{4,5},{5,4},{6,7},{7,6},{8,9},{9,8},{10,11... | collective-permute-start | bytes 983048 | tf_op jit(solution)/shard_map/ppermute | solution.py:45
  75.8 7.1 %collective-permute-start.18 = (bf16[4,160,256]{2,1,0:T(8,128)(2,1)}, bf16[4,160,256]{2,1,0:T(8,128)(2,1)}, u32[]{:S(2)}, u32[]{:S(2)}) collective-permute-start(bf16[4,160,256]{2,1,0:T(8,128)(2,1)} %collective-permute-done.14.g2b), channel_id=1, source_target_pairs={{0,1},{1,0},{2,3},{3,2},{4,5},{5,4},{6,7},{7,6},{8,9},{9,8},{10,11... | collective-permute-start | bytes 983048 | tf_op jit(solution)/shard_map/ppermute | solution.py:45
  99.4 5.1 %collective-permute-start.20 = (bf16[4,4,320,256]{3,2,1,0:T(8,128)(2,1)}, bf16[4,4,320,256]{3,2,1,0:T(8,128)(2,1)S(1)}, u32[]{:S(2)}, u32[]{:S(2)}) collective-permute-start(bf16[4,4,320,256]{3,2,1,0:T(8,128)(2,1)} %get-tuple-element.8), channel_id=1, source_target_pairs={{0,1},{1,0},{2,3},{3,2},{4,5},{5,4},{6,7},{7,6},{8,9},{9,8},{10,11... | collective-permute-start | bytes 7864328 | tf_op jit(solution)/shard_map/ppermute | solution.py:45
  107.8 11.3 %collective-permute-start.21 = (bf16[4,160,256]{2,1,0:T(8,128)(2,1)S(1)}, bf16[4,160,256]{2,1,0:T(8,128)(2,1)S(1)}, u32[]{:S(2)}, u32[]{:S(2)}) collective-permute-start(bf16[4,160,256]{2,1,0:T(8,128)(2,1)S(1)} %get-tuple-element.13), channel_id=1, source_target_pairs={{0,16},{16,32},{32,48},{48,0},{64,80},{80,96},{96,112},{112,64},{1... | collective-permute-start | bytes 983048 | tf_op jit(solution)/shard_map/ppermute | solution.py:18
  108.4 11.0 %collective-permute-start.23 = (bf16[4,160,256]{2,1,0:T(8,128)(2,1)S(1)}, bf16[4,160,256]{2,1,0:T(8,128)(2,1)S(1)}, u32[]{:S(2)}, u32[]{:S(2)}) collective-permute-start(bf16[4,160,256]{2,1,0:T(8,128)(2,1)S(1)} %get-tuple-element.14), channel_id=1, source_target_pairs={{0,48},{16,0},{32,16},{48,32},{64,112},{80,64},{96,80},{112,96},{1... | collective-permute-start | bytes 983048 | tf_op jit(solution)/shard_map/ppermute | solution.py:18
  119.3 17.5 %collective-permute-start.22 = (bf16[4,320,256]{2,1,0:T(8,128)(2,1)S(1)}, bf16[4,320,256]{2,1,0:T(8,128)(2,1)S(1)}, u32[]{:S(2)}, u32[]{:S(2)}) collective-permute-start(bf16[4,320,256]{2,1,0:T(8,128)(2,1)S(1)} %pad_maximum_fusion.1), channel_id=1, source_target_pairs={{0,16},{16,32},{32,48},{48,0},{64,80},{80,96},{96,112},{112,64},{1... | collective-permute-start | bytes 1966088 | tf_op jit(solution)/shard_map/ppermute | solution.py:18
  119.6 50.0 %copy-start.1 = (bf16[128,256]{1,0:T(8,128)(2,1)S(1)}, bf16[128,256]{1,0:T(8,128)(2,1)}, u32[]{:S(2)}) copy-start(bf16[128,256]{1,0:T(8,128)(2,1)} %param.6) | copy-start | bytes 196612
  119.6 17.2 %collective-permute-start.24 = (bf16[4,320,256]{2,1,0:T(8,128)(2,1)S(1)}, bf16[4,320,256]{2,1,0:T(8,128)(2,1)S(1)}, u32[]{:S(2)}, u32[]{:S(2)}) collective-permute-start(bf16[4,320,256]{2,1,0:T(8,128)(2,1)S(1)} %pad_maximum_fusion.2), channel_id=1, source_target_pairs={{0,48},{16,0},{32,16},{48,32},{64,112},{80,64},{96,80},{112,96},{1... | collective-permute-start | bytes 1966088 | tf_op jit(solution)/shard_map/ppermute | solution.py:18
  137.1 9.1 %collective-permute-start.25 = (bf16[320,256]{1,0:T(8,128)(2,1)S(1)}, bf16[320,256]{1,0:T(8,128)(2,1)S(1)}, u32[]{:S(2)}, u32[]{:S(2)}) collective-permute-start(bf16[320,256]{1,0:T(8,128)(2,1)S(1)} %get-tuple-element.17), channel_id=1, source_target_pairs={{0,64},{16,80},{32,96},{48,112},{64,128},{80,144},{96,160},{112,17... | collective-permute-start | bytes 491528 | tf_op jit(solution)/shard_map/ppermute | solution.py:23
  137.2 13.8 %collective-permute-start.26 = (bf16[320,256]{1,0:T(8,128)(2,1)S(1)}, bf16[320,256]{1,0:T(8,128)(2,1)S(1)}, u32[]{:S(2)}, u32[]{:S(2)}) collective-permute-start(bf16[320,256]{1,0:T(8,128)(2,1)S(1)} %get-tuple-element.19), channel_id=1, source_target_pairs={{0,128},{16,144},{32,160},{48,176},{64,192},{80,208},{96,224},{112... | collective-permute-start | bytes 491528 | tf_op jit(solution)/shard_map/ppermute | solution.py:23
  139.1 11.9 %collective-permute-start.27 = (bf16[320,256]{1,0:T(8,128)(2,1)S(1)}, bf16[320,256]{1,0:T(8,128)(2,1)S(1)}, u32[]{:S(2)}, u32[]{:S(2)}) collective-permute-start(bf16[320,256]{1,0:T(8,128)(2,1)S(1)} %get-tuple-element.18), channel_id=1, source_target_pairs={{0,192},{16,208},{32,224},{48,240},{64,0},{80,16},{96,32},{112,48}... | collective-permute-start | bytes 491528 | tf_op jit(solution)/shard_map/ppermute | solution.py:23
  151.1 4.8 %collective-permute-start.28 = (bf16[2,40,256]{2,1,0:T(8,128)(2,1)S(1)}, bf16[2,40,256]{2,1,0:T(8,128)(2,1)S(1)}, u32[]{:S(2)}, u32[]{:S(2)}) collective-permute-start(bf16[2,40,256]{2,1,0:T(8,128)(2,1)S(1)} %bitcast.134), channel_id=1, source_target_pairs={{0,6},{1,7},{2,0},{3,1},{4,2},{5,3},{6,4},{7,5},{8,14},{9,15},{10,... | collective-permute-start | bytes 122888 | tf_op jit(solution)/shard_map/ppermute | solution.py:37
  152.1 5.8 %collective-permute-start.29 = (bf16[2,40,256]{2,1,0:T(8,128)(2,1)S(1)}, bf16[2,40,256]{2,1,0:T(8,128)(2,1)S(1)}, u32[]{:S(2)}, u32[]{:S(2)}) collective-permute-start(bf16[2,40,256]{2,1,0:T(8,128)(2,1)S(1)} %bitcast.131), channel_id=1, source_target_pairs={{0,4},{1,5},{2,6},{3,7},{4,0},{5,1},{6,2},{7,3},{8,12},{9,13},{10,... | collective-permute-start | bytes 122888 | tf_op jit(solution)/shard_map/ppermute | solution.py:37
  155.9 4.0 %collective-permute-start.30 = (bf16[2,40,256]{2,1,0:T(8,128)(2,1)S(1)}, bf16[2,40,256]{2,1,0:T(8,128)(2,1)S(1)}, u32[]{:S(2)}, u32[]{:S(2)}) collective-permute-start(bf16[2,40,256]{2,1,0:T(8,128)(2,1)S(1)} %bitcast.128), channel_id=1, source_target_pairs={{0,2},{1,3},{2,4},{3,5},{4,6},{5,7},{6,0},{7,1},{8,10},{9,11},{10,... | collective-permute-start | bytes 122888 | tf_op jit(solution)/shard_map/ppermute | solution.py:37
  160.0 9.3 %collective-permute-start.31 = (bf16[4,40,256]{2,1,0:T(8,128)(2,1)S(1)}, bf16[4,40,256]{2,1,0:T(8,128)(2,1)S(1)}, u32[]{:S(2)}, u32[]{:S(2)}) collective-permute-start(bf16[4,40,256]{2,1,0:T(8,128)(2,1)S(1)} %get-tuple-element.21), channel_id=1, source_target_pairs={{0,8},{1,9},{2,10},{3,11},{4,12},{5,13},{6,14},{7,15},{8,0},{9,1},... | collective-permute-start | bytes 245768 | tf_op jit(solution)/shard_map/ppermute | solution.py:41

commit v2 on v0

v2 whole, which is shorter than its diff:
```python
import jax
import jax.numpy as jnp
from jax import lax
from jax.experimental import pallas as pl
from jax.experimental.pallas import tpu as pltpu
from jax.sharding import PartitionSpec as P

BF16 = jnp.bfloat16
F32 = jnp.float32

NZ, NY, NH, NX = 4, 4, 2, 4
GROUPS = ((0, 1), (2, 3))


def move(value, target):
    pairs = []
    for zl in range(NZ):
        for y in range(NY):
            for zh in range(NH):
                for x in range(NX):
                    for c in range(2):
                        a = ((zl * NY + y) * NH + zh) * NX * 2 + x * 2 + c
                        tz, ty, th, tx, tc = target(zl, y, zh, x, c)
                        b = ((tz * NY + ty) * NH + th) * NX * 2 + tx % NX * 2 + tc
                        pairs.append((a, b))
    return lax.ppermute(value, ("section", "dp"), pairs)


def shift_x(value, step):
    return move(value, lambda zl, y, zh, x, c: (zl, y, zh, x + step, c))


def xor_z(value, mask):
    return move(value, lambda zl, y, zh, x, c: (zl ^ mask, y, zh, x, c))


def xor_y(value, mask):
    return move(value, lambda zl, y, zh, x, c: (zl, y ^ mask, zh, x, c))


def far_y(value):
    return move(value, lambda zl, y, zh, x, c: (zl, y ^ (3 - 2 * c), zh, x, c))


def swap_h(value):
    return move(value, lambda zl, y, zh, x, c: (zl, y, zh ^ 1, x, c))


def swap_core(value):
    return move(value, lambda zl, y, zh, x, c: (zl, y, zh, x, c ^ 1))


def after(value, *others):
    return lax.optimization_barrier((value,) + others)[0]


def load(place, group, w_up, slab, sems):
    zl, y = place[0], place[1]
    copies = []
    for n, d in enumerate(group):
        for j in range(NY):
            start = pl.multiple_of(((zl ^ d) * NY + (y ^ j)) * WIDTH, WIDTH)
            copies.append(
                pltpu.make_async_copy(
                    w_up.at[pl.ds(start, WIDTH)],
                    slab.at[n, pl.ds(j * WIDTH, WIDTH)],
                    sems.at[n * NY + j],
                )
            )
    for copy in copies:
        copy.start()
    return copies


def square(blocks, squares, extras):
    count = squares.shape[0] // 2
    inverse = []
    sums = extras[...]
    for n in range(len(GROUPS[0])):
        for j in range(NY):
            extra = blocks[2 * j][n, count:].astype(F32)
            sums += extra
            inverse.append(1.0 / (extra[9:10] + extra[10:11] + extra[11:12]))
    extras[...] = sums
    step = 32

    def body(r, carry):
        start = pl.multiple_of(r * step, step)
        for side in range(2):
            place_at = pl.ds(pl.multiple_of(side * count + start, step), step)
            sums = squares[place_at, :]
            for n in range(len(GROUPS[0])):
                for j in range(NY):
                    plain = blocks[2 * j + side][n, pl.ds(start, step)].astype(F32)
                    plain = plain * inverse[n * NY + j]
                    sums += plain * plain
            squares[place_at, :] = sums
        return carry

    lax.fori_loop(0, count // step, body, 0)


def project(blocks, total, slab, copies):
    count = total.shape[0] // 2
    for n in range(len(GROUPS[0])):
        for copy in copies[n * NY : n * NY + NY] if copies else ():
            copy.wait()
        left = jnp.concatenate(
            [
                jnp.concatenate([blocks[2 * j + side][n, :count] for j in range(NY)], axis=1)
                for side in range(2)
            ],
            axis=0,
        )
        total[...] += jnp.dot(left, slab[n], preferred_element_type=F32)


def expand(place, act, w_down, own, give, group):
    zl, y = place[0], place[1]
    count = act.shape[0] // 2
    for n, d in enumerate(group):
        for j in range(NY):
            start = pl.multiple_of(((zl ^ d) * NY + (y ^ j)) * WIDTH, WIDTH)
            result = jnp.dot(act[...], w_down[:, pl.ds(start, WIDTH)], preferred_element_type=F32)
            own[j][n] = result[:count]
            give[j, n] = result[count:].astype(BF16)


def first_kernel(place, *refs):
    blocks, refs = refs[:8], refs[8:]
    w_up, w_down, total, squares, extras, next_slab, down, slab, sems, next_sems, sem = refs
    copies = load(place, GROUPS[0], w_up, slab, sems)
    later = load(place, GROUPS[1], w_up, next_slab, next_sems)
    whole = pltpu.make_async_copy(w_down, down, sem)
    whole.start()
    squares[...] = jnp.zeros_like(squares)
    extras[...] = jnp.zeros_like(extras)
    square(blocks, squares, extras)
    total[...] = jnp.zeros_like(total)
    project(blocks, total, slab, copies)
    for copy in later:
        copy.wait()
    whole.wait()


def second_kernel(place, *refs):
    blocks, refs = refs[:8], refs[8:]
    (total_in, squares_in, extras_in, slab, w_down, act), refs = refs[:6], refs[6:]
    own, (give, extras, total, squares) = refs[:NY], refs[NY:]
    units, model = w_down.shape
    total[...] = total_in[...]
    squares[...] = squares_in[...]
    extras[...] = extras_in[...]
    square(blocks, squares, extras)
    project(blocks, total, slab, None)
    mean = jnp.sum(squares[...], axis=1, keepdims=True) / model
    scale = lax.rsqrt(mean + 1e-05)
    act[...] = (jax.nn.silu(total[:, :units] * scale) * (total[:, units:] * scale)).astype(BF16)
    expand(place, act, w_down, own, give, GROUPS[1])


def third_kernel(place, act, w_down, *refs):
    expand(place, act, w_down, refs[:NY], refs[NY], GROUPS[0])


def call(kernel, out_shape, scratch, flops, remote, *args):
    vmem = pl.BlockSpec(memory_space=pltpu.VMEM)
    specs = [pl.BlockSpec(memory_space=pltpu.SMEM)] + [vmem] * (len(args) - 1)
    for k in range(len(args) - remote, len(args)):
        specs[k] = pl.BlockSpec(memory_space=pl.ANY)
    return pl.pallas_call(
        kernel,
        out_shape=out_shape,
        in_specs=specs,
        out_specs=(vmem,) * len(out_shape),
        scratch_shapes=scratch,
        compiler_params=pltpu.CompilerParams(vmem_limit_bytes=VMEM * 1024 * 1024),
        cost_estimate=pl.CostEstimate(flops=flops, bytes_accessed=8 * 1024 * 1024, transcendentals=0),
    )(*args)


VMEM = 24
WIDTH = 256


def shapes(blocks, units):
    count = blocks[0].shape[1] - 16
    totals = ((2 * count, 2 * units), (2 * count, WIDTH))
    slab = (len(GROUPS[0]), NY * WIDTH, 2 * units)
    return count, totals, slab, 4 * count * units * NZ * NY * WIDTH


def expert_first(place, blocks, w_up, w_down):
    shape = jax.ShapeDtypeStruct
    count, totals, slab, flops = shapes(blocks, w_down.shape[0])
    out = (shape(totals[0], F32), shape(totals[1], F32), shape((16, WIDTH), F32))
    out += (shape(slab, BF16), shape(w_down.shape, BF16))
    sems = pltpu.SemaphoreType.DMA((len(GROUPS[0]) * NY,))
    scratch = [pltpu.VMEM(slab, BF16), sems, sems, pltpu.SemaphoreType.DMA]
    return call(first_kernel, out, scratch, flops, 2, place, *blocks, w_up, w_down)


def expert_rest(place, blocks, state):
    shape = jax.ShapeDtypeStruct
    units = state[-1].shape[0]
    count, totals, slab, flops = shapes(blocks, units)
    part = (len(GROUPS[0]), count, WIDTH)
    sums = (shape(part, F32),) * NY + (shape((NY,) + part, BF16),)
    act, *second, extras = call(
        second_kernel,
        (shape((2 * count, units), BF16),) + sums + (shape((16, WIDTH), F32),),
        [pltpu.VMEM(t, F32) for t in totals],
        2 * flops,
        0,
        place,
        *blocks,
        *state,
    )
    first = call(third_kernel, sums, [], flops // 2, 0, place, act, state[-1])
    return first, second, extras


def split(value):
    high = lax.reduce_precision(value, 8, 7)
    return high.astype(BF16), (value - high).astype(BF16)


def slots(routes, names, capacity):
    tokens = routes.shape[0]
    chosen = jnp.sum((routes[:, :, None] == names[None, None, :]).astype(F32), axis=1)
    earlier = (jnp.arange(tokens)[:, None] > jnp.arange(tokens)[None, :]).astype(F32)
    rank = jnp.dot(earlier, chosen, preferred_element_type=F32)
    order = jnp.arange(capacity, dtype=F32)
    picks = chosen.T[:, None, :] * (rank.T[:, None, :] == order[None, :, None]).astype(F32)
    return picks.reshape(names.shape[0] * capacity, tokens)


def local(inputs, norm_gain, router, w_in, w_out, routes):
    tokens, width = inputs.shape
    experts = router.shape[1]
    capacity = min(tokens, 5 * tokens // (2 * experts))
    units = w_out.shape[1]
    model = w_in.shape[1]
    section = lax.axis_index("section")
    dp = lax.axis_index("dp")
    zl, y = section // NY, section % NY
    zh, x, core = dp // (2 * NX), dp // 2 % NX, dp % 2
    place = jnp.stack([zl, y]).astype(jnp.int32)
    w_down = w_out[0]

    acts = inputs.astype(F32)
    scaled = (acts * norm_gain).astype(BF16)
    named = jnp.zeros((16, width), BF16).at[:2, :tokens].set(routes.T.astype(BF16))
    partial_logits = lax.dot_general(
        router, scaled, (((0,), (1,)), ((), ())), preferred_element_type=F32
    )
    logit_rows = jnp.concatenate(split(partial_logits)).reshape(experts, width)
    square_row = jnp.concatenate(split(jnp.sum(acts * acts, axis=1)))[None, :]
    gain_high, _ = split(norm_gain)
    rest = norm_gain - gain_high.astype(F32)
    gain_rows = jnp.stack([gain_high, *split(rest)])
    extra = jnp.concatenate([logit_rows, square_row, gain_rows, jnp.zeros((4, width), BF16)])
    crossed = swap_h(jnp.concatenate([scaled, named], axis=0))
    near = (x + jnp.arange(NX, dtype=jnp.int32)) % NX
    names = jnp.concatenate([zh * NX + near, (zh ^ 1) * NX + near])
    picks = slots(routes, names, capacity)
    other_routes = crossed[tokens : tokens + 2, :tokens].T.astype(jnp.int32)
    other_picks = slots(other_routes, names[:NX], capacity)
    select = lambda p, v: jnp.dot(p.astype(BF16), v, preferred_element_type=F32).astype(BF16)
    mine = select(picks[: NX * capacity], scaled).reshape(NX, capacity, width)
    others = select(other_picks, crossed[:tokens]).reshape(NX, capacity, width)
    sent = jnp.stack([mine, others], axis=1)

    arrived = jnp.stack([sent[0]] + [shift_x(sent[k], k) for k in range(1, NX)])
    arrived = jnp.concatenate([arrived.reshape(NX * NH * capacity, width), extra])
    spread = [arrived] + [xor_z(arrived, d) for d in range(1, NZ)]
    blocks = []
    for group in GROUPS:
        own = jnp.stack([spread[d] for d in group])
        one, three = xor_y(own, 1), xor_y(own, 3)
        turn = jnp.where(core == 0, one, three)
        if group is GROUPS[0]:
            w_up = after(w_in, arrived)[0].reshape(model, 2 * units)
        far = far_y(turn)
        for piece in (own, one, far, three):
            if group is not GROUPS[0]:
                piece = after(piece, state[0])
            blocks += [piece, swap_core(piece)]
        if group is GROUPS[0]:
            state = expert_first(place, blocks, w_up, w_down)

    first, second, extras = expert_rest(place, blocks[8:], state)
    results = (first, second)
    sums = (extras[:4] + extras[4:8]).reshape(experts, tokens)
    inverse = lax.rsqrt((extras[8, :tokens] + extras[8, tokens:]) / model + 1e-05)
    logits = (sums * inverse[None, :]).T

    terms = [None] * NZ
    for g in (1, 0):
        *own, give = results[g]
        given = swap_core(give)
        parts = [own[j] + given[j].astype(F32) for j in range(NY)]
        passed = far_y(parts[2].astype(BF16)).astype(F32)
        one = xor_y((parts[1] + jnp.where(core == 0, passed, 0.0)).astype(BF16), 1)
        three = xor_y((parts[3] + jnp.where(core == 0, 0.0, passed)).astype(BF16), 3)
        column = parts[0] + one.astype(F32) + three.astype(F32)
        for n, d in enumerate(GROUPS[g]):
            terms[d] = xor_z(column[n].astype(BF16), d).astype(F32) if d else column[n]
    full = sum(terms[1:], terms[0]).astype(BF16).reshape(NX, NH, capacity, width)
    back = jnp.stack([full[0]] + [shift_x(full[k], -k) for k in range(1, NX)], axis=1)
    back = jnp.concatenate([back[0], swap_h(back[1])]).reshape(experts * capacity, width)

    hits = (routes[:, :, None] == names[None, None, :]).astype(F32)
    table = (routes[:, :, None] == jnp.arange(experts)[None, None, :]).astype(F32)
    gates = jax.nn.softmax(jnp.sum(table * logits[:, None, :], axis=2), axis=1)
    gate_of = jnp.sum(hits * gates[:, :, None], axis=1)
    weight = jnp.repeat(gate_of.T, capacity, axis=0) * picks
    high, low = split(weight)
    mix = lambda w: lax.dot_general(w, back, (((0,), (0,)), ((), ())), preferred_element_type=F32)
    return (acts + (mix(high) + mix(low))).astype(BF16)


def solution(mesh):
    return jax.shard_map(
        local,
        mesh=mesh,
        in_specs=(
            P("dp", "section"),
            P("section"),
            P("section", None),
            P("dp", None, None, "section"),
            P("dp", "section", None),
            P("dp", None),
        ),
        out_specs=P("dp", "section"),
        check_vma=False,
    )
```

time: 392 us -> 139 us (0.35)
  waiting for transfers between devices: 213 us -> 49.7 us
  blocking collectives: 109 us -> 0 us
  starting transfers between devices: 7.34 us -> 52.7 us
  local copies, waits for them, and re-layouts: 27.9 us -> 4.65 us
  Pallas kernels: 0 us -> 17.8 us
  between operations: 13.6 us -> 0.37 us
  matrix products: 13.6 us -> 1.81 us
  other arithmetic: 5.73 us -> 11.8 us
    reduce_scatter x1 -> x0, waiting for transfers between devices: 126 us -> none  [local(): lax.psum_scatter(lax.dot_general(w_down, hidden_act, (((0,), (1,)), ((),...]
    psum x2 -> x0, blocking collectives: 90.8 us -> none  [the longest x1 45.9 us: local(): lax.psum(jnp.dot(normed, router, preferred_element_type=jnp.float32), 'se...]
    all_gather x1 -> x0, waiting for transfers between devices: 87.4 us -> none  [local(): lax.all_gather(shaped, 'section', axis=1, tiled=True)]
    ppermute x0 -> x36, starting transfers between devices: none -> 52.7 us  [move(): return lax.ppermute(value, ('section', 'dp'), pairs)]
    ppermute x0 -> x36, waiting for transfers between devices: none -> 49.7 us  [move(): return lax.ppermute(value, ('section', 'dp'), pairs)]
    all_to_all x1 -> x0, blocking collectives: 18 us -> none  [local(): lax.all_to_all(outgoing, 'dp', split_axis=0, concat_axis=0, tiled=True)]
    pallas_call x0 -> x3, Pallas kernels: none -> 17.8 us  [call(): pl.pallas_call(kernel, out_shape=out_shape, in_specs=specs, out_specs=(vm...]
    scatter x1 -> x0, local copies, waits for them, and re-layouts: 13.2 us -> none  [local(): buffer = jnp.zeros((experts, capacity, local_width), jnp.bfloat16).at[exp...]
  transfers between devices with their start and end apart: 3 -> 36, of which waited for: 2 -> 20; matrix products, arithmetic and copies ran while one was open for 2% -> 10% of each run, Pallas kernels for 0% -> 8%
where the time goes in v2:
time: 139 us
  starting transfers between devices  52.7 us (38%)
  waiting for transfers between devices  49.7 us (36%)
  Pallas kernels  17.8 us (13%)
  other arithmetic  11.8 us (8%)
  local copies, waits for them, and re-layouts  4.65 us (3%)
  matrix products  1.81 us (1%)
    ppermute x36, starting transfers between devices, move(): return lax.ppermute(value, ('section', 'dp'), pairs)  52.7 us
    ppermute x36, waiting for transfers between devices, move(): return lax.ppermute(value, ('section', 'dp'), pairs)  49.7 us
    pallas_call x3, Pallas kernels, call(): pl.pallas_call(kernel, out_shape=out_shape, in_specs=specs, out_specs=(vm...  17.8 us
    unnamed x23, local copies, waits for them, and re-layouts  4.34 us
  transfers between devices with their start and end apart: 36, of which 20 were waited for; matrix products, arithmetic and copies ran while one was open for 10% of the time, Pallas kernels for 8%

profile of v2, /device:TPU:4, one launch (start us, length us, event | category | flops | bytes accessed | tf_op | source)
XLA Modules:
  0.0 138.8 jit_solution(3205961484773908725)
XLA Ops:
  0.0 0.7 convert_bitcast_fusion.1
  0.7 0.9 fusion.27
  1.7 7.3 %collective-permute-start = (bf16[144,256]{1,0:T(8,128)(2,1)S(1)}, bf16[144,256]{1,0:T(8,128)(2,1)S(1)}, u32[]{:S(2)}, u32[]{:S(2)}) collective-permute-start(bf16[144,256]{1,0:T(8,128)(2,1)S(1)} %fusion.38), channel_id=1, source_target_pairs={{0,8},{1,9},{2,10},{3,11},{4,12},{5,13},{6,14},{7,15},{8,0},{9,1},... | collective-permute-start | bytes 221192 | tf_op jit(solution)/shard_map/ppermute | solution.py:26
  8.9 0.7 fusion.51
  9.8 0.8 fusion.48
  11.1 0.6 collective-permute-done
  12.2 1.3 collective-permute-start.1
  13.5 0.8 collective-permute-start.2
  14.3 1.2 collective-permute-start.3
  15.6 0.7 collective-permute-done.1
  16.3 2.7 %collective-permute-done.2 = bf16[2,40,256]{2,1,0:T(8,128)(2,1)S(1)} collective-permute-done((bf16[2,40,256]{2,1,0:T(8,128)(2,1)S(1)}, bf16[2,40,256]{2,1,0:T(8,128)(2,1)S(1)}, u32[]{:S(2)}, u32[]{:S(2)}) %collective-permute-start.2) | collective-permute-done | bytes 40992 | tf_op jit(solution)/shard_map/ppermute | solution.py:26
  19.1 1.8 %collective-permute-start.6 = (bf16[336,256]{1,0:T(8,128)(2,1)S(1)}, bf16[336,256]{1,0:T(8,128)(2,1)S(1)}, u32[]{:S(2)}, u32[]{:S(2)}) collective-permute-start(bf16[336,256]{1,0:T(8,128)(2,1)S(1)} %concatenate.24), channel_id=1, source_target_pairs={{0,64},{1,65},{2,66},{3,67},{4,68},{5,69},{6,70},{7,71},{8,72},{9,... | collective-permute-start | bytes 516104 | tf_op jit(solution)/shard_map/ppermute | solution.py:26
  21.0 3.7 %collective-permute-done.6 = bf16[336,256]{1,0:T(8,128)(2,1)S(1)} collective-permute-done((bf16[336,256]{1,0:T(8,128)(2,1)S(1)}, bf16[336,256]{1,0:T(8,128)(2,1)S(1)}, u32[]{:S(2)}, u32[]{:S(2)}) %collective-permute-start.6) | collective-permute-done | bytes 172064 | tf_op jit(solution)/shard_map/ppermute | solution.py:26
  24.7 3.1 %collective-permute-start.10 = (bf16[2,336,256]{2,1,0:T(8,128)(2,1)S(1)}, bf16[2,336,256]{2,1,0:T(8,128)(2,1)S(1)}, u32[]{:S(2)}, u32[]{:S(2)}) collective-permute-start(bf16[2,336,256]{2,1,0:T(8,128)(2,1)S(1)} %pad_maximum_fusion.1.refs_0_), channel_id=1, source_target_pairs={{0,48},{1,49},{2,50},{3,51},{4,52},{5,53},{6,54},{7,55},{8,56},{9,... | collective-permute-start | bytes 1032200 | tf_op jit(solution)/shard_map/ppermute | solution.py:26
  27.9 3.9 %collective-permute-start.4 = (bf16[336,256]{1,0:T(8,128)(2,1)S(1)}, bf16[336,256]{1,0:T(8,128)(2,1)S(1)}, u32[]{:S(2)}, u32[]{:S(2)}) collective-permute-start(bf16[336,256]{1,0:T(8,128)(2,1)S(1)} %concatenate.24), channel_id=1, source_target_pairs={{0,128},{1,129},{2,130},{3,131},{4,132},{5,133},{6,134},{7,135},{8... | collective-permute-start | bytes 516104 | tf_op jit(solution)/shard_map/ppermute | solution.py:26
  32.0 8.8 %collective-permute-done.4 = bf16[336,256]{1,0:T(8,128)(2,1)S(1)} collective-permute-done((bf16[336,256]{1,0:T(8,128)(2,1)S(1)}, bf16[336,256]{1,0:T(8,128)(2,1)S(1)}, u32[]{:S(2)}, u32[]{:S(2)}) %collective-permute-start.4) | collective-permute-done | bytes 172064 | tf_op jit(solution)/shard_map/ppermute | solution.py:26
  40.9 0.7 collective-permute-start.17
  41.6 2.7 %collective-permute-start.11 = (bf16[2,336,256]{2,1,0:T(8,128)(2,1)S(1)}, bf16[2,336,256]{2,1,0:T(8,128)(2,1)S(1)}, u32[]{:S(2)}, u32[]{:S(2)}) collective-permute-start(bf16[2,336,256]{2,1,0:T(8,128)(2,1)S(1)} %broadcast_select_fusion.1), channel_id=1, source_target_pairs={{0,48},{1,17},{2,50},{3,19},{4,52},{5,21},{6,54},{7,23},{8,56},{9,... | collective-permute-start | bytes 1032200 | tf_op jit(solution)/shard_map/ppermute | solution.py:26
  44.3 0.6 collective-permute-start.15
  44.9 0.5 collective-permute-start.13
  45.4 4.0 %collective-permute-done.17.refs_6_ = bf16[2,336,256]{2,1,0:T(8,128)(2,1)S(1)} collective-permute-done((bf16[2,336,256]{2,1,0:T(8,128)(2,1)S(1)}, bf16[2,336,256]{2,1,0:T(8,128)(2,1)S(1)}, u32[]{:S(2)}, u32[]{:S(2)}) %collective-permute-start.17) | collective-permute-done | bytes 344096 | tf_op jit(solution)/shard_map/ppermute | solution.py:26
  49.4 3.7 %collective-permute-done.11.refs_4_ = bf16[2,336,256]{2,1,0:T(8,128)(2,1)S(1)} collective-permute-done((bf16[2,336,256]{2,1,0:T(8,128)(2,1)S(1)}, bf16[2,336,256]{2,1,0:T(8,128)(2,1)S(1)}, u32[]{:S(2)}, u32[]{:S(2)}) %collective-permute-start.11) | collective-permute-done | bytes 344096 | tf_op jit(solution)/shard_map/ppermute | solution.py:26
  53.1 0.8 broadcast_select_fusion
  53.9 0.6 collective-permute-start.18
  54.6 4.0 %copy.17 = bf16[512,8,2,384]{3,1,2,0:T(8,128)(2,1)S(1)} copy(bf16[512,8,2,384]{3,2,1,0:T(2,128)(2,1)} %bitcast.136) | data formatting | bytes 12582912
  58.6 7.8 %shard_map.64 = (f32[640,768]{1,0:T(8,128)S(1)}, f32[640,256]{1,0:T(8,128)S(1)}, f32[16,256]{1,0:T(8,128)S(1)}, bf16[2,1024,768]{2,1,0:T(8,128)(2,1)S(1)}, bf16[384,4096]{1,0:T(8,128)(2,1)S(1)}) custom-call(s32[2]{0:T(128)S(1)} %pad_add_fusion.1.place, bf16[2,336,256]{2,1,0:T(8,128)(2,1)S(1)} %pad_maximum_fusion.1.refs_0_, ...), custom_call_target="tpu_custom_call" | custom-call | flops 2013265920 | bytes 8388608 | tf_op jit(solution)/shard_map/pallas_call | solution.py:171
  66.5 0.3 collective-permute-start.20
  66.8 0.3 collective-permute-start.19
  67.3 0.3 collective-permute-start.14
  67.6 0.6 collective-permute-done.20.refs_7_
  68.2 0.7 collective-permute-done.19.refs_5_
  68.9 0.3 collective-permute-done.16.refs_3_
  69.2 0.5 collective-permute-done.14.refs_1_
  69.7 6.9 %shard_map.65 = (bf16[640,384]{1,0:T(8,128)(2,1)S(1)}, f32[2,320,256]{2,1,0:T(8,128)S(1)}, f32[2,320,256]{2,1,0:T(8,128)S(1)}, f32[2,320,256]{2,1,0:T(8,128)S(1)...) custom-call(s32[2]{0:T(128)S(1)} %pad_add_fusion.1.place, ...), custom_call_target="tpu_custom_call" | custom-call | flops 4026531840 | bytes 8388608 | tf_op jit(solution)/shard_map/pallas_call | solution.py:171
  76.6 0.3 collective-permute-start.26
  76.9 3.1 %shard_map.66 = (f32[2,320,256]{2,1,0:T(8,128)S(1)}, f32[2,320,256]{2,1,0:T(8,128)S(1)}, f32[2,320,256]{2,1,0:T(8,128)S(1)}, f32[2,320,256]{2,1,0:T(8,128)S(1)}, bf16[4,2,320,256]{3,2,1,0:T(8,128)(2,1)}) custom-call(s32[2]{0:T(128)S(1)} %pad_add_fusion.1.place, bf16[640,384]{1,0:T(8,128)(2,1)S(1)} %get-tuple-element.50.act, ...), custom_call_target="tpu_custom_call" | custom-call | flops 1006632960 | bytes 8388608 | tf_op jit(solution)/shard_map/pallas_call | solution.py:171
  80.0 0.3 collective-permute-start.21
  80.3 0.9 fusion.11
  81.5 2.7 %collective-permute-start.27 = (bf16[2,320,256]{2,1,0:T(8,128)(2,1)}, bf16[2,320,256]{2,1,0:T(8,128)(2,1)}, u32[]{:S(2)}, u32[]{:S(2)}) collective-permute-start(bf16[2,320,256]{2,1,0:T(8,128)(2,1)} %fusion.11), channel_id=1, source_target_pairs={{0,48},{1,17},{2,50},{3,19},{4,52},{5,21},{6,54},{7,23},{8,56},{9,... | collective-permute-start | bytes 983048 | tf_op jit(solution)/shard_map/ppermute | solution.py:26
  84.2 1.2 fusion.15
  85.4 1.8 %collective-permute-start.22 = (bf16[2,320,256]{2,1,0:T(8,128)(2,1)S(1)}, bf16[2,320,256]{2,1,0:T(8,128)(2,1)S(1)}, u32[]{:S(2)}, u32[]{:S(2)}) collective-permute-start(bf16[2,320,256]{2,1,0:T(8,128)(2,1)S(1)} %fusion.15), channel_id=1, source_target_pairs={{0,48},{1,17},{2,50},{3,19},{4,52},{5,21},{6,54},{7,23},{8,56},{9,... | collective-permute-start | bytes 983048 | tf_op jit(solution)/shard_map/ppermute | solution.py:26
  87.1 3.0 %collective-permute-done.27 = bf16[2,320,256]{2,1,0:T(8,128)(2,1)} collective-permute-done((bf16[2,320,256]{2,1,0:T(8,128)(2,1)}, bf16[2,320,256]{2,1,0:T(8,128)(2,1)}, u32[]{:S(2)}, u32[]{:S(2)}) %collective-permute-start.27) | collective-permute-done | bytes 327712 | tf_op jit(solution)/shard_map/ppermute | solution.py:26
  90.1 1.4 %fusion.8 = (bf16[2,320,256]{2,1,0:T(8,128)(2,1)S(1)}, bf16[2,320,256]{2,1,0:T(8,128)(2,1)S(1)}) fusion(bf16[2,320,256]{2,1,0:T(8,128)(2,1)} %collective-permute-done.27, f32[2,320,256]{2,1,0:T(8,128)S(1)} %copy-done.3, bf16[4,2,320,256]{3,2,1,0:T(8,128)(2,1)} %copy-done.8, pred[]{:T(512)S(6)} %eq.111, f32[2,320,256]{2,1,0:T(8,128)S(1)} %copy-done.5), kind=kLoop, calls=%fused_computation.17 | loop fusion | flops 1802240 | bytes 2949121 | tf_op jit(solution)/shard_map/convert_element_type | solution.py:304
  91.7 2.7 %collective-permute-start.29 = (bf16[2,320,256]{2,1,0:T(8,128)(2,1)S(1)}, bf16[2,320,256]{2,1,0:T(8,128)(2,1)S(1)}, u32[]{:S(2)}, u32[]{:S(2)}) collective-permute-start(bf16[2,320,256]{2,1,0:T(8,128)(2,1)S(1)} %get-tuple-element.62), channel_id=1, source_target_pairs={{0,48},{1,49},{2,50},{3,51},{4,52},{5,53},{6,54},{7,55},{8,56},{9,... | collective-permute-start | bytes 983048 | tf_op jit(solution)/shard_map/ppermute | solution.py:26
  94.4 1.3 fusion.4
  95.7 1.4 %collective-permute-start.23 = (bf16[2,320,256]{2,1,0:T(8,128)(2,1)S(1)}, bf16[2,320,256]{2,1,0:T(8,128)(2,1)S(1)}, u32[]{:S(2)}, u32[]{:S(2)}) collective-permute-start(bf16[2,320,256]{2,1,0:T(8,128)(2,1)S(1)} %get-tuple-element.63), channel_id=1, source_target_pairs={{0,16},{1,17},{2,18},{3,19},{4,20},{5,21},{6,22},{7,23},{8,24},{9,... | collective-permute-start | bytes 983048 | tf_op jit(solution)/shard_map/ppermute | solution.py:26
  97.2 0.6 collective-permute-start.24
  97.8 4.5 %collective-permute-done.28 = bf16[2,320,256]{2,1,0:T(8,128)(2,1)S(1)} collective-permute-done((bf16[2,320,256]{2,1,0:T(8,128)(2,1)S(1)}, bf16[2,320,256]{2,1,0:T(8,128)(2,1)S(1)}, u32[]{:S(2)}, u32[]{:S(2)}) %collective-permute-start.28) | collective-permute-done | bytes 327712 | tf_op jit(solution)/shard_map/ppermute | solution.py:26
  102.3 1.3 collective-permute-done.29
  103.6 1.2 fusion.14
  104.8 6.0 %collective-permute-start.30 = (bf16[320,256]{1,0:T(8,128)(2,1)S(1)}, bf16[320,256]{1,0:T(8,128)(2,1)S(1)}, u32[]{:S(2)}, u32[]{:S(2)}) collective-permute-start(bf16[320,256]{1,0:T(8,128)(2,1)S(1)} %get-tuple-element.65), channel_id=1, source_target_pairs={{0,128},{1,129},{2,130},{3,131},{4,132},{5,133},{6,134},{7,135},{8... | collective-permute-start | bytes 491528 | tf_op jit(solution)/shard_map/ppermute | solution.py:26
  110.8 1.2 collective-permute-start.31
  112.0 1.1 fusion.17
  113.2 0.5 collective-permute-start.25
  113.8 2.8 %collective-permute-done.30 = bf16[320,256]{1,0:T(8,128)(2,1)S(1)} collective-permute-done((bf16[320,256]{1,0:T(8,128)(2,1)S(1)}, bf16[320,256]{1,0:T(8,128)(2,1)S(1)}, u32[]{:S(2)}, u32[]{:S(2)}) %collective-permute-start.30) | collective-permute-done | bytes 163872 | tf_op jit(solution)/shard_map/ppermute | solution.py:26
  116.6 2.4 %collective-permute-done.31 = bf16[320,256]{1,0:T(8,128)(2,1)S(1)} collective-permute-done((bf16[320,256]{1,0:T(8,128)(2,1)S(1)}, bf16[320,256]{1,0:T(8,128)(2,1)S(1)}, u32[]{:S(2)}, u32[]{:S(2)}) %collective-permute-start.31) | collective-permute-done | bytes 163872 | tf_op jit(solution)/shard_map/ppermute | solution.py:26
  118.9 1.3 collective-permute-done.25
  120.3 0.5 collective-permute-start.32
  120.8 4.4 %collective-permute-start.33 = (bf16[2,40,256]{2,1,0:T(8,128)(2,1)S(1)}, bf16[2,40,256]{2,1,0:T(8,128)(2,1)S(1)}, u32[]{:S(2)}, u32[]{:S(2)}) collective-permute-start(bf16[2,40,256]{2,1,0:T(8,128)(2,1)S(1)} %bitcast.151), channel_id=1, source_target_pairs={{0,4},{1,5},{2,6},{3,7},{4,0},{5,1},{6,2},{7,3},{8,12},{9,13},{10,... | collective-permute-start | bytes 122888 | tf_op jit(solution)/shard_map/ppermute | solution.py:26
  125.2 2.0 %collective-permute-done.33 = bf16[2,40,256]{2,1,0:T(8,128)(2,1)S(1)} collective-permute-done((bf16[2,40,256]{2,1,0:T(8,128)(2,1)S(1)}, bf16[2,40,256]{2,1,0:T(8,128)(2,1)S(1)}, u32[]{:S(2)}, u32[]{:S(2)}) %collective-permute-start.33) | collective-permute-done | bytes 40992 | tf_op jit(solution)/shard_map/ppermute | solution.py:26
  127.2 2.0 %collective-permute-done.34 = bf16[2,40,256]{2,1,0:T(8,128)(2,1)S(1)} collective-permute-done((bf16[2,40,256]{2,1,0:T(8,128)(2,1)S(1)}, bf16[2,40,256]{2,1,0:T(8,128)(2,1)S(1)}, u32[]{:S(2)}, u32[]{:S(2)}) %collective-permute-start.34) | collective-permute-done | bytes 40992 | tf_op jit(solution)/shard_map/ppermute | solution.py:26
  129.3 4.3 %collective-permute-start.35 = (bf16[4,40,256]{2,1,0:T(8,128)(2,1)S(1)}, bf16[4,40,256]{2,1,0:T(8,128)(2,1)S(1)}, u32[]{:S(2)}, u32[]{:S(2)}) collective-permute-start(bf16[4,40,256]{2,1,0:T(8,128)(2,1)S(1)} %get-tuple-element.68), channel_id=1, source_target_pairs={{0,8},{1,9},{2,10},{3,11},{4,12},{5,13},{6,14},{7,15},{8,0},{9,1},... | collective-permute-start | bytes 245768 | tf_op jit(solution)/shard_map/ppermute | solution.py:26
  133.6 4.1 %collective-permute-done.35 = bf16[4,40,256]{2,1,0:T(8,128)(2,1)S(1)} collective-permute-done((bf16[4,40,256]{2,1,0:T(8,128)(2,1)S(1)}, bf16[4,40,256]{2,1,0:T(8,128)(2,1)S(1)}, u32[]{:S(2)}, u32[]{:S(2)}) %collective-permute-start.35) | collective-permute-done | bytes 81952 | tf_op jit(solution)/shard_map/ppermute | solution.py:26
  137.9 0.9 fusion.2
  (94 shorter events, 3.1 us)
Async XLA Ops:
  0.0 10.9 %copy-start = (bf16[256,8]{0,1:T(8,128)(2,1)S(1)}, bf16[256,8]{0,1:T(8,128)(2,1)}, u32[]{:S(2)}) copy-start(bf16[256,8]{0,1:T(8,128)(2,1)} %param.10) | copy-start | bytes 12292
  1.7 10.0 %collective-permute-start = (bf16[144,256]{1,0:T(8,128)(2,1)S(1)}, bf16[144,256]{1,0:T(8,128)(2,1)S(1)}, u32[]{:S(2)}, u32[]{:S(2)}) collective-permute-start(bf16[144,256]{1,0:T(8,128)(2,1)S(1)} %fusion.38), channel_id=1, source_target_pairs={{0,8},{1,9},{2,10},{3,11},{4,12},{5,13},{6,14},{7,15},{8,0},{9,1},... | collective-permute-start | bytes 221192 | tf_op jit(solution)/shard_map/ppermute | solution.py:26
  12.2 4.1 %collective-permute-start.1 = (bf16[2,40,256]{2,1,0:T(8,128)(2,1)S(1)}, bf16[2,40,256]{2,1,0:T(8,128)(2,1)S(1)}, u32[]{:S(2)}, u32[]{:S(2)}) collective-permute-start(bf16[2,40,256]{2,1,0:T(8,128)(2,1)S(1)} %get-tuple-element.74), channel_id=1, source_target_pairs={{0,2},{1,3},{2,4},{3,5},{4,6},{5,7},{6,0},{7,1},{8,10},{9,11},{10,... | collective-permute-start | bytes 122888 | tf_op jit(solution)/shard_map/ppermute | solution.py:26
  13.5 5.5 %collective-permute-start.2 = (bf16[2,40,256]{2,1,0:T(8,128)(2,1)S(1)}, bf16[2,40,256]{2,1,0:T(8,128)(2,1)S(1)}, u32[]{:S(2)}, u32[]{:S(2)}) collective-permute-start(bf16[2,40,256]{2,1,0:T(8,128)(2,1)S(1)} %get-tuple-element.76), channel_id=1, source_target_pairs={{0,4},{1,5},{2,6},{3,7},{4,0},{5,1},{6,2},{7,3},{8,12},{9,13},{10,... | collective-permute-start | bytes 122888 | tf_op jit(solution)/shard_map/ppermute | solution.py:26
  14.3 4.7 %collective-permute-start.3 = (bf16[2,40,256]{2,1,0:T(8,128)(2,1)S(1)}, bf16[2,40,256]{2,1,0:T(8,128)(2,1)S(1)}, u32[]{:S(2)}, u32[]{:S(2)}) collective-permute-start(bf16[2,40,256]{2,1,0:T(8,128)(2,1)S(1)} %get-tuple-element.75), channel_id=1, source_target_pairs={{0,6},{1,7},{2,0},{3,1},{4,2},{5,3},{6,4},{7,5},{8,14},{9,15},{10,... | collective-permute-start | bytes 122888 | tf_op jit(solution)/shard_map/ppermute | solution.py:26
  19.1 5.5 %collective-permute-start.6 = (bf16[336,256]{1,0:T(8,128)(2,1)S(1)}, bf16[336,256]{1,0:T(8,128)(2,1)S(1)}, u32[]{:S(2)}, u32[]{:S(2)}) collective-permute-start(bf16[336,256]{1,0:T(8,128)(2,1)S(1)} %concatenate.24), channel_id=1, source_target_pairs={{0,64},{1,65},{2,66},{3,67},{4,68},{5,69},{6,70},{7,71},{8,72},{9,... | collective-permute-start | bytes 516104 | tf_op jit(solution)/shard_map/ppermute | solution.py:26
  24.7 16.9 %collective-permute-start.10 = (bf16[2,336,256]{2,1,0:T(8,128)(2,1)S(1)}, bf16[2,336,256]{2,1,0:T(8,128)(2,1)S(1)}, u32[]{:S(2)}, u32[]{:S(2)}) collective-permute-start(bf16[2,336,256]{2,1,0:T(8,128)(2,1)S(1)} %pad_maximum_fusion.1.refs_0_), channel_id=1, source_target_pairs={{0,48},{1,49},{2,50},{3,51},{4,52},{5,53},{6,54},{7,55},{8,56},{9,... | collective-permute-start | bytes 1032200 | tf_op jit(solution)/shard_map/ppermute | solution.py:26
  27.8 13.8 %collective-permute-start.8 = (bf16[2,336,256]{2,1,0:T(8,128)(2,1)S(1)}, bf16[2,336,256]{2,1,0:T(8,128)(2,1)S(1)}, u32[]{:S(2)}, u32[]{:S(2)}) collective-permute-start(bf16[2,336,256]{2,1,0:T(8,128)(2,1)S(1)} %pad_maximum_fusion.1.refs_0_), channel_id=1, source_target_pairs={{0,16},{1,17},{2,18},{3,19},{4,20},{5,21},{6,22},{7,23},{8,24},{9,... | collective-permute-start | bytes 1032200 | tf_op jit(solution)/shard_map/ppermute | solution.py:26
  27.9 12.9 %collective-permute-start.4 = (bf16[336,256]{1,0:T(8,128)(2,1)S(1)}, bf16[336,256]{1,0:T(8,128)(2,1)S(1)}, u32[]{:S(2)}, u32[]{:S(2)}) collective-permute-start(bf16[336,256]{1,0:T(8,128)(2,1)S(1)} %concatenate.24), channel_id=1, source_target_pairs={{0,128},{1,129},{2,130},{3,131},{4,132},{5,133},{6,134},{7,135},{8... | collective-permute-start | bytes 516104 | tf_op jit(solution)/shard_map/ppermute | solution.py:26
  31.8 9.0 %collective-permute-start.5 = (bf16[336,256]{1,0:T(8,128)(2,1)S(1)}, bf16[336,256]{1,0:T(8,128)(2,1)S(1)}, u32[]{:S(2)}, u32[]{:S(2)}) collective-permute-start(bf16[336,256]{1,0:T(8,128)(2,1)S(1)} %concatenate.24), channel_id=1, source_target_pairs={{0,192},{1,193},{2,194},{3,195},{4,196},{5,197},{6,198},{7,199},{8... | collective-permute-start | bytes 516104 | tf_op jit(solution)/shard_map/ppermute | solution.py:26
  40.9 12.3 %copy-start.6 = (bf16[2,336,256]{2,1,0:T(8,128)(2,1)}, bf16[2,336,256]{2,1,0:T(8,128)(2,1)S(1)}, u32[]{:S(2)}) copy-start(bf16[2,336,256]{2,1,0:T(8,128)(2,1)S(1)} %pad_maximum_fusion.refs_0_) | copy-start | bytes 1032196
  40.9 8.5 %collective-permute-start.17 = (bf16[2,336,256]{2,1,0:T(8,128)(2,1)S(1)}, bf16[2,336,256]{2,1,0:T(8,128)(2,1)S(1)}, u32[]{:S(2)}, u32[]{:S(2)}) collective-permute-start(bf16[2,336,256]{2,1,0:T(8,128)(2,1)S(1)} %pad_maximum_fusion.refs_0_), channel_id=1, source_target_pairs={{0,48},{1,49},{2,50},{3,51},{4,52},{5,53},{6,54},{7,55},{8,56},{9,... | collective-permute-start | bytes 1032200 | tf_op jit(solution)/shard_map/ppermute | solution.py:26
  41.6 11.5 %collective-permute-start.11 = (bf16[2,336,256]{2,1,0:T(8,128)(2,1)S(1)}, bf16[2,336,256]{2,1,0:T(8,128)(2,1)S(1)}, u32[]{:S(2)}, u32[]{:S(2)}) collective-permute-start(bf16[2,336,256]{2,1,0:T(8,128)(2,1)S(1)} %broadcast_select_fusion.1), channel_id=1, source_target_pairs={{0,48},{1,17},{2,50},{3,19},{4,52},{5,21},{6,54},{7,23},{8,56},{9,... | collective-permute-start | bytes 1032200 | tf_op jit(solution)/shard_map/ppermute | solution.py:26
  44.3 8.8 %collective-permute-start.15 = (bf16[2,336,256]{2,1,0:T(8,128)(2,1)S(1)}, bf16[2,336,256]{2,1,0:T(8,128)(2,1)S(1)}, u32[]{:S(2)}, u32[]{:S(2)}) collective-permute-start(bf16[2,336,256]{2,1,0:T(8,128)(2,1)S(1)} %pad_maximum_fusion.refs_0_), channel_id=1, source_target_pairs={{0,16},{1,17},{2,18},{3,19},{4,20},{5,21},{6,22},{7,23},{8,24},{9,... | collective-permute-start | bytes 1032200 | tf_op jit(solution)/shard_map/ppermute | solution.py:26
  44.9 13.7 %collective-permute-start.7 = (bf16[2,336,256]{2,1,0:T(8,128)(2,1)S(1)}, bf16[2,336,256]{2,1,0:T(8,128)(2,1)S(1)}, u32[]{:S(2)}, u32[]{:S(2)}) collective-permute-start(bf16[2,336,256]{2,1,0:T(8,128)(2,1)S(1)} %pad_maximum_fusion.1.refs_0_), channel_id=1, source_target_pairs={{0,1},{1,0},{2,3},{3,2},{4,5},{5,4},{6,7},{7,6},{8,9},{9,8},{10,11... | collective-permute-start | bytes 1032200 | tf_op jit(solution)/shard_map/ppermute | solution.py:26
  44.9 13.7 %collective-permute-start.13 = (bf16[2,336,256]{2,1,0:T(8,128)(2,1)S(1)}, bf16[2,336,256]{2,1,0:T(8,128)(2,1)S(1)}, u32[]{:S(2)}, u32[]{:S(2)}) collective-permute-start(bf16[2,336,256]{2,1,0:T(8,128)(2,1)S(1)} %collective-permute-done.10.refs_6_), channel_id=1, source_target_pairs={{0,1},{1,0},{2,3},{3,2},{4,5},{5,4},{6,7},{7,6},{8,9},{9,8},{10,11... | collective-permute-start | bytes 1032200 | tf_op jit(solution)/shard_map/ppermute | solution.py:26
  49.4 9.2 %collective-permute-start.9 = (bf16[2,336,256]{2,1,0:T(8,128)(2,1)S(1)}, bf16[2,336,256]{2,1,0:T(8,128)(2,1)S(1)}, u32[]{:S(2)}, u32[]{:S(2)}) collective-permute-start(bf16[2,336,256]{2,1,0:T(8,128)(2,1)S(1)} %collective-permute-done.8.refs_2_), channel_id=1, source_target_pairs={{0,1},{1,0},{2,3},{3,2},{4,5},{5,4},{6,7},{7,6},{8,9},{9,8},{10,11... | collective-permute-start | bytes 1032200 | tf_op jit(solution)/shard_map/ppermute | solution.py:26
  53.1 5.5 %collective-permute-start.12 = (bf16[2,336,256]{2,1,0:T(8,128)(2,1)S(1)}, bf16[2,336,256]{2,1,0:T(8,128)(2,1)S(1)}, u32[]{:S(2)}, u32[]{:S(2)}) collective-permute-start(bf16[2,336,256]{2,1,0:T(8,128)(2,1)S(1)} %collective-permute-done.11.refs_4_), channel_id=1, source_target_pairs={{0,1},{1,0},{2,3},{3,2},{4,5},{5,4},{6,7},{7,6},{8,9},{9,8},{10,11... | collective-permute-start | bytes 1032200 | tf_op jit(solution)/shard_map/ppermute | solution.py:26
  53.9 12.9 %collective-permute-start.18 = (bf16[2,336,256]{2,1,0:T(8,128)(2,1)}, bf16[2,336,256]{2,1,0:T(8,128)(2,1)}, u32[]{:S(2)}, u32[]{:S(2)}) collective-permute-start(bf16[2,336,256]{2,1,0:T(8,128)(2,1)} %broadcast_select_fusion), channel_id=1, source_target_pairs={{0,48},{1,17},{2,50},{3,19},{4,52},{5,21},{6,54},{7,23},{8,56},{9,... | collective-permute-start | bytes 1032200 | tf_op jit(solution)/shard_map/ppermute | solution.py:26
  54.6 4.1 %copy-start.1 = (bf16[1,384,4096]{2,1,0:T(8,128)(2,1)S(1)}, bf16[1,384,4096]{2,1,0:T(8,128)(2,1)}, u32[]{:S(2)}) copy-start(bf16[1,384,4096]{2,1,0:T(8,128)(2,1)} %param.12) | copy-start | bytes 9437188
  58.6 8.6 %copy-start.7 = (bf16[2,336,256]{2,1,0:T(8,128)(2,1)S(1)}, bf16[2,336,256]{2,1,0:T(8,128)(2,1)}, u32[]{:S(2)}) copy-start(bf16[2,336,256]{2,1,0:T(8,128)(2,1)} %copy-done.6) | copy-start | bytes 1032196
  66.5 1.7 %collective-permute-start.20 = (bf16[2,336,256]{2,1,0:T(8,128)(2,1)S(1)}, bf16[2,336,256]{2,1,0:T(8,128)(2,1)S(1)}, u32[]{:S(2)}, u32[]{:S(2)}) collective-permute-start(bf16[2,336,256]{2,1,0:T(8,128)(2,1)S(1)} %collective-permute-done.17.refs_6_), channel_id=1, source_target_pairs={{0,1},{1,0},{2,3},{3,2},{4,5},{5,4},{6,7},{7,6},{8,9},{9,8},{10,11... | collective-permute-start | bytes 1032200 | tf_op jit(solution)/shard_map/ppermute | solution.py:26
  66.8 2.1 %collective-permute-start.19 = (bf16[2,336,256]{2,1,0:T(8,128)(2,1)}, bf16[2,336,256]{2,1,0:T(8,128)(2,1)S(1)}, u32[]{:S(2)}, u32[]{:S(2)}) collective-permute-start(bf16[2,336,256]{2,1,0:T(8,128)(2,1)} %collective-permute-done.18.refs_4_), channel_id=1, source_target_pairs={{0,1},{1,0},{2,3},{3,2},{4,5},{5,4},{6,7},{7,6},{8,9},{9,8},{10,11... | collective-permute-start | bytes 1032200 | tf_op jit(solution)/shard_map/ppermute | solution.py:26
  67.1 2.1 %collective-permute-start.16 = (bf16[2,336,256]{2,1,0:T(8,128)(2,1)S(1)}, bf16[2,336,256]{2,1,0:T(8,128)(2,1)S(1)}, u32[]{:S(2)}, u32[]{:S(2)}) collective-permute-start(bf16[2,336,256]{2,1,0:T(8,128)(2,1)S(1)} %collective-permute-done.15.refs_2_), channel_id=1, source_target_pairs={{0,1},{1,0},{2,3},{3,2},{4,5},{5,4},{6,7},{7,6},{8,9},{9,8},{10,11... | collective-permute-start | bytes 1032200 | tf_op jit(solution)/shard_map/ppermute | solution.py:26
  67.3 2.4 %collective-permute-start.14 = (bf16[2,336,256]{2,1,0:T(8,128)(2,1)S(1)}, bf16[2,336,256]{2,1,0:T(8,128)(2,1)S(1)}, u32[]{:S(2)}, u32[]{:S(2)}) collective-permute-start(bf16[2,336,256]{2,1,0:T(8,128)(2,1)S(1)} %copy-done.7), channel_id=1, source_target_pairs={{0,1},{1,0},{2,3},{3,2},{4,5},{5,4},{6,7},{7,6},{8,9},{9,8},{10,11... | collective-permute-start | bytes 1032200 | tf_op jit(solution)/shard_map/ppermute | solution.py:26
  76.6 3.5 %copy-start.2 = (f32[2,320,256]{2,1,0:T(8,128)}, f32[2,320,256]{2,1,0:T(8,128)S(1)}, u32[]{:S(2)}) copy-start(f32[2,320,256]{2,1,0:T(8,128)S(1)} %get-tuple-element.58) | copy-start | bytes 1966084
  76.6 3.4 %copy-start.4 = (f32[2,320,256]{2,1,0:T(8,128)}, f32[2,320,256]{2,1,0:T(8,128)S(1)}, u32[]{:S(2)}) copy-start(f32[2,320,256]{2,1,0:T(8,128)S(1)} %get-tuple-element.60) | copy-start | bytes 1966084
  76.6 3.7 %collective-permute-start.26 = (bf16[4,2,320,256]{3,2,1,0:T(8,128)(2,1)S(1)}, bf16[4,2,320,256]{3,2,1,0:T(8,128)(2,1)S(1)}, u32[]{:S(2)}, u32[]{:S(2)}) collective-permute-start(bf16[4,2,320,256]{3,2,1,0:T(8,128)(2,1)S(1)} %get-tuple-element.57), channel_id=1, source_target_pairs={{0,1},{1,0},{2,3},{3,2},{4,5},{5,4},{6,7},{7,6},{8,9},{9,8},{10,11... | collective-permute-start | bytes 3932168 | tf_op jit(solution)/shard_map/ppermute | solution.py:26
  80.0 4.2 %collective-permute-start.21 = (bf16[4,2,320,256]{3,2,1,0:T(8,128)(2,1)}, bf16[4,2,320,256]{3,2,1,0:T(8,128)(2,1)}, u32[]{:S(2)}, u32[]{:S(2)}) collective-permute-start(bf16[4,2,320,256]{3,2,1,0:T(8,128)(2,1)} %get-tuple-element.52), channel_id=1, source_target_pairs={{0,1},{1,0},{2,3},{3,2},{4,5},{5,4},{6,7},{7,6},{8,9},{9,8},{10,11... | collective-permute-start | bytes 3932168 | tf_op jit(solution)/shard_map/ppermute | solution.py:26
  80.3 1.2 copy-start.8
  81.5 8.6 %collective-permute-start.27 = (bf16[2,320,256]{2,1,0:T(8,128)(2,1)}, bf16[2,320,256]{2,1,0:T(8,128)(2,1)}, u32[]{:S(2)}, u32[]{:S(2)}) collective-permute-start(bf16[2,320,256]{2,1,0:T(8,128)(2,1)} %fusion.11), channel_id=1, source_target_pairs={{0,48},{1,17},{2,50},{3,19},{4,52},{5,21},{6,54},{7,23},{8,56},{9,... | collective-permute-start | bytes 983048 | tf_op jit(solution)/shard_map/ppermute | solution.py:26
  84.2 5.9 %copy-start.3 = (f32[2,320,256]{2,1,0:T(8,128)S(1)}, f32[2,320,256]{2,1,0:T(8,128)}, u32[]{:S(2)}) copy-start(f32[2,320,256]{2,1,0:T(8,128)} %copy-done.2) | copy-start | bytes 1966084
  84.2 5.9 %copy-start.5 = (f32[2,320,256]{2,1,0:T(8,128)S(1)}, f32[2,320,256]{2,1,0:T(8,128)}, u32[]{:S(2)}) copy-start(f32[2,320,256]{2,1,0:T(8,128)} %copy-done.4) | copy-start | bytes 1966084
  85.4 9.0 %collective-permute-start.22 = (bf16[2,320,256]{2,1,0:T(8,128)(2,1)S(1)}, bf16[2,320,256]{2,1,0:T(8,128)(2,1)S(1)}, u32[]{:S(2)}, u32[]{:S(2)}) collective-permute-start(bf16[2,320,256]{2,1,0:T(8,128)(2,1)S(1)} %fusion.15), channel_id=1, source_target_pairs={{0,48},{1,17},{2,50},{3,19},{4,52},{5,21},{6,54},{7,23},{8,56},{9,... | collective-permute-start | bytes 983048 | tf_op jit(solution)/shard_map/ppermute | solution.py:26
  91.6 10.7 %collective-permute-start.28 = (bf16[2,320,256]{2,1,0:T(8,128)(2,1)S(1)}, bf16[2,320,256]{2,1,0:T(8,128)(2,1)S(1)}, u32[]{:S(2)}, u32[]{:S(2)}) collective-permute-start(bf16[2,320,256]{2,1,0:T(8,128)(2,1)S(1)} %get-tuple-element.61), channel_id=1, source_target_pairs={{0,16},{1,17},{2,18},{3,19},{4,20},{5,21},{6,22},{7,23},{8,24},{9,... | collective-permute-start | bytes 983048 | tf_op jit(solution)/shard_map/ppermute | solution.py:26
  91.7 11.9 %collective-permute-start.29 = (bf16[2,320,256]{2,1,0:T(8,128)(2,1)S(1)}, bf16[2,320,256]{2,1,0:T(8,128)(2,1)S(1)}, u32[]{:S(2)}, u32[]{:S(2)}) collective-permute-start(bf16[2,320,256]{2,1,0:T(8,128)(2,1)S(1)} %get-tuple-element.62), channel_id=1, source_target_pairs={{0,48},{1,49},{2,50},{3,51},{4,52},{5,53},{6,54},{7,55},{8,56},{9,... | collective-permute-start | bytes 983048 | tf_op jit(solution)/shard_map/ppermute | solution.py:26
  95.7 16.3 %collective-permute-start.23 = (bf16[2,320,256]{2,1,0:T(8,128)(2,1)S(1)}, bf16[2,320,256]{2,1,0:T(8,128)(2,1)S(1)}, u32[]{:S(2)}, u32[]{:S(2)}) collective-permute-start(bf16[2,320,256]{2,1,0:T(8,128)(2,1)S(1)} %get-tuple-element.63), channel_id=1, source_target_pairs={{0,16},{1,17},{2,18},{3,19},{4,20},{5,21},{6,22},{7,23},{8,24},{9,... | collective-permute-start | bytes 983048 | tf_op jit(solution)/shard_map/ppermute | solution.py:26
  97.2 14.9 %collective-permute-start.24 = (bf16[2,320,256]{2,1,0:T(8,128)(2,1)S(1)}, bf16[2,320,256]{2,1,0:T(8,128)(2,1)S(1)}, u32[]{:S(2)}, u32[]{:S(2)}) collective-permute-start(bf16[2,320,256]{2,1,0:T(8,128)(2,1)S(1)} %get-tuple-element.64), channel_id=1, source_target_pairs={{0,48},{1,49},{2,50},{3,51},{4,52},{5,53},{6,54},{7,55},{8,56},{9,... | collective-permute-start | bytes 983048 | tf_op jit(solution)/shard_map/ppermute | solution.py:26
  104.8 11.7 %collective-permute-start.30 = (bf16[320,256]{1,0:T(8,128)(2,1)S(1)}, bf16[320,256]{1,0:T(8,128)(2,1)S(1)}, u32[]{:S(2)}, u32[]{:S(2)}) collective-permute-start(bf16[320,256]{1,0:T(8,128)(2,1)S(1)} %get-tuple-element.65), channel_id=1, source_target_pairs={{0,128},{1,129},{2,130},{3,131},{4,132},{5,133},{6,134},{7,135},{8... | collective-permute-start | bytes 491528 | tf_op jit(solution)/shard_map/ppermute | solution.py:26
  110.8 8.1 %collective-permute-start.31 = (bf16[320,256]{1,0:T(8,128)(2,1)S(1)}, bf16[320,256]{1,0:T(8,128)(2,1)S(1)}, u32[]{:S(2)}, u32[]{:S(2)}) collective-permute-start(bf16[320,256]{1,0:T(8,128)(2,1)S(1)} %get-tuple-element.66), channel_id=1, source_target_pairs={{0,192},{1,193},{2,194},{3,195},{4,196},{5,197},{6,198},{7,199},{8... | collective-permute-start | bytes 491528 | tf_op jit(solution)/shard_map/ppermute | solution.py:26
  112.0 1.7 %copy-start.10 = (s32[128,2]{0,1:T(2,128)S(1)}, s32[128,2]{0,1:T(2,128)}, u32[]{:S(2)}) copy-start(s32[128,2]{0,1:T(2,128)} %param.13) | copy-start | bytes 3076
  113.2 24.7 %copy-start.9 = (bf16[128,256]{1,0:T(8,128)(2,1)S(1)}, bf16[128,256]{1,0:T(8,128)(2,1)}, u32[]{:S(2)}) copy-start(bf16[128,256]{1,0:T(8,128)(2,1)} %param.8) | copy-start | bytes 196612
  113.2 7.0 %collective-permute-start.25 = (bf16[320,256]{1,0:T(8,128)(2,1)S(1)}, bf16[320,256]{1,0:T(8,128)(2,1)S(1)}, u32[]{:S(2)}, u32[]{:S(2)}) collective-permute-start(bf16[320,256]{1,0:T(8,128)(2,1)S(1)} %fusion.23), channel_id=1, source_target_pairs={{0,64},{1,65},{2,66},{3,67},{4,68},{5,69},{6,70},{7,71},{8,72},{9,... | collective-permute-start | bytes 491528 | tf_op jit(solution)/shard_map/ppermute | solution.py:26
  120.3 4.9 %collective-permute-start.32 = (bf16[2,40,256]{2,1,0:T(8,128)(2,1)S(1)}, bf16[2,40,256]{2,1,0:T(8,128)(2,1)S(1)}, u32[]{:S(2)}, u32[]{:S(2)}) collective-permute-start(bf16[2,40,256]{2,1,0:T(8,128)(2,1)S(1)} %bitcast.153), channel_id=1, source_target_pairs={{0,6},{1,7},{2,0},{3,1},{4,2},{5,3},{6,4},{7,5},{8,14},{9,15},{10,... | collective-permute-start | bytes 122888 | tf_op jit(solution)/shard_map/ppermute | solution.py:26
  120.8 6.4 %collective-permute-start.33 = (bf16[2,40,256]{2,1,0:T(8,128)(2,1)S(1)}, bf16[2,40,256]{2,1,0:T(8,128)(2,1)S(1)}, u32[]{:S(2)}, u32[]{:S(2)}) collective-permute-start(bf16[2,40,256]{2,1,0:T(8,128)(2,1)S(1)} %bitcast.151), channel_id=1, source_target_pairs={{0,4},{1,5},{2,6},{3,7},{4,0},{5,1},{6,2},{7,3},{8,12},{9,13},{10,... | collective-permute-start | bytes 122888 | tf_op jit(solution)/shard_map/ppermute | solution.py:26
  125.2 4.0 %collective-permute-start.34 = (bf16[2,40,256]{2,1,0:T(8,128)(2,1)S(1)}, bf16[2,40,256]{2,1,0:T(8,128)(2,1)S(1)}, u32[]{:S(2)}, u32[]{:S(2)}) collective-permute-start(bf16[2,40,256]{2,1,0:T(8,128)(2,1)S(1)} %bitcast.149), channel_id=1, source_target_pairs={{0,2},{1,3},{2,4},{3,5},{4,6},{5,7},{6,0},{7,1},{8,10},{9,11},{10,... | collective-permute-start | bytes 122888 | tf_op jit(solution)/shard_map/ppermute | solution.py:26
  129.3 8.4 %collective-permute-start.35 = (bf16[4,40,256]{2,1,0:T(8,128)(2,1)S(1)}, bf16[4,40,256]{2,1,0:T(8,128)(2,1)S(1)}, u32[]{:S(2)}, u32[]{:S(2)}) collective-permute-start(bf16[4,40,256]{2,1,0:T(8,128)(2,1)S(1)} %get-tuple-element.68), channel_id=1, source_target_pairs={{0,8},{1,9},{2,10},{3,11},{4,12},{5,13},{6,14},{7,15},{8,0},{9,1},... | collective-permute-start | bytes 245768 | tf_op jit(solution)/shard_map/ppermute | solution.py:26

commit v3 on v2

--- a/solution.py
+++ b/solution.py
@@ -115,6 +115,42 @@
         total[...] += jnp.dot(left, slab[n], preferred_element_type=F32)
 
 
+def arrange(place, blocks, rows, inverse, extras):
+    zl, y = place[0], place[1]
+    count = blocks[0].shape[1] - 16
+    sums = extras[...]
+    for j in range(NY):
+        for n in range(2):
+            k = ((zl ^ n) % 2) * NY + (y ^ j)
+            rows[k, :count] = blocks[2 * j][n, :count]
+            rows[k, count:] = blocks[2 * j + 1][n, :count]
+            extra = blocks[2 * j][n, count:].astype(F32)
+            sums += extra
+            inverse[pl.ds(k, 1), :] = 1.0 / (extra[9:10] + extra[10:11] + extra[11:12])
+    extras[...] = sums
+
+
+def near_square(rows, inverse, squares):
+    step = 32
+
+    def body(r, carry):
+        at = pl.ds(pl.multiple_of(r * step, step), step)
+        sums = squares[at, :]
+        for k in range(2 * NY):
+            plain = rows[k, at, :].astype(F32) * inverse[k : k + 1, :]
+            sums += plain * plain
+        squares[at, :] = sums
+        return carry
+
+    lax.fori_loop(0, rows.shape[1] // step, body, 0)
+
+
+def near_project(rows, w_up, first):
+    left = jnp.concatenate([rows[k] for k in range(2 * NY)], axis=1)
+    start = pl.multiple_of(first * (2 * NY * WIDTH), 2 * NY * WIDTH)
+    return jnp.dot(left, w_up[pl.ds(start, 2 * NY * WIDTH), :], preferred_element_type=F32)
+
+
 def expand(place, act, w_down, own, give, group):
     zl, y = place[0], place[1]
     count = act.shape[0] // 2
@@ -127,17 +163,16 @@
 
 
 def first_kernel(place, *refs):
-    blocks, refs = refs[:8], refs[8:]
-    w_up, w_down, total, squares, extras, next_slab, down, slab, sems, next_sems, sem = refs
-    copies = load(place, GROUPS[0], w_up, slab, sems)
-    later = load(place, GROUPS[1], w_up, next_slab, next_sems)
+    blocks, refs = refs[: 2 * NY], refs[2 * NY :]
+    w_up, w_down, total, squares, extras, next_slab, down, rows, inverse, sems, sem = refs
+    later = load(place, GROUPS[1], w_up, next_slab, sems)
     whole = pltpu.make_async_copy(w_down, down, sem)
     whole.start()
     squares[...] = jnp.zeros_like(squares)
     extras[...] = jnp.zeros_like(extras)
-    square(blocks, squares, extras)
-    total[...] = jnp.zeros_like(total)
-    project(blocks, total, slab, copies)
+    arrange(place, blocks, rows, inverse, extras)
+    total[...] = near_project(rows, w_up, place[0] // 2)
+    near_square(rows, inverse, squares)
     for copy in later:
         copy.wait()
     whole.wait()
@@ -166,8 +201,8 @@
 def call(kernel, out_shape, scratch, flops, remote, *args):
     vmem = pl.BlockSpec(memory_space=pltpu.VMEM)
     specs = [pl.BlockSpec(memory_space=pltpu.SMEM)] + [vmem] * (len(args) - 1)
-    for k in range(len(args) - remote, len(args)):
-        specs[k] = pl.BlockSpec(memory_space=pl.ANY)
+    if remote:
+        specs[-1] = pl.BlockSpec(memory_space=pl.ANY)
     return pl.pallas_call(
         kernel,
         out_shape=out_shape,
@@ -196,8 +231,9 @@
     out = (shape(totals[0], F32), shape(totals[1], F32), shape((16, WIDTH), F32))
     out += (shape(slab, BF16), shape(w_down.shape, BF16))
     sems = pltpu.SemaphoreType.DMA((len(GROUPS[0]) * NY,))
-    scratch = [pltpu.VMEM(slab, BF16), sems, sems, pltpu.SemaphoreType.DMA]
-    return call(first_kernel, out, scratch, flops, 2, place, *blocks, w_up, w_down)
+    scratch = [pltpu.VMEM((2 * NY, 2 * count, WIDTH), BF16), pltpu.VMEM((2 * NY, WIDTH), F32)]
+    scratch += [sems, pltpu.SemaphoreType.DMA]
+    return call(first_kernel, out, scratch, flops, True, place, *blocks, w_up, w_down)
 
 
 def expert_rest(place, blocks, state):
@@ -211,12 +247,12 @@
         (shape((2 * count, units), BF16),) + sums + (shape((16, WIDTH), F32),),
         [pltpu.VMEM(t, F32) for t in totals],
         2 * flops,
-        0,
+        False,
         place,
         *blocks,
         *state,
     )
-    first = call(third_kernel, sums, [], flops // 2, 0, place, act, state[-1])
+    first = call(third_kernel, sums, [], flops // 2, False, place, act, state[-1])
     return first, second, extras
 
 

time: 139 us -> 137 us (0.986)
  Pallas kernels: 17.8 us -> 15.6 us
    pallas_call x3, Pallas kernels: 17.8 us -> 15.6 us  [call(): pl.pallas_call(kernel, out_shape=out_shape, in_specs=specs, out_specs=(vm...]
  transfers between devices with their start and end apart: 36 -> 36, of which waited for: 20 -> 20; matrix products, arithmetic and copies ran while one was open for 10% -> 11% of each run, Pallas kernels for 8% -> 6%
where the time goes in v3:
time: 137 us
  starting transfers between devices  52.9 us (39%)
  waiting for transfers between devices  49.4 us (36%)
  Pallas kernels  15.6 us (11%)
  other arithmetic  11.8 us (9%)
  local copies, waits for them, and re-layouts  4.65 us (3%)
  matrix products  1.81 us (1%)
    ppermute x36, starting transfers between devices, move(): return lax.ppermute(value, ('section', 'dp'), pairs)  52.9 us
    ppermute x36, waiting for transfers between devices, move(): return lax.ppermute(value, ('section', 'dp'), pairs)  49.4 us
    pallas_call x3, Pallas kernels, call(): pl.pallas_call(kernel, out_shape=out_shape, in_specs=specs, out_specs=(vm...  15.6 us
    unnamed x23, local copies, waits for them, and re-layouts  4.34 us
    convert_element_type x2, other arithmetic, local(): one = xor_y((parts[1] + jnp.where(core == 0, passed, 0.0)).astype(BF16), 1)  2.78 us
  transfers between devices with their start and end apart: 36, of which 20 were waited for; matrix products, arithmetic and copies ran while one was open for 11% of the time, Pallas kernels for 6%

profile of v3, /device:TPU:4, one launch (start us, length us, event | category | flops | bytes accessed | tf_op | source)
XLA Modules:
  0.0 136.6 jit_solution(15703500602878978827)
XLA Ops:
  0.0 0.7 convert_bitcast_fusion.1
  0.7 0.9 fusion.27
  1.7 7.3 %collective-permute-start = (bf16[144,256]{1,0:T(8,128)(2,1)S(1)}, bf16[144,256]{1,0:T(8,128)(2,1)S(1)}, u32[]{:S(2)}, u32[]{:S(2)}) collective-permute-start(bf16[144,256]{1,0:T(8,128)(2,1)S(1)} %fusion.38), channel_id=1, source_target_pairs={{0,8},{1,9},{2,10},{3,11},{4,12},{5,13},{6,14},{7,15},{8,0},{9,1},... | collective-permute-start | bytes 221192 | tf_op jit(solution)/shard_map/ppermute | solution.py:26
  8.9 0.7 fusion.51
  9.8 0.8 fusion.48
  11.1 0.6 collective-permute-done
  12.2 1.3 collective-permute-start.1
  13.5 0.8 collective-permute-start.2
  14.3 1.2 collective-permute-start.3
  15.6 0.7 collective-permute-done.1
  16.3 2.7 %collective-permute-done.2 = bf16[2,40,256]{2,1,0:T(8,128)(2,1)S(1)} collective-permute-done((bf16[2,40,256]{2,1,0:T(8,128)(2,1)S(1)}, bf16[2,40,256]{2,1,0:T(8,128)(2,1)S(1)}, u32[]{:S(2)}, u32[]{:S(2)}) %collective-permute-start.2) | collective-permute-done | bytes 40992 | tf_op jit(solution)/shard_map/ppermute | solution.py:26
  19.1 1.8 %collective-permute-start.6 = (bf16[336,256]{1,0:T(8,128)(2,1)S(1)}, bf16[336,256]{1,0:T(8,128)(2,1)S(1)}, u32[]{:S(2)}, u32[]{:S(2)}) collective-permute-start(bf16[336,256]{1,0:T(8,128)(2,1)S(1)} %concatenate.24), channel_id=1, source_target_pairs={{0,64},{1,65},{2,66},{3,67},{4,68},{5,69},{6,70},{7,71},{8,72},{9,... | collective-permute-start | bytes 516104 | tf_op jit(solution)/shard_map/ppermute | solution.py:26
  21.0 3.7 %collective-permute-done.6 = bf16[336,256]{1,0:T(8,128)(2,1)S(1)} collective-permute-done((bf16[336,256]{1,0:T(8,128)(2,1)S(1)}, bf16[336,256]{1,0:T(8,128)(2,1)S(1)}, u32[]{:S(2)}, u32[]{:S(2)}) %collective-permute-start.6) | collective-permute-done | bytes 172064 | tf_op jit(solution)/shard_map/ppermute | solution.py:26
  24.7 3.1 %collective-permute-start.10 = (bf16[2,336,256]{2,1,0:T(8,128)(2,1)S(1)}, bf16[2,336,256]{2,1,0:T(8,128)(2,1)S(1)}, u32[]{:S(2)}, u32[]{:S(2)}) collective-permute-start(bf16[2,336,256]{2,1,0:T(8,128)(2,1)S(1)} %pad_maximum_fusion.1.refs_0_), channel_id=1, source_target_pairs={{0,48},{1,49},{2,50},{3,51},{4,52},{5,53},{6,54},{7,55},{8,56},{9,... | collective-permute-start | bytes 1032200 | tf_op jit(solution)/shard_map/ppermute | solution.py:26
  27.9 3.9 %collective-permute-start.4 = (bf16[336,256]{1,0:T(8,128)(2,1)S(1)}, bf16[336,256]{1,0:T(8,128)(2,1)S(1)}, u32[]{:S(2)}, u32[]{:S(2)}) collective-permute-start(bf16[336,256]{1,0:T(8,128)(2,1)S(1)} %concatenate.24), channel_id=1, source_target_pairs={{0,128},{1,129},{2,130},{3,131},{4,132},{5,133},{6,134},{7,135},{8... | collective-permute-start | bytes 516104 | tf_op jit(solution)/shard_map/ppermute | solution.py:26
  32.0 8.8 %collective-permute-done.4 = bf16[336,256]{1,0:T(8,128)(2,1)S(1)} collective-permute-done((bf16[336,256]{1,0:T(8,128)(2,1)S(1)}, bf16[336,256]{1,0:T(8,128)(2,1)S(1)}, u32[]{:S(2)}, u32[]{:S(2)}) %collective-permute-start.4) | collective-permute-done | bytes 172064 | tf_op jit(solution)/shard_map/ppermute | solution.py:26
  40.9 0.7 collective-permute-start.17
  41.6 2.7 %collective-permute-start.11 = (bf16[2,336,256]{2,1,0:T(8,128)(2,1)S(1)}, bf16[2,336,256]{2,1,0:T(8,128)(2,1)S(1)}, u32[]{:S(2)}, u32[]{:S(2)}) collective-permute-start(bf16[2,336,256]{2,1,0:T(8,128)(2,1)S(1)} %broadcast_select_fusion.1), channel_id=1, source_target_pairs={{0,48},{1,17},{2,50},{3,19},{4,52},{5,21},{6,54},{7,23},{8,56},{9,... | collective-permute-start | bytes 1032200 | tf_op jit(solution)/shard_map/ppermute | solution.py:26
  44.3 0.6 collective-permute-start.15
  44.9 0.5 collective-permute-start.13
  45.4 4.0 %collective-permute-done.17.refs_6_ = bf16[2,336,256]{2,1,0:T(8,128)(2,1)S(1)} collective-permute-done((bf16[2,336,256]{2,1,0:T(8,128)(2,1)S(1)}, bf16[2,336,256]{2,1,0:T(8,128)(2,1)S(1)}, u32[]{:S(2)}, u32[]{:S(2)}) %collective-permute-start.17) | collective-permute-done | bytes 344096 | tf_op jit(solution)/shard_map/ppermute | solution.py:26
  49.4 3.7 %collective-permute-done.11.refs_4_ = bf16[2,336,256]{2,1,0:T(8,128)(2,1)S(1)} collective-permute-done((bf16[2,336,256]{2,1,0:T(8,128)(2,1)S(1)}, bf16[2,336,256]{2,1,0:T(8,128)(2,1)S(1)}, u32[]{:S(2)}, u32[]{:S(2)}) %collective-permute-start.11) | collective-permute-done | bytes 344096 | tf_op jit(solution)/shard_map/ppermute | solution.py:26
  53.1 0.8 broadcast_select_fusion
  53.9 0.6 collective-permute-start.18
  54.6 4.0 %copy.17 = bf16[512,8,2,384]{3,1,2,0:T(8,128)(2,1)S(1)} copy(bf16[512,8,2,384]{3,2,1,0:T(2,128)(2,1)} %bitcast.136) | data formatting | bytes 12582912
  58.6 5.6 %shard_map.64 = (f32[640,768]{1,0:T(8,128)S(1)}, f32[640,256]{1,0:T(8,128)S(1)}, f32[16,256]{1,0:T(8,128)S(1)}, bf16[2,1024,768]{2,1,0:T(8,128)(2,1)S(1)}, bf16[384,4096]{1,0:T(8,128)(2,1)S(1)}) custom-call(s32[2]{0:T(128)S(1)} %pad_add_fusion.1.place, bf16[2,336,256]{2,1,0:T(8,128)(2,1)S(1)} %pad_maximum_fusion.1.refs_0_, ...), custom_call_target="tpu_custom_call" | custom-call | flops 2013265920 | bytes 8388608 | tf_op jit(solution)/shard_map/pallas_call | solution.py:206
  64.2 0.3 collective-permute-start.20
  64.5 0.3 collective-permute-start.19
  65.1 0.3 collective-permute-start.14
  65.4 0.6 collective-permute-done.20.refs_7_
  66.0 0.7 collective-permute-done.19.refs_5_
  66.7 0.3 collective-permute-done.16.refs_3_
  67.0 0.5 collective-permute-done.14.refs_1_
  67.5 6.9 %shard_map.65 = (bf16[640,384]{1,0:T(8,128)(2,1)S(1)}, f32[2,320,256]{2,1,0:T(8,128)S(1)}, f32[2,320,256]{2,1,0:T(8,128)S(1)}, f32[2,320,256]{2,1,0:T(8,128)S(1)...) custom-call(s32[2]{0:T(128)S(1)} %pad_add_fusion.1.place, ...), custom_call_target="tpu_custom_call" | custom-call | flops 4026531840 | bytes 8388608 | tf_op jit(solution)/shard_map/pallas_call | solution.py:206
  74.4 0.3 collective-permute-start.26
  74.7 3.1 %shard_map.66 = (f32[2,320,256]{2,1,0:T(8,128)S(1)}, f32[2,320,256]{2,1,0:T(8,128)S(1)}, f32[2,320,256]{2,1,0:T(8,128)S(1)}, f32[2,320,256]{2,1,0:T(8,128)S(1)}, bf16[4,2,320,256]{3,2,1,0:T(8,128)(2,1)}) custom-call(s32[2]{0:T(128)S(1)} %pad_add_fusion.1.place, bf16[640,384]{1,0:T(8,128)(2,1)S(1)} %get-tuple-element.50.act, ...), custom_call_target="tpu_custom_call" | custom-call | flops 1006632960 | bytes 8388608 | tf_op jit(solution)/shard_map/pallas_call | solution.py:206
  77.8 0.3 collective-permute-start.21
  78.1 0.9 fusion.11
  79.3 2.6 %collective-permute-start.27 = (bf16[2,320,256]{2,1,0:T(8,128)(2,1)}, bf16[2,320,256]{2,1,0:T(8,128)(2,1)}, u32[]{:S(2)}, u32[]{:S(2)}) collective-permute-start(bf16[2,320,256]{2,1,0:T(8,128)(2,1)} %fusion.11), channel_id=1, source_target_pairs={{0,48},{1,17},{2,50},{3,19},{4,52},{5,21},{6,54},{7,23},{8,56},{9,... | collective-permute-start | bytes 983048 | tf_op jit(solution)/shard_map/ppermute | solution.py:26
  82.0 1.2 fusion.15
  83.1 2.0 %collective-permute-start.22 = (bf16[2,320,256]{2,1,0:T(8,128)(2,1)S(1)}, bf16[2,320,256]{2,1,0:T(8,128)(2,1)S(1)}, u32[]{:S(2)}, u32[]{:S(2)}) collective-permute-start(bf16[2,320,256]{2,1,0:T(8,128)(2,1)S(1)} %fusion.15), channel_id=1, source_target_pairs={{0,48},{1,17},{2,50},{3,19},{4,52},{5,21},{6,54},{7,23},{8,56},{9,... | collective-permute-start | bytes 983048 | tf_op jit(solution)/shard_map/ppermute | solution.py:26
  85.1 2.8 %collective-permute-done.27 = bf16[2,320,256]{2,1,0:T(8,128)(2,1)} collective-permute-done((bf16[2,320,256]{2,1,0:T(8,128)(2,1)}, bf16[2,320,256]{2,1,0:T(8,128)(2,1)}, u32[]{:S(2)}, u32[]{:S(2)}) %collective-permute-start.27) | collective-permute-done | bytes 327712 | tf_op jit(solution)/shard_map/ppermute | solution.py:26
  87.9 1.4 %fusion.8 = (bf16[2,320,256]{2,1,0:T(8,128)(2,1)S(1)}, bf16[2,320,256]{2,1,0:T(8,128)(2,1)S(1)}) fusion(bf16[2,320,256]{2,1,0:T(8,128)(2,1)} %collective-permute-done.27, f32[2,320,256]{2,1,0:T(8,128)S(1)} %copy-done.3, bf16[4,2,320,256]{3,2,1,0:T(8,128)(2,1)} %copy-done.8, pred[]{:T(512)S(6)} %eq.111, f32[2,320,256]{2,1,0:T(8,128)S(1)} %copy-done.5), kind=kLoop, calls=%fused_computation.17 | loop fusion | flops 1802240 | bytes 2949121 | tf_op jit(solution)/shard_map/convert_element_type | solution.py:340
  89.5 2.7 %collective-permute-start.29 = (bf16[2,320,256]{2,1,0:T(8,128)(2,1)S(1)}, bf16[2,320,256]{2,1,0:T(8,128)(2,1)S(1)}, u32[]{:S(2)}, u32[]{:S(2)}) collective-permute-start(bf16[2,320,256]{2,1,0:T(8,128)(2,1)S(1)} %get-tuple-element.62), channel_id=1, source_target_pairs={{0,48},{1,49},{2,50},{3,51},{4,52},{5,53},{6,54},{7,55},{8,56},{9,... | collective-permute-start | bytes 983048 | tf_op jit(solution)/shard_map/ppermute | solution.py:26
  92.2 1.3 fusion.4
  93.5 1.4 %collective-permute-start.23 = (bf16[2,320,256]{2,1,0:T(8,128)(2,1)S(1)}, bf16[2,320,256]{2,1,0:T(8,128)(2,1)S(1)}, u32[]{:S(2)}, u32[]{:S(2)}) collective-permute-start(bf16[2,320,256]{2,1,0:T(8,128)(2,1)S(1)} %get-tuple-element.63), channel_id=1, source_target_pairs={{0,16},{1,17},{2,18},{3,19},{4,20},{5,21},{6,22},{7,23},{8,24},{9,... | collective-permute-start | bytes 983048 | tf_op jit(solution)/shard_map/ppermute | solution.py:26
  94.9 0.6 collective-permute-start.24
  95.5 4.5 %collective-permute-done.28 = bf16[2,320,256]{2,1,0:T(8,128)(2,1)S(1)} collective-permute-done((bf16[2,320,256]{2,1,0:T(8,128)(2,1)S(1)}, bf16[2,320,256]{2,1,0:T(8,128)(2,1)S(1)}, u32[]{:S(2)}, u32[]{:S(2)}) %collective-permute-start.28) | collective-permute-done | bytes 327712 | tf_op jit(solution)/shard_map/ppermute | solution.py:26
  100.1 1.3 collective-permute-done.29
  101.4 1.2 fusion.14
  102.6 6.0 %collective-permute-start.30 = (bf16[320,256]{1,0:T(8,128)(2,1)S(1)}, bf16[320,256]{1,0:T(8,128)(2,1)S(1)}, u32[]{:S(2)}, u32[]{:S(2)}) collective-permute-start(bf16[320,256]{1,0:T(8,128)(2,1)S(1)} %get-tuple-element.65), channel_id=1, source_target_pairs={{0,128},{1,129},{2,130},{3,131},{4,132},{5,133},{6,134},{7,135},{8... | collective-permute-start | bytes 491528 | tf_op jit(solution)/shard_map/ppermute | solution.py:26
  108.6 1.2 collective-permute-start.31
  109.8 1.1 fusion.17
  111.0 0.5 collective-permute-start.25
  111.5 2.8 %collective-permute-done.30 = bf16[320,256]{1,0:T(8,128)(2,1)S(1)} collective-permute-done((bf16[320,256]{1,0:T(8,128)(2,1)S(1)}, bf16[320,256]{1,0:T(8,128)(2,1)S(1)}, u32[]{:S(2)}, u32[]{:S(2)}) %collective-permute-start.30) | collective-permute-done | bytes 163872 | tf_op jit(solution)/shard_map/ppermute | solution.py:26
  114.4 2.3 %collective-permute-done.31 = bf16[320,256]{1,0:T(8,128)(2,1)S(1)} collective-permute-done((bf16[320,256]{1,0:T(8,128)(2,1)S(1)}, bf16[320,256]{1,0:T(8,128)(2,1)S(1)}, u32[]{:S(2)}, u32[]{:S(2)}) %collective-permute-start.31) | collective-permute-done | bytes 163872 | tf_op jit(solution)/shard_map/ppermute | solution.py:26
  116.7 1.3 collective-permute-done.25
  118.1 0.5 collective-permute-start.32
  118.6 4.4 %collective-permute-start.33 = (bf16[2,40,256]{2,1,0:T(8,128)(2,1)S(1)}, bf16[2,40,256]{2,1,0:T(8,128)(2,1)S(1)}, u32[]{:S(2)}, u32[]{:S(2)}) collective-permute-start(bf16[2,40,256]{2,1,0:T(8,128)(2,1)S(1)} %bitcast.151), channel_id=1, source_target_pairs={{0,4},{1,5},{2,6},{3,7},{4,0},{5,1},{6,2},{7,3},{8,12},{9,13},{10,... | collective-permute-start | bytes 122888 | tf_op jit(solution)/shard_map/ppermute | solution.py:26
  123.0 2.0 %collective-permute-done.33 = bf16[2,40,256]{2,1,0:T(8,128)(2,1)S(1)} collective-permute-done((bf16[2,40,256]{2,1,0:T(8,128)(2,1)S(1)}, bf16[2,40,256]{2,1,0:T(8,128)(2,1)S(1)}, u32[]{:S(2)}, u32[]{:S(2)}) %collective-permute-start.33) | collective-permute-done | bytes 40992 | tf_op jit(solution)/shard_map/ppermute | solution.py:26
  125.0 2.0 %collective-permute-done.34 = bf16[2,40,256]{2,1,0:T(8,128)(2,1)S(1)} collective-permute-done((bf16[2,40,256]{2,1,0:T(8,128)(2,1)S(1)}, bf16[2,40,256]{2,1,0:T(8,128)(2,1)S(1)}, u32[]{:S(2)}, u32[]{:S(2)}) %collective-permute-start.34) | collective-permute-done | bytes 40992 | tf_op jit(solution)/shard_map/ppermute | solution.py:26
  127.0 4.3 %collective-permute-start.35 = (bf16[4,40,256]{2,1,0:T(8,128)(2,1)S(1)}, bf16[4,40,256]{2,1,0:T(8,128)(2,1)S(1)}, u32[]{:S(2)}, u32[]{:S(2)}) collective-permute-start(bf16[4,40,256]{2,1,0:T(8,128)(2,1)S(1)} %get-tuple-element.68), channel_id=1, source_target_pairs={{0,8},{1,9},{2,10},{3,11},{4,12},{5,13},{6,14},{7,15},{8,0},{9,1},... | collective-permute-start | bytes 245768 | tf_op jit(solution)/shard_map/ppermute | solution.py:26
  131.4 4.1 %collective-permute-done.35 = bf16[4,40,256]{2,1,0:T(8,128)(2,1)S(1)} collective-permute-done((bf16[4,40,256]{2,1,0:T(8,128)(2,1)S(1)}, bf16[4,40,256]{2,1,0:T(8,128)(2,1)S(1)}, u32[]{:S(2)}, u32[]{:S(2)}) %collective-permute-start.35) | collective-permute-done | bytes 81952 | tf_op jit(solution)/shard_map/ppermute | solution.py:26
  135.7 0.9 fusion.2
  (94 shorter events, 3.1 us)
Async XLA Ops:
  0.0 10.9 %copy-start = (bf16[256,8]{0,1:T(8,128)(2,1)S(1)}, bf16[256,8]{0,1:T(8,128)(2,1)}, u32[]{:S(2)}) copy-start(bf16[256,8]{0,1:T(8,128)(2,1)} %param.10) | copy-start | bytes 12292
  1.7 10.0 %collective-permute-start = (bf16[144,256]{1,0:T(8,128)(2,1)S(1)}, bf16[144,256]{1,0:T(8,128)(2,1)S(1)}, u32[]{:S(2)}, u32[]{:S(2)}) collective-permute-start(bf16[144,256]{1,0:T(8,128)(2,1)S(1)} %fusion.38), channel_id=1, source_target_pairs={{0,8},{1,9},{2,10},{3,11},{4,12},{5,13},{6,14},{7,15},{8,0},{9,1},... | collective-permute-start | bytes 221192 | tf_op jit(solution)/shard_map/ppermute | solution.py:26
  12.2 4.1 %collective-permute-start.1 = (bf16[2,40,256]{2,1,0:T(8,128)(2,1)S(1)}, bf16[2,40,256]{2,1,0:T(8,128)(2,1)S(1)}, u32[]{:S(2)}, u32[]{:S(2)}) collective-permute-start(bf16[2,40,256]{2,1,0:T(8,128)(2,1)S(1)} %get-tuple-element.74), channel_id=1, source_target_pairs={{0,2},{1,3},{2,4},{3,5},{4,6},{5,7},{6,0},{7,1},{8,10},{9,11},{10,... | collective-permute-start | bytes 122888 | tf_op jit(solution)/shard_map/ppermute | solution.py:26
  13.5 5.5 %collective-permute-start.2 = (bf16[2,40,256]{2,1,0:T(8,128)(2,1)S(1)}, bf16[2,40,256]{2,1,0:T(8,128)(2,1)S(1)}, u32[]{:S(2)}, u32[]{:S(2)}) collective-permute-start(bf16[2,40,256]{2,1,0:T(8,128)(2,1)S(1)} %get-tuple-element.76), channel_id=1, source_target_pairs={{0,4},{1,5},{2,6},{3,7},{4,0},{5,1},{6,2},{7,3},{8,12},{9,13},{10,... | collective-permute-start | bytes 122888 | tf_op jit(solution)/shard_map/ppermute | solution.py:26
  14.3 4.7 %collective-permute-start.3 = (bf16[2,40,256]{2,1,0:T(8,128)(2,1)S(1)}, bf16[2,40,256]{2,1,0:T(8,128)(2,1)S(1)}, u32[]{:S(2)}, u32[]{:S(2)}) collective-permute-start(bf16[2,40,256]{2,1,0:T(8,128)(2,1)S(1)} %get-tuple-element.75), channel_id=1, source_target_pairs={{0,6},{1,7},{2,0},{3,1},{4,2},{5,3},{6,4},{7,5},{8,14},{9,15},{10,... | collective-permute-start | bytes 122888 | tf_op jit(solution)/shard_map/ppermute | solution.py:26
  19.1 5.5 %collective-permute-start.6 = (bf16[336,256]{1,0:T(8,128)(2,1)S(1)}, bf16[336,256]{1,0:T(8,128)(2,1)S(1)}, u32[]{:S(2)}, u32[]{:S(2)}) collective-permute-start(bf16[336,256]{1,0:T(8,128)(2,1)S(1)} %concatenate.24), channel_id=1, source_target_pairs={{0,64},{1,65},{2,66},{3,67},{4,68},{5,69},{6,70},{7,71},{8,72},{9,... | collective-permute-start | bytes 516104 | tf_op jit(solution)/shard_map/ppermute | solution.py:26
  24.7 16.9 %collective-permute-start.10 = (bf16[2,336,256]{2,1,0:T(8,128)(2,1)S(1)}, bf16[2,336,256]{2,1,0:T(8,128)(2,1)S(1)}, u32[]{:S(2)}, u32[]{:S(2)}) collective-permute-start(bf16[2,336,256]{2,1,0:T(8,128)(2,1)S(1)} %pad_maximum_fusion.1.refs_0_), channel_id=1, source_target_pairs={{0,48},{1,49},{2,50},{3,51},{4,52},{5,53},{6,54},{7,55},{8,56},{9,... | collective-permute-start | bytes 1032200 | tf_op jit(solution)/shard_map/ppermute | solution.py:26
  27.8 13.8 %collective-permute-start.8 = (bf16[2,336,256]{2,1,0:T(8,128)(2,1)S(1)}, bf16[2,336,256]{2,1,0:T(8,128)(2,1)S(1)}, u32[]{:S(2)}, u32[]{:S(2)}) collective-permute-start(bf16[2,336,256]{2,1,0:T(8,128)(2,1)S(1)} %pad_maximum_fusion.1.refs_0_), channel_id=1, source_target_pairs={{0,16},{1,17},{2,18},{3,19},{4,20},{5,21},{6,22},{7,23},{8,24},{9,... | collective-permute-start | bytes 1032200 | tf_op jit(solution)/shard_map/ppermute | solution.py:26
  27.9 12.9 %collective-permute-start.4 = (bf16[336,256]{1,0:T(8,128)(2,1)S(1)}, bf16[336,256]{1,0:T(8,128)(2,1)S(1)}, u32[]{:S(2)}, u32[]{:S(2)}) collective-permute-start(bf16[336,256]{1,0:T(8,128)(2,1)S(1)} %concatenate.24), channel_id=1, source_target_pairs={{0,128},{1,129},{2,130},{3,131},{4,132},{5,133},{6,134},{7,135},{8... | collective-permute-start | bytes 516104 | tf_op jit(solution)/shard_map/ppermute | solution.py:26
  31.8 9.0 %collective-permute-start.5 = (bf16[336,256]{1,0:T(8,128)(2,1)S(1)}, bf16[336,256]{1,0:T(8,128)(2,1)S(1)}, u32[]{:S(2)}, u32[]{:S(2)}) collective-permute-start(bf16[336,256]{1,0:T(8,128)(2,1)S(1)} %concatenate.24), channel_id=1, source_target_pairs={{0,192},{1,193},{2,194},{3,195},{4,196},{5,197},{6,198},{7,199},{8... | collective-permute-start | bytes 516104 | tf_op jit(solution)/shard_map/ppermute | solution.py:26
  40.9 12.3 %copy-start.6 = (bf16[2,336,256]{2,1,0:T(8,128)(2,1)}, bf16[2,336,256]{2,1,0:T(8,128)(2,1)S(1)}, u32[]{:S(2)}) copy-start(bf16[2,336,256]{2,1,0:T(8,128)(2,1)S(1)} %pad_maximum_fusion.refs_0_) | copy-start | bytes 1032196
  40.9 8.5 %collective-permute-start.17 = (bf16[2,336,256]{2,1,0:T(8,128)(2,1)S(1)}, bf16[2,336,256]{2,1,0:T(8,128)(2,1)S(1)}, u32[]{:S(2)}, u32[]{:S(2)}) collective-permute-start(bf16[2,336,256]{2,1,0:T(8,128)(2,1)S(1)} %pad_maximum_fusion.refs_0_), channel_id=1, source_target_pairs={{0,48},{1,49},{2,50},{3,51},{4,52},{5,53},{6,54},{7,55},{8,56},{9,... | collective-permute-start | bytes 1032200 | tf_op jit(solution)/shard_map/ppermute | solution.py:26
  41.6 11.5 %collective-permute-start.11 = (bf16[2,336,256]{2,1,0:T(8,128)(2,1)S(1)}, bf16[2,336,256]{2,1,0:T(8,128)(2,1)S(1)}, u32[]{:S(2)}, u32[]{:S(2)}) collective-permute-start(bf16[2,336,256]{2,1,0:T(8,128)(2,1)S(1)} %broadcast_select_fusion.1), channel_id=1, source_target_pairs={{0,48},{1,17},{2,50},{3,19},{4,52},{5,21},{6,54},{7,23},{8,56},{9,... | collective-permute-start | bytes 1032200 | tf_op jit(solution)/shard_map/ppermute | solution.py:26
  44.3 8.8 %collective-permute-start.15 = (bf16[2,336,256]{2,1,0:T(8,128)(2,1)S(1)}, bf16[2,336,256]{2,1,0:T(8,128)(2,1)S(1)}, u32[]{:S(2)}, u32[]{:S(2)}) collective-permute-start(bf16[2,336,256]{2,1,0:T(8,128)(2,1)S(1)} %pad_maximum_fusion.refs_0_), channel_id=1, source_target_pairs={{0,16},{1,17},{2,18},{3,19},{4,20},{5,21},{6,22},{7,23},{8,24},{9,... | collective-permute-start | bytes 1032200 | tf_op jit(solution)/shard_map/ppermute | solution.py:26
  44.9 13.7 %collective-permute-start.7 = (bf16[2,336,256]{2,1,0:T(8,128)(2,1)S(1)}, bf16[2,336,256]{2,1,0:T(8,128)(2,1)S(1)}, u32[]{:S(2)}, u32[]{:S(2)}) collective-permute-start(bf16[2,336,256]{2,1,0:T(8,128)(2,1)S(1)} %pad_maximum_fusion.1.refs_0_), channel_id=1, source_target_pairs={{0,1},{1,0},{2,3},{3,2},{4,5},{5,4},{6,7},{7,6},{8,9},{9,8},{10,11... | collective-permute-start | bytes 1032200 | tf_op jit(solution)/shard_map/ppermute | solution.py:26
  44.9 13.7 %collective-permute-start.13 = (bf16[2,336,256]{2,1,0:T(8,128)(2,1)S(1)}, bf16[2,336,256]{2,1,0:T(8,128)(2,1)S(1)}, u32[]{:S(2)}, u32[]{:S(2)}) collective-permute-start(bf16[2,336,256]{2,1,0:T(8,128)(2,1)S(1)} %collective-permute-done.10.refs_6_), channel_id=1, source_target_pairs={{0,1},{1,0},{2,3},{3,2},{4,5},{5,4},{6,7},{7,6},{8,9},{9,8},{10,11... | collective-permute-start | bytes 1032200 | tf_op jit(solution)/shard_map/ppermute | solution.py:26
  49.4 9.2 %collective-permute-start.9 = (bf16[2,336,256]{2,1,0:T(8,128)(2,1)S(1)}, bf16[2,336,256]{2,1,0:T(8,128)(2,1)S(1)}, u32[]{:S(2)}, u32[]{:S(2)}) collective-permute-start(bf16[2,336,256]{2,1,0:T(8,128)(2,1)S(1)} %collective-permute-done.8.refs_2_), channel_id=1, source_target_pairs={{0,1},{1,0},{2,3},{3,2},{4,5},{5,4},{6,7},{7,6},{8,9},{9,8},{10,11... | collective-permute-start | bytes 1032200 | tf_op jit(solution)/shard_map/ppermute | solution.py:26
  53.1 5.5 %collective-permute-start.12 = (bf16[2,336,256]{2,1,0:T(8,128)(2,1)S(1)}, bf16[2,336,256]{2,1,0:T(8,128)(2,1)S(1)}, u32[]{:S(2)}, u32[]{:S(2)}) collective-permute-start(bf16[2,336,256]{2,1,0:T(8,128)(2,1)S(1)} %collective-permute-done.11.refs_4_), channel_id=1, source_target_pairs={{0,1},{1,0},{2,3},{3,2},{4,5},{5,4},{6,7},{7,6},{8,9},{9,8},{10,11... | collective-permute-start | bytes 1032200 | tf_op jit(solution)/shard_map/ppermute | solution.py:26
  53.9 10.6 %collective-permute-start.18 = (bf16[2,336,256]{2,1,0:T(8,128)(2,1)}, bf16[2,336,256]{2,1,0:T(8,128)(2,1)}, u32[]{:S(2)}, u32[]{:S(2)}) collective-permute-start(bf16[2,336,256]{2,1,0:T(8,128)(2,1)} %broadcast_select_fusion), channel_id=1, source_target_pairs={{0,48},{1,17},{2,50},{3,19},{4,52},{5,21},{6,54},{7,23},{8,56},{9,... | collective-permute-start | bytes 1032200 | tf_op jit(solution)/shard_map/ppermute | solution.py:26
  54.6 4.1 %copy-start.1 = (bf16[1,384,4096]{2,1,0:T(8,128)(2,1)S(1)}, bf16[1,384,4096]{2,1,0:T(8,128)(2,1)}, u32[]{:S(2)}) copy-start(bf16[1,384,4096]{2,1,0:T(8,128)(2,1)} %param.12) | copy-start | bytes 9437188
  58.6 6.4 %copy-start.7 = (bf16[2,336,256]{2,1,0:T(8,128)(2,1)S(1)}, bf16[2,336,256]{2,1,0:T(8,128)(2,1)}, u32[]{:S(2)}) copy-start(bf16[2,336,256]{2,1,0:T(8,128)(2,1)} %copy-done.6) | copy-start | bytes 1032196
  64.2 1.7 %collective-permute-start.20 = (bf16[2,336,256]{2,1,0:T(8,128)(2,1)S(1)}, bf16[2,336,256]{2,1,0:T(8,128)(2,1)S(1)}, u32[]{:S(2)}, u32[]{:S(2)}) collective-permute-start(bf16[2,336,256]{2,1,0:T(8,128)(2,1)S(1)} %collective-permute-done.17.refs_6_), channel_id=1, source_target_pairs={{0,1},{1,0},{2,3},{3,2},{4,5},{5,4},{6,7},{7,6},{8,9},{9,8},{10,11... | collective-permute-start | bytes 1032200 | tf_op jit(solution)/shard_map/ppermute | solution.py:26
  64.5 2.1 %collective-permute-start.19 = (bf16[2,336,256]{2,1,0:T(8,128)(2,1)}, bf16[2,336,256]{2,1,0:T(8,128)(2,1)S(1)}, u32[]{:S(2)}, u32[]{:S(2)}) collective-permute-start(bf16[2,336,256]{2,1,0:T(8,128)(2,1)} %collective-permute-done.18.refs_4_), channel_id=1, source_target_pairs={{0,1},{1,0},{2,3},{3,2},{4,5},{5,4},{6,7},{7,6},{8,9},{9,8},{10,11... | collective-permute-start | bytes 1032200 | tf_op jit(solution)/shard_map/ppermute | solution.py:26
  64.8 2.1 %collective-permute-start.16 = (bf16[2,336,256]{2,1,0:T(8,128)(2,1)S(1)}, bf16[2,336,256]{2,1,0:T(8,128)(2,1)S(1)}, u32[]{:S(2)}, u32[]{:S(2)}) collective-permute-start(bf16[2,336,256]{2,1,0:T(8,128)(2,1)S(1)} %collective-permute-done.15.refs_2_), channel_id=1, source_target_pairs={{0,1},{1,0},{2,3},{3,2},{4,5},{5,4},{6,7},{7,6},{8,9},{9,8},{10,11... | collective-permute-start | bytes 1032200 | tf_op jit(solution)/shard_map/ppermute | solution.py:26
  65.1 2.4 %collective-permute-start.14 = (bf16[2,336,256]{2,1,0:T(8,128)(2,1)S(1)}, bf16[2,336,256]{2,1,0:T(8,128)(2,1)S(1)}, u32[]{:S(2)}, u32[]{:S(2)}) collective-permute-start(bf16[2,336,256]{2,1,0:T(8,128)(2,1)S(1)} %copy-done.7), channel_id=1, source_target_pairs={{0,1},{1,0},{2,3},{3,2},{4,5},{5,4},{6,7},{7,6},{8,9},{9,8},{10,11... | collective-permute-start | bytes 1032200 | tf_op jit(solution)/shard_map/ppermute | solution.py:26
  74.4 3.5 %copy-start.2 = (f32[2,320,256]{2,1,0:T(8,128)}, f32[2,320,256]{2,1,0:T(8,128)S(1)}, u32[]{:S(2)}) copy-start(f32[2,320,256]{2,1,0:T(8,128)S(1)} %get-tuple-element.58) | copy-start | bytes 1966084
  74.4 3.4 %copy-start.4 = (f32[2,320,256]{2,1,0:T(8,128)}, f32[2,320,256]{2,1,0:T(8,128)S(1)}, u32[]{:S(2)}) copy-start(f32[2,320,256]{2,1,0:T(8,128)S(1)} %get-tuple-element.60) | copy-start | bytes 1966084
  74.4 3.7 %collective-permute-start.26 = (bf16[4,2,320,256]{3,2,1,0:T(8,128)(2,1)S(1)}, bf16[4,2,320,256]{3,2,1,0:T(8,128)(2,1)S(1)}, u32[]{:S(2)}, u32[]{:S(2)}) collective-permute-start(bf16[4,2,320,256]{3,2,1,0:T(8,128)(2,1)S(1)} %get-tuple-element.57), channel_id=1, source_target_pairs={{0,1},{1,0},{2,3},{3,2},{4,5},{5,4},{6,7},{7,6},{8,9},{9,8},{10,11... | collective-permute-start | bytes 3932168 | tf_op jit(solution)/shard_map/ppermute | solution.py:26
  77.8 4.2 %collective-permute-start.21 = (bf16[4,2,320,256]{3,2,1,0:T(8,128)(2,1)}, bf16[4,2,320,256]{3,2,1,0:T(8,128)(2,1)}, u32[]{:S(2)}, u32[]{:S(2)}) collective-permute-start(bf16[4,2,320,256]{3,2,1,0:T(8,128)(2,1)} %get-tuple-element.52), channel_id=1, source_target_pairs={{0,1},{1,0},{2,3},{3,2},{4,5},{5,4},{6,7},{7,6},{8,9},{9,8},{10,11... | collective-permute-start | bytes 3932168 | tf_op jit(solution)/shard_map/ppermute | solution.py:26
  78.1 1.2 copy-start.8
  79.3 8.6 %collective-permute-start.27 = (bf16[2,320,256]{2,1,0:T(8,128)(2,1)}, bf16[2,320,256]{2,1,0:T(8,128)(2,1)}, u32[]{:S(2)}, u32[]{:S(2)}) collective-permute-start(bf16[2,320,256]{2,1,0:T(8,128)(2,1)} %fusion.11), channel_id=1, source_target_pairs={{0,48},{1,17},{2,50},{3,19},{4,52},{5,21},{6,54},{7,23},{8,56},{9,... | collective-permute-start | bytes 983048 | tf_op jit(solution)/shard_map/ppermute | solution.py:26
  82.0 5.9 %copy-start.3 = (f32[2,320,256]{2,1,0:T(8,128)S(1)}, f32[2,320,256]{2,1,0:T(8,128)}, u32[]{:S(2)}) copy-start(f32[2,320,256]{2,1,0:T(8,128)} %copy-done.2) | copy-start | bytes 1966084
  82.0 5.9 %copy-start.5 = (f32[2,320,256]{2,1,0:T(8,128)S(1)}, f32[2,320,256]{2,1,0:T(8,128)}, u32[]{:S(2)}) copy-start(f32[2,320,256]{2,1,0:T(8,128)} %copy-done.4) | copy-start | bytes 1966084
  83.1 9.0 %collective-permute-start.22 = (bf16[2,320,256]{2,1,0:T(8,128)(2,1)S(1)}, bf16[2,320,256]{2,1,0:T(8,128)(2,1)S(1)}, u32[]{:S(2)}, u32[]{:S(2)}) collective-permute-start(bf16[2,320,256]{2,1,0:T(8,128)(2,1)S(1)} %fusion.15), channel_id=1, source_target_pairs={{0,48},{1,17},{2,50},{3,19},{4,52},{5,21},{6,54},{7,23},{8,56},{9,... | collective-permute-start | bytes 983048 | tf_op jit(solution)/shard_map/ppermute | solution.py:26
  89.3 10.7 %collective-permute-start.28 = (bf16[2,320,256]{2,1,0:T(8,128)(2,1)S(1)}, bf16[2,320,256]{2,1,0:T(8,128)(2,1)S(1)}, u32[]{:S(2)}, u32[]{:S(2)}) collective-permute-start(bf16[2,320,256]{2,1,0:T(8,128)(2,1)S(1)} %get-tuple-element.61), channel_id=1, source_target_pairs={{0,16},{1,17},{2,18},{3,19},{4,20},{5,21},{6,22},{7,23},{8,24},{9,... | collective-permute-start | bytes 983048 | tf_op jit(solution)/shard_map/ppermute | solution.py:26
  89.5 11.9 %collective-permute-start.29 = (bf16[2,320,256]{2,1,0:T(8,128)(2,1)S(1)}, bf16[2,320,256]{2,1,0:T(8,128)(2,1)S(1)}, u32[]{:S(2)}, u32[]{:S(2)}) collective-permute-start(bf16[2,320,256]{2,1,0:T(8,128)(2,1)S(1)} %get-tuple-element.62), channel_id=1, source_target_pairs={{0,48},{1,49},{2,50},{3,51},{4,52},{5,53},{6,54},{7,55},{8,56},{9,... | collective-permute-start | bytes 983048 | tf_op jit(solution)/shard_map/ppermute | solution.py:26
  93.5 16.3 %collective-permute-start.23 = (bf16[2,320,256]{2,1,0:T(8,128)(2,1)S(1)}, bf16[2,320,256]{2,1,0:T(8,128)(2,1)S(1)}, u32[]{:S(2)}, u32[]{:S(2)}) collective-permute-start(bf16[2,320,256]{2,1,0:T(8,128)(2,1)S(1)} %get-tuple-element.63), channel_id=1, source_target_pairs={{0,16},{1,17},{2,18},{3,19},{4,20},{5,21},{6,22},{7,23},{8,24},{9,... | collective-permute-start | bytes 983048 | tf_op jit(solution)/shard_map/ppermute | solution.py:26
  94.9 14.9 %collective-permute-start.24 = (bf16[2,320,256]{2,1,0:T(8,128)(2,1)S(1)}, bf16[2,320,256]{2,1,0:T(8,128)(2,1)S(1)}, u32[]{:S(2)}, u32[]{:S(2)}) collective-permute-start(bf16[2,320,256]{2,1,0:T(8,128)(2,1)S(1)} %get-tuple-element.64), channel_id=1, source_target_pairs={{0,48},{1,49},{2,50},{3,51},{4,52},{5,53},{6,54},{7,55},{8,56},{9,... | collective-permute-start | bytes 983048 | tf_op jit(solution)/shard_map/ppermute | solution.py:26
  102.6 11.8 %collective-permute-start.30 = (bf16[320,256]{1,0:T(8,128)(2,1)S(1)}, bf16[320,256]{1,0:T(8,128)(2,1)S(1)}, u32[]{:S(2)}, u32[]{:S(2)}) collective-permute-start(bf16[320,256]{1,0:T(8,128)(2,1)S(1)} %get-tuple-element.65), channel_id=1, source_target_pairs={{0,128},{1,129},{2,130},{3,131},{4,132},{5,133},{6,134},{7,135},{8... | collective-permute-start | bytes 491528 | tf_op jit(solution)/shard_map/ppermute | solution.py:26
  108.6 8.1 %collective-permute-start.31 = (bf16[320,256]{1,0:T(8,128)(2,1)S(1)}, bf16[320,256]{1,0:T(8,128)(2,1)S(1)}, u32[]{:S(2)}, u32[]{:S(2)}) collective-permute-start(bf16[320,256]{1,0:T(8,128)(2,1)S(1)} %get-tuple-element.66), channel_id=1, source_target_pairs={{0,192},{1,193},{2,194},{3,195},{4,196},{5,197},{6,198},{7,199},{8... | collective-permute-start | bytes 491528 | tf_op jit(solution)/shard_map/ppermute | solution.py:26
  109.8 1.7 %copy-start.10 = (s32[128,2]{0,1:T(2,128)S(1)}, s32[128,2]{0,1:T(2,128)}, u32[]{:S(2)}) copy-start(s32[128,2]{0,1:T(2,128)} %param.13) | copy-start | bytes 3076
  111.0 24.7 %copy-start.9 = (bf16[128,256]{1,0:T(8,128)(2,1)S(1)}, bf16[128,256]{1,0:T(8,128)(2,1)}, u32[]{:S(2)}) copy-start(bf16[128,256]{1,0:T(8,128)(2,1)} %param.8) | copy-start | bytes 196612
  111.0 7.0 %collective-permute-start.25 = (bf16[320,256]{1,0:T(8,128)(2,1)S(1)}, bf16[320,256]{1,0:T(8,128)(2,1)S(1)}, u32[]{:S(2)}, u32[]{:S(2)}) collective-permute-start(bf16[320,256]{1,0:T(8,128)(2,1)S(1)} %fusion.23), channel_id=1, source_target_pairs={{0,64},{1,65},{2,66},{3,67},{4,68},{5,69},{6,70},{7,71},{8,72},{9,... | collective-permute-start | bytes 491528 | tf_op jit(solution)/shard_map/ppermute | solution.py:26
  118.1 4.9 %collective-permute-start.32 = (bf16[2,40,256]{2,1,0:T(8,128)(2,1)S(1)}, bf16[2,40,256]{2,1,0:T(8,128)(2,1)S(1)}, u32[]{:S(2)}, u32[]{:S(2)}) collective-permute-start(bf16[2,40,256]{2,1,0:T(8,128)(2,1)S(1)} %bitcast.153), channel_id=1, source_target_pairs={{0,6},{1,7},{2,0},{3,1},{4,2},{5,3},{6,4},{7,5},{8,14},{9,15},{10,... | collective-permute-start | bytes 122888 | tf_op jit(solution)/shard_map/ppermute | solution.py:26
  118.6 6.4 %collective-permute-start.33 = (bf16[2,40,256]{2,1,0:T(8,128)(2,1)S(1)}, bf16[2,40,256]{2,1,0:T(8,128)(2,1)S(1)}, u32[]{:S(2)}, u32[]{:S(2)}) collective-permute-start(bf16[2,40,256]{2,1,0:T(8,128)(2,1)S(1)} %bitcast.151), channel_id=1, source_target_pairs={{0,4},{1,5},{2,6},{3,7},{4,0},{5,1},{6,2},{7,3},{8,12},{9,13},{10,... | collective-permute-start | bytes 122888 | tf_op jit(solution)/shard_map/ppermute | solution.py:26
  123.0 4.0 %collective-permute-start.34 = (bf16[2,40,256]{2,1,0:T(8,128)(2,1)S(1)}, bf16[2,40,256]{2,1,0:T(8,128)(2,1)S(1)}, u32[]{:S(2)}, u32[]{:S(2)}) collective-permute-start(bf16[2,40,256]{2,1,0:T(8,128)(2,1)S(1)} %bitcast.149), channel_id=1, source_target_pairs={{0,2},{1,3},{2,4},{3,5},{4,6},{5,7},{6,0},{7,1},{8,10},{9,11},{10,... | collective-permute-start | bytes 122888 | tf_op jit(solution)/shard_map/ppermute | solution.py:26
  127.0 8.4 %collective-permute-start.35 = (bf16[4,40,256]{2,1,0:T(8,128)(2,1)S(1)}, bf16[4,40,256]{2,1,0:T(8,128)(2,1)S(1)}, u32[]{:S(2)}, u32[]{:S(2)}) collective-permute-start(bf16[4,40,256]{2,1,0:T(8,128)(2,1)S(1)} %get-tuple-element.68), channel_id=1, source_target_pairs={{0,8},{1,9},{2,10},{3,11},{4,12},{5,13},{6,14},{7,15},{8,0},{9,1},... | collective-permute-start | bytes 245768 | tf_op jit(solution)/shard_map/ppermute | solution.py:26

commit v4 on v3

--- a/solution.py
+++ b/solution.py
@@ -100,19 +100,13 @@
     lax.fori_loop(0, count // step, body, 0)
 
 
-def project(blocks, total, slab, copies):
-    count = total.shape[0] // 2
-    for n in range(len(GROUPS[0])):
-        for copy in copies[n * NY : n * NY + NY] if copies else ():
-            copy.wait()
-        left = jnp.concatenate(
-            [
-                jnp.concatenate([blocks[2 * j + side][n, :count] for j in range(NY)], axis=1)
-                for side in range(2)
-            ],
-            axis=0,
-        )
-        total[...] += jnp.dot(left, slab[n], preferred_element_type=F32)
+def part_of(blocks, n, slab):
+    count = blocks[0].shape[1] - 16
+    sides = [
+        jnp.concatenate([blocks[2 * j + side][n, :count] for j in range(NY)], axis=1)
+        for side in range(2)
+    ]
+    return jnp.dot(jnp.concatenate(sides, axis=0), slab[n], preferred_element_type=F32)
 
 
 def arrange(place, blocks, rows, inverse, extras):
@@ -183,11 +177,11 @@
     (total_in, squares_in, extras_in, slab, w_down, act), refs = refs[:6], refs[6:]
     own, (give, extras, total, squares) = refs[:NY], refs[NY:]
     units, model = w_down.shape
-    total[...] = total_in[...]
     squares[...] = squares_in[...]
     extras[...] = extras_in[...]
     square(blocks, squares, extras)
-    project(blocks, total, slab, None)
+    total[...] = total_in[...] + part_of(blocks, 0, slab)
+    total[...] += part_of(blocks, 1, slab)
     mean = jnp.sum(squares[...], axis=1, keepdims=True) / model
     scale = lax.rsqrt(mean + 1e-05)
     act[...] = (jax.nn.silu(total[:, :units] * scale) * (total[:, units:] * scale)).astype(BF16)

time: 137 us -> 137 us (level)
  no operation moved by 1% of the time
where the time goes in v4:
time: 137 us; the launch traced here: 136 us
  starting transfers between devices  52.9 us (39%)
  waiting for transfers between devices  49.5 us (36%)
  Pallas kernels  15.5 us (11%)
  other arithmetic  11.8 us (9%)
  local copies, waits for them, and re-layouts  4.65 us (3%)
  matrix products  1.81 us (1%)
    ppermute x36, starting transfers between devices, move(): return lax.ppermute(value, ('section', 'dp'), pairs)  52.9 us
    ppermute x36, waiting for transfers between devices, move(): return lax.ppermute(value, ('section', 'dp'), pairs)  49.5 us
    pallas_call x3, Pallas kernels, call(): pl.pallas_call(kernel, out_shape=out_shape, in_specs=specs, out_specs=(vm...  15.5 us
    unnamed x23, local copies, waits for them, and re-layouts  4.34 us
    convert_element_type x2, other arithmetic, local(): one = xor_y((parts[1] + jnp.where(core == 0, passed, 0.0)).astype(BF16), 1)  2.78 us
  transfers between devices with their start and end apart: 36, of which 20 were waited for; matrix products, arithmetic and copies ran while one was open for 11% of the time, Pallas kernels for 6%

profile of v4, /device:TPU:4, one launch (start us, length us, event | category | flops | bytes accessed | tf_op | source)
XLA Modules:
  0.0 136.5 jit_solution(5091977907228969137)
XLA Ops:
  0.0 0.7 convert_bitcast_fusion.1
  0.7 0.9 fusion.27
  1.7 7.3 %collective-permute-start = (bf16[144,256]{1,0:T(8,128)(2,1)S(1)}, bf16[144,256]{1,0:T(8,128)(2,1)S(1)}, u32[]{:S(2)}, u32[]{:S(2)}) collective-permute-start(bf16[144,256]{1,0:T(8,128)(2,1)S(1)} %fusion.38), channel_id=1, source_target_pairs={{0,8},{1,9},{2,10},{3,11},{4,12},{5,13},{6,14},{7,15},{8,0},{9,1},... | collective-permute-start | bytes 221192 | tf_op jit(solution)/shard_map/ppermute | solution.py:26
  8.9 0.7 fusion.51
  9.8 0.8 fusion.48
  11.1 0.6 collective-permute-done
  12.2 1.3 collective-permute-start.1
  13.5 0.8 collective-permute-start.2
  14.3 1.2 collective-permute-start.3
  15.6 0.7 collective-permute-done.1
  16.3 2.7 %collective-permute-done.2 = bf16[2,40,256]{2,1,0:T(8,128)(2,1)S(1)} collective-permute-done((bf16[2,40,256]{2,1,0:T(8,128)(2,1)S(1)}, bf16[2,40,256]{2,1,0:T(8,128)(2,1)S(1)}, u32[]{:S(2)}, u32[]{:S(2)}) %collective-permute-start.2) | collective-permute-done | bytes 40992 | tf_op jit(solution)/shard_map/ppermute | solution.py:26
  19.1 1.8 %collective-permute-start.6 = (bf16[336,256]{1,0:T(8,128)(2,1)S(1)}, bf16[336,256]{1,0:T(8,128)(2,1)S(1)}, u32[]{:S(2)}, u32[]{:S(2)}) collective-permute-start(bf16[336,256]{1,0:T(8,128)(2,1)S(1)} %concatenate.24), channel_id=1, source_target_pairs={{0,64},{1,65},{2,66},{3,67},{4,68},{5,69},{6,70},{7,71},{8,72},{9,... | collective-permute-start | bytes 516104 | tf_op jit(solution)/shard_map/ppermute | solution.py:26
  21.0 3.7 %collective-permute-done.6 = bf16[336,256]{1,0:T(8,128)(2,1)S(1)} collective-permute-done((bf16[336,256]{1,0:T(8,128)(2,1)S(1)}, bf16[336,256]{1,0:T(8,128)(2,1)S(1)}, u32[]{:S(2)}, u32[]{:S(2)}) %collective-permute-start.6) | collective-permute-done | bytes 172064 | tf_op jit(solution)/shard_map/ppermute | solution.py:26
  24.7 3.1 %collective-permute-start.10 = (bf16[2,336,256]{2,1,0:T(8,128)(2,1)S(1)}, bf16[2,336,256]{2,1,0:T(8,128)(2,1)S(1)}, u32[]{:S(2)}, u32[]{:S(2)}) collective-permute-start(bf16[2,336,256]{2,1,0:T(8,128)(2,1)S(1)} %pad_maximum_fusion.1.refs_0_), channel_id=1, source_target_pairs={{0,48},{1,49},{2,50},{3,51},{4,52},{5,53},{6,54},{7,55},{8,56},{9,... | collective-permute-start | bytes 1032200 | tf_op jit(solution)/shard_map/ppermute | solution.py:26
  27.9 3.9 %collective-permute-start.4 = (bf16[336,256]{1,0:T(8,128)(2,1)S(1)}, bf16[336,256]{1,0:T(8,128)(2,1)S(1)}, u32[]{:S(2)}, u32[]{:S(2)}) collective-permute-start(bf16[336,256]{1,0:T(8,128)(2,1)S(1)} %concatenate.24), channel_id=1, source_target_pairs={{0,128},{1,129},{2,130},{3,131},{4,132},{5,133},{6,134},{7,135},{8... | collective-permute-start | bytes 516104 | tf_op jit(solution)/shard_map/ppermute | solution.py:26
  32.0 8.8 %collective-permute-done.4 = bf16[336,256]{1,0:T(8,128)(2,1)S(1)} collective-permute-done((bf16[336,256]{1,0:T(8,128)(2,1)S(1)}, bf16[336,256]{1,0:T(8,128)(2,1)S(1)}, u32[]{:S(2)}, u32[]{:S(2)}) %collective-permute-start.4) | collective-permute-done | bytes 172064 | tf_op jit(solution)/shard_map/ppermute | solution.py:26
  40.9 0.7 collective-permute-start.17
  41.6 2.7 %collective-permute-start.11 = (bf16[2,336,256]{2,1,0:T(8,128)(2,1)S(1)}, bf16[2,336,256]{2,1,0:T(8,128)(2,1)S(1)}, u32[]{:S(2)}, u32[]{:S(2)}) collective-permute-start(bf16[2,336,256]{2,1,0:T(8,128)(2,1)S(1)} %broadcast_select_fusion.1), channel_id=1, source_target_pairs={{0,48},{1,17},{2,50},{3,19},{4,52},{5,21},{6,54},{7,23},{8,56},{9,... | collective-permute-start | bytes 1032200 | tf_op jit(solution)/shard_map/ppermute | solution.py:26
  44.3 0.6 collective-permute-start.15
  44.9 0.5 collective-permute-start.13
  45.4 4.0 %collective-permute-done.17.refs_6_ = bf16[2,336,256]{2,1,0:T(8,128)(2,1)S(1)} collective-permute-done((bf16[2,336,256]{2,1,0:T(8,128)(2,1)S(1)}, bf16[2,336,256]{2,1,0:T(8,128)(2,1)S(1)}, u32[]{:S(2)}, u32[]{:S(2)}) %collective-permute-start.17) | collective-permute-done | bytes 344096 | tf_op jit(solution)/shard_map/ppermute | solution.py:26
  49.4 3.7 %collective-permute-done.11.refs_4_ = bf16[2,336,256]{2,1,0:T(8,128)(2,1)S(1)} collective-permute-done((bf16[2,336,256]{2,1,0:T(8,128)(2,1)S(1)}, bf16[2,336,256]{2,1,0:T(8,128)(2,1)S(1)}, u32[]{:S(2)}, u32[]{:S(2)}) %collective-permute-start.11) | collective-permute-done | bytes 344096 | tf_op jit(solution)/shard_map/ppermute | solution.py:26
  53.1 0.8 broadcast_select_fusion
  53.9 0.6 collective-permute-start.18
  54.6 4.0 %copy.17 = bf16[512,8,2,384]{3,1,2,0:T(8,128)(2,1)S(1)} copy(bf16[512,8,2,384]{3,2,1,0:T(2,128)(2,1)} %bitcast.136) | data formatting | bytes 12582912
  58.6 5.6 %shard_map.64 = (f32[640,768]{1,0:T(8,128)S(1)}, f32[640,256]{1,0:T(8,128)S(1)}, f32[16,256]{1,0:T(8,128)S(1)}, bf16[2,1024,768]{2,1,0:T(8,128)(2,1)S(1)}, bf16[384,4096]{1,0:T(8,128)(2,1)S(1)}) custom-call(s32[2]{0:T(128)S(1)} %pad_add_fusion.1.place, bf16[2,336,256]{2,1,0:T(8,128)(2,1)S(1)} %pad_maximum_fusion.1.refs_0_, ...), custom_call_target="tpu_custom_call" | custom-call | flops 2013265920 | bytes 8388608 | tf_op jit(solution)/shard_map/pallas_call | solution.py:200
  64.2 0.3 collective-permute-start.20
  64.5 0.3 collective-permute-start.19
  65.1 0.3 collective-permute-start.14
  65.4 0.6 collective-permute-done.20.refs_7_
  66.0 0.7 collective-permute-done.19.refs_5_
  66.7 0.3 collective-permute-done.16.refs_3_
  67.0 0.5 collective-permute-done.14.refs_1_
  67.5 6.7 %shard_map.65 = (bf16[640,384]{1,0:T(8,128)(2,1)S(1)}, f32[2,320,256]{2,1,0:T(8,128)S(1)}, f32[2,320,256]{2,1,0:T(8,128)S(1)}, f32[2,320,256]{2,1,0:T(8,128)S(1)...) custom-call(s32[2]{0:T(128)S(1)} %pad_add_fusion.1.place, ...), custom_call_target="tpu_custom_call" | custom-call | flops 4026531840 | bytes 8388608 | tf_op jit(solution)/shard_map/pallas_call | solution.py:200
  74.2 0.3 collective-permute-start.26
  74.5 3.1 %shard_map.66 = (f32[2,320,256]{2,1,0:T(8,128)S(1)}, f32[2,320,256]{2,1,0:T(8,128)S(1)}, f32[2,320,256]{2,1,0:T(8,128)S(1)}, f32[2,320,256]{2,1,0:T(8,128)S(1)}, bf16[4,2,320,256]{3,2,1,0:T(8,128)(2,1)}) custom-call(s32[2]{0:T(128)S(1)} %pad_add_fusion.1.place, bf16[640,384]{1,0:T(8,128)(2,1)S(1)} %get-tuple-element.50.act, ...), custom_call_target="tpu_custom_call" | custom-call | flops 1006632960 | bytes 8388608 | tf_op jit(solution)/shard_map/pallas_call | solution.py:200
  77.7 0.3 collective-permute-start.21
  78.0 0.9 fusion.11
  79.1 2.7 %collective-permute-start.27 = (bf16[2,320,256]{2,1,0:T(8,128)(2,1)}, bf16[2,320,256]{2,1,0:T(8,128)(2,1)}, u32[]{:S(2)}, u32[]{:S(2)}) collective-permute-start(bf16[2,320,256]{2,1,0:T(8,128)(2,1)} %fusion.11), channel_id=1, source_target_pairs={{0,48},{1,17},{2,50},{3,19},{4,52},{5,21},{6,54},{7,23},{8,56},{9,... | collective-permute-start | bytes 983048 | tf_op jit(solution)/shard_map/ppermute | solution.py:26
  81.8 1.2 fusion.15
  83.0 2.0 %collective-permute-start.22 = (bf16[2,320,256]{2,1,0:T(8,128)(2,1)S(1)}, bf16[2,320,256]{2,1,0:T(8,128)(2,1)S(1)}, u32[]{:S(2)}, u32[]{:S(2)}) collective-permute-start(bf16[2,320,256]{2,1,0:T(8,128)(2,1)S(1)} %fusion.15), channel_id=1, source_target_pairs={{0,48},{1,17},{2,50},{3,19},{4,52},{5,21},{6,54},{7,23},{8,56},{9,... | collective-permute-start | bytes 983048 | tf_op jit(solution)/shard_map/ppermute | solution.py:26
  85.0 2.8 %collective-permute-done.27 = bf16[2,320,256]{2,1,0:T(8,128)(2,1)} collective-permute-done((bf16[2,320,256]{2,1,0:T(8,128)(2,1)}, bf16[2,320,256]{2,1,0:T(8,128)(2,1)}, u32[]{:S(2)}, u32[]{:S(2)}) %collective-permute-start.27) | collective-permute-done | bytes 327712 | tf_op jit(solution)/shard_map/ppermute | solution.py:26
  87.7 1.4 %fusion.8 = (bf16[2,320,256]{2,1,0:T(8,128)(2,1)S(1)}, bf16[2,320,256]{2,1,0:T(8,128)(2,1)S(1)}) fusion(bf16[2,320,256]{2,1,0:T(8,128)(2,1)} %collective-permute-done.27, f32[2,320,256]{2,1,0:T(8,128)S(1)} %copy-done.3, bf16[4,2,320,256]{3,2,1,0:T(8,128)(2,1)} %copy-done.8, pred[]{:T(512)S(6)} %eq.111, f32[2,320,256]{2,1,0:T(8,128)S(1)} %copy-done.5), kind=kLoop, calls=%fused_computation.17 | loop fusion | flops 1802240 | bytes 2949121 | tf_op jit(solution)/shard_map/convert_element_type | solution.py:334
  89.4 2.7 %collective-permute-start.29 = (bf16[2,320,256]{2,1,0:T(8,128)(2,1)S(1)}, bf16[2,320,256]{2,1,0:T(8,128)(2,1)S(1)}, u32[]{:S(2)}, u32[]{:S(2)}) collective-permute-start(bf16[2,320,256]{2,1,0:T(8,128)(2,1)S(1)} %get-tuple-element.62), channel_id=1, source_target_pairs={{0,48},{1,49},{2,50},{3,51},{4,52},{5,53},{6,54},{7,55},{8,56},{9,... | collective-permute-start | bytes 983048 | tf_op jit(solution)/shard_map/ppermute | solution.py:26
  92.0 1.3 fusion.4
  93.4 1.4 %collective-permute-start.23 = (bf16[2,320,256]{2,1,0:T(8,128)(2,1)S(1)}, bf16[2,320,256]{2,1,0:T(8,128)(2,1)S(1)}, u32[]{:S(2)}, u32[]{:S(2)}) collective-permute-start(bf16[2,320,256]{2,1,0:T(8,128)(2,1)S(1)} %get-tuple-element.63), channel_id=1, source_target_pairs={{0,16},{1,17},{2,18},{3,19},{4,20},{5,21},{6,22},{7,23},{8,24},{9,... | collective-permute-start | bytes 983048 | tf_op jit(solution)/shard_map/ppermute | solution.py:26
  94.8 0.6 collective-permute-start.24
  95.4 4.5 %collective-permute-done.28 = bf16[2,320,256]{2,1,0:T(8,128)(2,1)S(1)} collective-permute-done((bf16[2,320,256]{2,1,0:T(8,128)(2,1)S(1)}, bf16[2,320,256]{2,1,0:T(8,128)(2,1)S(1)}, u32[]{:S(2)}, u32[]{:S(2)}) %collective-permute-start.28) | collective-permute-done | bytes 327712 | tf_op jit(solution)/shard_map/ppermute | solution.py:26
  99.9 1.3 collective-permute-done.29
  101.2 1.2 fusion.14
  102.4 6.0 %collective-permute-start.30 = (bf16[320,256]{1,0:T(8,128)(2,1)S(1)}, bf16[320,256]{1,0:T(8,128)(2,1)S(1)}, u32[]{:S(2)}, u32[]{:S(2)}) collective-permute-start(bf16[320,256]{1,0:T(8,128)(2,1)S(1)} %get-tuple-element.65), channel_id=1, source_target_pairs={{0,128},{1,129},{2,130},{3,131},{4,132},{5,133},{6,134},{7,135},{8... | collective-permute-start | bytes 491528 | tf_op jit(solution)/shard_map/ppermute | solution.py:26
  108.4 1.2 collective-permute-start.31
  109.6 1.1 fusion.17
  110.8 0.5 collective-permute-start.25
  111.4 2.9 %collective-permute-done.30 = bf16[320,256]{1,0:T(8,128)(2,1)S(1)} collective-permute-done((bf16[320,256]{1,0:T(8,128)(2,1)S(1)}, bf16[320,256]{1,0:T(8,128)(2,1)S(1)}, u32[]{:S(2)}, u32[]{:S(2)}) %collective-permute-start.30) | collective-permute-done | bytes 163872 | tf_op jit(solution)/shard_map/ppermute | solution.py:26
  114.3 2.3 %collective-permute-done.31 = bf16[320,256]{1,0:T(8,128)(2,1)S(1)} collective-permute-done((bf16[320,256]{1,0:T(8,128)(2,1)S(1)}, bf16[320,256]{1,0:T(8,128)(2,1)S(1)}, u32[]{:S(2)}, u32[]{:S(2)}) %collective-permute-start.31) | collective-permute-done | bytes 163872 | tf_op jit(solution)/shard_map/ppermute | solution.py:26
  116.5 1.2 collective-permute-done.25
  117.9 0.5 collective-permute-start.32
  118.4 4.4 %collective-permute-start.33 = (bf16[2,40,256]{2,1,0:T(8,128)(2,1)S(1)}, bf16[2,40,256]{2,1,0:T(8,128)(2,1)S(1)}, u32[]{:S(2)}, u32[]{:S(2)}) collective-permute-start(bf16[2,40,256]{2,1,0:T(8,128)(2,1)S(1)} %bitcast.151), channel_id=1, source_target_pairs={{0,4},{1,5},{2,6},{3,7},{4,0},{5,1},{6,2},{7,3},{8,12},{9,13},{10,... | collective-permute-start | bytes 122888 | tf_op jit(solution)/shard_map/ppermute | solution.py:26
  122.9 2.0 %collective-permute-done.33 = bf16[2,40,256]{2,1,0:T(8,128)(2,1)S(1)} collective-permute-done((bf16[2,40,256]{2,1,0:T(8,128)(2,1)S(1)}, bf16[2,40,256]{2,1,0:T(8,128)(2,1)S(1)}, u32[]{:S(2)}, u32[]{:S(2)}) %collective-permute-start.33) | collective-permute-done | bytes 40992 | tf_op jit(solution)/shard_map/ppermute | solution.py:26
  124.8 2.0 %collective-permute-done.34 = bf16[2,40,256]{2,1,0:T(8,128)(2,1)S(1)} collective-permute-done((bf16[2,40,256]{2,1,0:T(8,128)(2,1)S(1)}, bf16[2,40,256]{2,1,0:T(8,128)(2,1)S(1)}, u32[]{:S(2)}, u32[]{:S(2)}) %collective-permute-start.34) | collective-permute-done | bytes 40992 | tf_op jit(solution)/shard_map/ppermute | solution.py:26
  126.9 4.2 %collective-permute-start.35 = (bf16[4,40,256]{2,1,0:T(8,128)(2,1)S(1)}, bf16[4,40,256]{2,1,0:T(8,128)(2,1)S(1)}, u32[]{:S(2)}, u32[]{:S(2)}) collective-permute-start(bf16[4,40,256]{2,1,0:T(8,128)(2,1)S(1)} %get-tuple-element.68), channel_id=1, source_target_pairs={{0,8},{1,9},{2,10},{3,11},{4,12},{5,13},{6,14},{7,15},{8,0},{9,1},... | collective-permute-start | bytes 245768 | tf_op jit(solution)/shard_map/ppermute | solution.py:26
  131.2 4.1 %collective-permute-done.35 = bf16[4,40,256]{2,1,0:T(8,128)(2,1)S(1)} collective-permute-done((bf16[4,40,256]{2,1,0:T(8,128)(2,1)S(1)}, bf16[4,40,256]{2,1,0:T(8,128)(2,1)S(1)}, u32[]{:S(2)}, u32[]{:S(2)}) %collective-permute-start.35) | collective-permute-done | bytes 81952 | tf_op jit(solution)/shard_map/ppermute | solution.py:26
  135.6 0.9 fusion.2
  (94 shorter events, 3.1 us)
Async XLA Ops:
  0.0 10.9 %copy-start = (bf16[256,8]{0,1:T(8,128)(2,1)S(1)}, bf16[256,8]{0,1:T(8,128)(2,1)}, u32[]{:S(2)}) copy-start(bf16[256,8]{0,1:T(8,128)(2,1)} %param.10) | copy-start | bytes 12292
  1.7 10.0 %collective-permute-start = (bf16[144,256]{1,0:T(8,128)(2,1)S(1)}, bf16[144,256]{1,0:T(8,128)(2,1)S(1)}, u32[]{:S(2)}, u32[]{:S(2)}) collective-permute-start(bf16[144,256]{1,0:T(8,128)(2,1)S(1)} %fusion.38), channel_id=1, source_target_pairs={{0,8},{1,9},{2,10},{3,11},{4,12},{5,13},{6,14},{7,15},{8,0},{9,1},... | collective-permute-start | bytes 221192 | tf_op jit(solution)/shard_map/ppermute | solution.py:26
  12.2 4.1 %collective-permute-start.1 = (bf16[2,40,256]{2,1,0:T(8,128)(2,1)S(1)}, bf16[2,40,256]{2,1,0:T(8,128)(2,1)S(1)}, u32[]{:S(2)}, u32[]{:S(2)}) collective-permute-start(bf16[2,40,256]{2,1,0:T(8,128)(2,1)S(1)} %get-tuple-element.74), channel_id=1, source_target_pairs={{0,2},{1,3},{2,4},{3,5},{4,6},{5,7},{6,0},{7,1},{8,10},{9,11},{10,... | collective-permute-start | bytes 122888 | tf_op jit(solution)/shard_map/ppermute | solution.py:26
  13.5 5.5 %collective-permute-start.2 = (bf16[2,40,256]{2,1,0:T(8,128)(2,1)S(1)}, bf16[2,40,256]{2,1,0:T(8,128)(2,1)S(1)}, u32[]{:S(2)}, u32[]{:S(2)}) collective-permute-start(bf16[2,40,256]{2,1,0:T(8,128)(2,1)S(1)} %get-tuple-element.76), channel_id=1, source_target_pairs={{0,4},{1,5},{2,6},{3,7},{4,0},{5,1},{6,2},{7,3},{8,12},{9,13},{10,... | collective-permute-start | bytes 122888 | tf_op jit(solution)/shard_map/ppermute | solution.py:26
  14.3 4.7 %collective-permute-start.3 = (bf16[2,40,256]{2,1,0:T(8,128)(2,1)S(1)}, bf16[2,40,256]{2,1,0:T(8,128)(2,1)S(1)}, u32[]{:S(2)}, u32[]{:S(2)}) collective-permute-start(bf16[2,40,256]{2,1,0:T(8,128)(2,1)S(1)} %get-tuple-element.75), channel_id=1, source_target_pairs={{0,6},{1,7},{2,0},{3,1},{4,2},{5,3},{6,4},{7,5},{8,14},{9,15},{10,... | collective-permute-start | bytes 122888 | tf_op jit(solution)/shard_map/ppermute | solution.py:26
  19.1 5.5 %collective-permute-start.6 = (bf16[336,256]{1,0:T(8,128)(2,1)S(1)}, bf16[336,256]{1,0:T(8,128)(2,1)S(1)}, u32[]{:S(2)}, u32[]{:S(2)}) collective-permute-start(bf16[336,256]{1,0:T(8,128)(2,1)S(1)} %concatenate.24), channel_id=1, source_target_pairs={{0,64},{1,65},{2,66},{3,67},{4,68},{5,69},{6,70},{7,71},{8,72},{9,... | collective-permute-start | bytes 516104 | tf_op jit(solution)/shard_map/ppermute | solution.py:26
  24.7 16.9 %collective-permute-start.10 = (bf16[2,336,256]{2,1,0:T(8,128)(2,1)S(1)}, bf16[2,336,256]{2,1,0:T(8,128)(2,1)S(1)}, u32[]{:S(2)}, u32[]{:S(2)}) collective-permute-start(bf16[2,336,256]{2,1,0:T(8,128)(2,1)S(1)} %pad_maximum_fusion.1.refs_0_), channel_id=1, source_target_pairs={{0,48},{1,49},{2,50},{3,51},{4,52},{5,53},{6,54},{7,55},{8,56},{9,... | collective-permute-start | bytes 1032200 | tf_op jit(solution)/shard_map/ppermute | solution.py:26
  27.8 13.8 %collective-permute-start.8 = (bf16[2,336,256]{2,1,0:T(8,128)(2,1)S(1)}, bf16[2,336,256]{2,1,0:T(8,128)(2,1)S(1)}, u32[]{:S(2)}, u32[]{:S(2)}) collective-permute-start(bf16[2,336,256]{2,1,0:T(8,128)(2,1)S(1)} %pad_maximum_fusion.1.refs_0_), channel_id=1, source_target_pairs={{0,16},{1,17},{2,18},{3,19},{4,20},{5,21},{6,22},{7,23},{8,24},{9,... | collective-permute-start | bytes 1032200 | tf_op jit(solution)/shard_map/ppermute | solution.py:26
  27.9 12.9 %collective-permute-start.4 = (bf16[336,256]{1,0:T(8,128)(2,1)S(1)}, bf16[336,256]{1,0:T(8,128)(2,1)S(1)}, u32[]{:S(2)}, u32[]{:S(2)}) collective-permute-start(bf16[336,256]{1,0:T(8,128)(2,1)S(1)} %concatenate.24), channel_id=1, source_target_pairs={{0,128},{1,129},{2,130},{3,131},{4,132},{5,133},{6,134},{7,135},{8... | collective-permute-start | bytes 516104 | tf_op jit(solution)/shard_map/ppermute | solution.py:26
  31.8 9.0 %collective-permute-start.5 = (bf16[336,256]{1,0:T(8,128)(2,1)S(1)}, bf16[336,256]{1,0:T(8,128)(2,1)S(1)}, u32[]{:S(2)}, u32[]{:S(2)}) collective-permute-start(bf16[336,256]{1,0:T(8,128)(2,1)S(1)} %concatenate.24), channel_id=1, source_target_pairs={{0,192},{1,193},{2,194},{3,195},{4,196},{5,197},{6,198},{7,199},{8... | collective-permute-start | bytes 516104 | tf_op jit(solution)/shard_map/ppermute | solution.py:26
  40.9 12.3 %copy-start.6 = (bf16[2,336,256]{2,1,0:T(8,128)(2,1)}, bf16[2,336,256]{2,1,0:T(8,128)(2,1)S(1)}, u32[]{:S(2)}) copy-start(bf16[2,336,256]{2,1,0:T(8,128)(2,1)S(1)} %pad_maximum_fusion.refs_0_) | copy-start | bytes 1032196
  40.9 8.5 %collective-permute-start.17 = (bf16[2,336,256]{2,1,0:T(8,128)(2,1)S(1)}, bf16[2,336,256]{2,1,0:T(8,128)(2,1)S(1)}, u32[]{:S(2)}, u32[]{:S(2)}) collective-permute-start(bf16[2,336,256]{2,1,0:T(8,128)(2,1)S(1)} %pad_maximum_fusion.refs_0_), channel_id=1, source_target_pairs={{0,48},{1,49},{2,50},{3,51},{4,52},{5,53},{6,54},{7,55},{8,56},{9,... | collective-permute-start | bytes 1032200 | tf_op jit(solution)/shard_map/ppermute | solution.py:26
  41.6 11.5 %collective-permute-start.11 = (bf16[2,336,256]{2,1,0:T(8,128)(2,1)S(1)}, bf16[2,336,256]{2,1,0:T(8,128)(2,1)S(1)}, u32[]{:S(2)}, u32[]{:S(2)}) collective-permute-start(bf16[2,336,256]{2,1,0:T(8,128)(2,1)S(1)} %broadcast_select_fusion.1), channel_id=1, source_target_pairs={{0,48},{1,17},{2,50},{3,19},{4,52},{5,21},{6,54},{7,23},{8,56},{9,... | collective-permute-start | bytes 1032200 | tf_op jit(solution)/shard_map/ppermute | solution.py:26
  44.3 8.8 %collective-permute-start.15 = (bf16[2,336,256]{2,1,0:T(8,128)(2,1)S(1)}, bf16[2,336,256]{2,1,0:T(8,128)(2,1)S(1)}, u32[]{:S(2)}, u32[]{:S(2)}) collective-permute-start(bf16[2,336,256]{2,1,0:T(8,128)(2,1)S(1)} %pad_maximum_fusion.refs_0_), channel_id=1, source_target_pairs={{0,16},{1,17},{2,18},{3,19},{4,20},{5,21},{6,22},{7,23},{8,24},{9,... | collective-permute-start | bytes 1032200 | tf_op jit(solution)/shard_map/ppermute | solution.py:26
  44.9 13.7 %collective-permute-start.7 = (bf16[2,336,256]{2,1,0:T(8,128)(2,1)S(1)}, bf16[2,336,256]{2,1,0:T(8,128)(2,1)S(1)}, u32[]{:S(2)}, u32[]{:S(2)}) collective-permute-start(bf16[2,336,256]{2,1,0:T(8,128)(2,1)S(1)} %pad_maximum_fusion.1.refs_0_), channel_id=1, source_target_pairs={{0,1},{1,0},{2,3},{3,2},{4,5},{5,4},{6,7},{7,6},{8,9},{9,8},{10,11... | collective-permute-start | bytes 1032200 | tf_op jit(solution)/shard_map/ppermute | solution.py:26
  44.9 13.7 %collective-permute-start.13 = (bf16[2,336,256]{2,1,0:T(8,128)(2,1)S(1)}, bf16[2,336,256]{2,1,0:T(8,128)(2,1)S(1)}, u32[]{:S(2)}, u32[]{:S(2)}) collective-permute-start(bf16[2,336,256]{2,1,0:T(8,128)(2,1)S(1)} %collective-permute-done.10.refs_6_), channel_id=1, source_target_pairs={{0,1},{1,0},{2,3},{3,2},{4,5},{5,4},{6,7},{7,6},{8,9},{9,8},{10,11... | collective-permute-start | bytes 1032200 | tf_op jit(solution)/shard_map/ppermute | solution.py:26
  49.4 9.2 %collective-permute-start.9 = (bf16[2,336,256]{2,1,0:T(8,128)(2,1)S(1)}, bf16[2,336,256]{2,1,0:T(8,128)(2,1)S(1)}, u32[]{:S(2)}, u32[]{:S(2)}) collective-permute-start(bf16[2,336,256]{2,1,0:T(8,128)(2,1)S(1)} %collective-permute-done.8.refs_2_), channel_id=1, source_target_pairs={{0,1},{1,0},{2,3},{3,2},{4,5},{5,4},{6,7},{7,6},{8,9},{9,8},{10,11... | collective-permute-start | bytes 1032200 | tf_op jit(solution)/shard_map/ppermute | solution.py:26
  53.1 5.5 %collective-permute-start.12 = (bf16[2,336,256]{2,1,0:T(8,128)(2,1)S(1)}, bf16[2,336,256]{2,1,0:T(8,128)(2,1)S(1)}, u32[]{:S(2)}, u32[]{:S(2)}) collective-permute-start(bf16[2,336,256]{2,1,0:T(8,128)(2,1)S(1)} %collective-permute-done.11.refs_4_), channel_id=1, source_target_pairs={{0,1},{1,0},{2,3},{3,2},{4,5},{5,4},{6,7},{7,6},{8,9},{9,8},{10,11... | collective-permute-start | bytes 1032200 | tf_op jit(solution)/shard_map/ppermute | solution.py:26
  53.9 10.6 %collective-permute-start.18 = (bf16[2,336,256]{2,1,0:T(8,128)(2,1)}, bf16[2,336,256]{2,1,0:T(8,128)(2,1)}, u32[]{:S(2)}, u32[]{:S(2)}) collective-permute-start(bf16[2,336,256]{2,1,0:T(8,128)(2,1)} %broadcast_select_fusion), channel_id=1, source_target_pairs={{0,48},{1,17},{2,50},{3,19},{4,52},{5,21},{6,54},{7,23},{8,56},{9,... | collective-permute-start | bytes 1032200 | tf_op jit(solution)/shard_map/ppermute | solution.py:26
  54.6 4.1 %copy-start.1 = (bf16[1,384,4096]{2,1,0:T(8,128)(2,1)S(1)}, bf16[1,384,4096]{2,1,0:T(8,128)(2,1)}, u32[]{:S(2)}) copy-start(bf16[1,384,4096]{2,1,0:T(8,128)(2,1)} %param.12) | copy-start | bytes 9437188
  58.6 6.4 %copy-start.7 = (bf16[2,336,256]{2,1,0:T(8,128)(2,1)S(1)}, bf16[2,336,256]{2,1,0:T(8,128)(2,1)}, u32[]{:S(2)}) copy-start(bf16[2,336,256]{2,1,0:T(8,128)(2,1)} %copy-done.6) | copy-start | bytes 1032196
  64.2 1.7 %collective-permute-start.20 = (bf16[2,336,256]{2,1,0:T(8,128)(2,1)S(1)}, bf16[2,336,256]{2,1,0:T(8,128)(2,1)S(1)}, u32[]{:S(2)}, u32[]{:S(2)}) collective-permute-start(bf16[2,336,256]{2,1,0:T(8,128)(2,1)S(1)} %collective-permute-done.17.refs_6_), channel_id=1, source_target_pairs={{0,1},{1,0},{2,3},{3,2},{4,5},{5,4},{6,7},{7,6},{8,9},{9,8},{10,11... | collective-permute-start | bytes 1032200 | tf_op jit(solution)/shard_map/ppermute | solution.py:26
  64.5 2.1 %collective-permute-start.19 = (bf16[2,336,256]{2,1,0:T(8,128)(2,1)}, bf16[2,336,256]{2,1,0:T(8,128)(2,1)S(1)}, u32[]{:S(2)}, u32[]{:S(2)}) collective-permute-start(bf16[2,336,256]{2,1,0:T(8,128)(2,1)} %collective-permute-done.18.refs_4_), channel_id=1, source_target_pairs={{0,1},{1,0},{2,3},{3,2},{4,5},{5,4},{6,7},{7,6},{8,9},{9,8},{10,11... | collective-permute-start | bytes 1032200 | tf_op jit(solution)/shard_map/ppermute | solution.py:26
  64.8 2.1 %collective-permute-start.16 = (bf16[2,336,256]{2,1,0:T(8,128)(2,1)S(1)}, bf16[2,336,256]{2,1,0:T(8,128)(2,1)S(1)}, u32[]{:S(2)}, u32[]{:S(2)}) collective-permute-start(bf16[2,336,256]{2,1,0:T(8,128)(2,1)S(1)} %collective-permute-done.15.refs_2_), channel_id=1, source_target_pairs={{0,1},{1,0},{2,3},{3,2},{4,5},{5,4},{6,7},{7,6},{8,9},{9,8},{10,11... | collective-permute-start | bytes 1032200 | tf_op jit(solution)/shard_map/ppermute | solution.py:26
  65.1 2.4 %collective-permute-start.14 = (bf16[2,336,256]{2,1,0:T(8,128)(2,1)S(1)}, bf16[2,336,256]{2,1,0:T(8,128)(2,1)S(1)}, u32[]{:S(2)}, u32[]{:S(2)}) collective-permute-start(bf16[2,336,256]{2,1,0:T(8,128)(2,1)S(1)} %copy-done.7), channel_id=1, source_target_pairs={{0,1},{1,0},{2,3},{3,2},{4,5},{5,4},{6,7},{7,6},{8,9},{9,8},{10,11... | collective-permute-start | bytes 1032200 | tf_op jit(solution)/shard_map/ppermute | solution.py:26
  74.2 3.5 %copy-start.2 = (f32[2,320,256]{2,1,0:T(8,128)}, f32[2,320,256]{2,1,0:T(8,128)S(1)}, u32[]{:S(2)}) copy-start(f32[2,320,256]{2,1,0:T(8,128)S(1)} %get-tuple-element.58) | copy-start | bytes 1966084
  74.2 3.4 %copy-start.4 = (f32[2,320,256]{2,1,0:T(8,128)}, f32[2,320,256]{2,1,0:T(8,128)S(1)}, u32[]{:S(2)}) copy-start(f32[2,320,256]{2,1,0:T(8,128)S(1)} %get-tuple-element.60) | copy-start | bytes 1966084
  74.2 3.7 %collective-permute-start.26 = (bf16[4,2,320,256]{3,2,1,0:T(8,128)(2,1)S(1)}, bf16[4,2,320,256]{3,2,1,0:T(8,128)(2,1)S(1)}, u32[]{:S(2)}, u32[]{:S(2)}) collective-permute-start(bf16[4,2,320,256]{3,2,1,0:T(8,128)(2,1)S(1)} %get-tuple-element.57), channel_id=1, source_target_pairs={{0,1},{1,0},{2,3},{3,2},{4,5},{5,4},{6,7},{7,6},{8,9},{9,8},{10,11... | collective-permute-start | bytes 3932168 | tf_op jit(solution)/shard_map/ppermute | solution.py:26
  77.7 4.2 %collective-permute-start.21 = (bf16[4,2,320,256]{3,2,1,0:T(8,128)(2,1)}, bf16[4,2,320,256]{3,2,1,0:T(8,128)(2,1)}, u32[]{:S(2)}, u32[]{:S(2)}) collective-permute-start(bf16[4,2,320,256]{3,2,1,0:T(8,128)(2,1)} %get-tuple-element.52), channel_id=1, source_target_pairs={{0,1},{1,0},{2,3},{3,2},{4,5},{5,4},{6,7},{7,6},{8,9},{9,8},{10,11... | collective-permute-start | bytes 3932168 | tf_op jit(solution)/shard_map/ppermute | solution.py:26
  78.0 1.2 copy-start.8
  79.1 8.6 %collective-permute-start.27 = (bf16[2,320,256]{2,1,0:T(8,128)(2,1)}, bf16[2,320,256]{2,1,0:T(8,128)(2,1)}, u32[]{:S(2)}, u32[]{:S(2)}) collective-permute-start(bf16[2,320,256]{2,1,0:T(8,128)(2,1)} %fusion.11), channel_id=1, source_target_pairs={{0,48},{1,17},{2,50},{3,19},{4,52},{5,21},{6,54},{7,23},{8,56},{9,... | collective-permute-start | bytes 983048 | tf_op jit(solution)/shard_map/ppermute | solution.py:26
  81.8 5.9 %copy-start.3 = (f32[2,320,256]{2,1,0:T(8,128)S(1)}, f32[2,320,256]{2,1,0:T(8,128)}, u32[]{:S(2)}) copy-start(f32[2,320,256]{2,1,0:T(8,128)} %copy-done.2) | copy-start | bytes 1966084
  81.8 5.9 %copy-start.5 = (f32[2,320,256]{2,1,0:T(8,128)S(1)}, f32[2,320,256]{2,1,0:T(8,128)}, u32[]{:S(2)}) copy-start(f32[2,320,256]{2,1,0:T(8,128)} %copy-done.4) | copy-start | bytes 1966084
  83.0 9.0 %collective-permute-start.22 = (bf16[2,320,256]{2,1,0:T(8,128)(2,1)S(1)}, bf16[2,320,256]{2,1,0:T(8,128)(2,1)S(1)}, u32[]{:S(2)}, u32[]{:S(2)}) collective-permute-start(bf16[2,320,256]{2,1,0:T(8,128)(2,1)S(1)} %fusion.15), channel_id=1, source_target_pairs={{0,48},{1,17},{2,50},{3,19},{4,52},{5,21},{6,54},{7,23},{8,56},{9,... | collective-permute-start | bytes 983048 | tf_op jit(solution)/shard_map/ppermute | solution.py:26
  89.2 10.7 %collective-permute-start.28 = (bf16[2,320,256]{2,1,0:T(8,128)(2,1)S(1)}, bf16[2,320,256]{2,1,0:T(8,128)(2,1)S(1)}, u32[]{:S(2)}, u32[]{:S(2)}) collective-permute-start(bf16[2,320,256]{2,1,0:T(8,128)(2,1)S(1)} %get-tuple-element.61), channel_id=1, source_target_pairs={{0,16},{1,17},{2,18},{3,19},{4,20},{5,21},{6,22},{7,23},{8,24},{9,... | collective-permute-start | bytes 983048 | tf_op jit(solution)/shard_map/ppermute | solution.py:26
  89.4 11.9 %collective-permute-start.29 = (bf16[2,320,256]{2,1,0:T(8,128)(2,1)S(1)}, bf16[2,320,256]{2,1,0:T(8,128)(2,1)S(1)}, u32[]{:S(2)}, u32[]{:S(2)}) collective-permute-start(bf16[2,320,256]{2,1,0:T(8,128)(2,1)S(1)} %get-tuple-element.62), channel_id=1, source_target_pairs={{0,48},{1,49},{2,50},{3,51},{4,52},{5,53},{6,54},{7,55},{8,56},{9,... | collective-permute-start | bytes 983048 | tf_op jit(solution)/shard_map/ppermute | solution.py:26
  93.4 16.3 %collective-permute-start.23 = (bf16[2,320,256]{2,1,0:T(8,128)(2,1)S(1)}, bf16[2,320,256]{2,1,0:T(8,128)(2,1)S(1)}, u32[]{:S(2)}, u32[]{:S(2)}) collective-permute-start(bf16[2,320,256]{2,1,0:T(8,128)(2,1)S(1)} %get-tuple-element.63), channel_id=1, source_target_pairs={{0,16},{1,17},{2,18},{3,19},{4,20},{5,21},{6,22},{7,23},{8,24},{9,... | collective-permute-start | bytes 983048 | tf_op jit(solution)/shard_map/ppermute | solution.py:26
  94.8 14.9 %collective-permute-start.24 = (bf16[2,320,256]{2,1,0:T(8,128)(2,1)S(1)}, bf16[2,320,256]{2,1,0:T(8,128)(2,1)S(1)}, u32[]{:S(2)}, u32[]{:S(2)}) collective-permute-start(bf16[2,320,256]{2,1,0:T(8,128)(2,1)S(1)} %get-tuple-element.64), channel_id=1, source_target_pairs={{0,48},{1,49},{2,50},{3,51},{4,52},{5,53},{6,54},{7,55},{8,56},{9,... | collective-permute-start | bytes 983048 | tf_op jit(solution)/shard_map/ppermute | solution.py:26
  102.4 11.9 %collective-permute-start.30 = (bf16[320,256]{1,0:T(8,128)(2,1)S(1)}, bf16[320,256]{1,0:T(8,128)(2,1)S(1)}, u32[]{:S(2)}, u32[]{:S(2)}) collective-permute-start(bf16[320,256]{1,0:T(8,128)(2,1)S(1)} %get-tuple-element.65), channel_id=1, source_target_pairs={{0,128},{1,129},{2,130},{3,131},{4,132},{5,133},{6,134},{7,135},{8... | collective-permute-start | bytes 491528 | tf_op jit(solution)/shard_map/ppermute | solution.py:26
  108.4 8.1 %collective-permute-start.31 = (bf16[320,256]{1,0:T(8,128)(2,1)S(1)}, bf16[320,256]{1,0:T(8,128)(2,1)S(1)}, u32[]{:S(2)}, u32[]{:S(2)}) collective-permute-start(bf16[320,256]{1,0:T(8,128)(2,1)S(1)} %get-tuple-element.66), channel_id=1, source_target_pairs={{0,192},{1,193},{2,194},{3,195},{4,196},{5,197},{6,198},{7,199},{8... | collective-permute-start | bytes 491528 | tf_op jit(solution)/shard_map/ppermute | solution.py:26
  109.6 1.7 %copy-start.10 = (s32[128,2]{0,1:T(2,128)S(1)}, s32[128,2]{0,1:T(2,128)}, u32[]{:S(2)}) copy-start(s32[128,2]{0,1:T(2,128)} %param.13) | copy-start | bytes 3076
  110.8 24.8 %copy-start.9 = (bf16[128,256]{1,0:T(8,128)(2,1)S(1)}, bf16[128,256]{1,0:T(8,128)(2,1)}, u32[]{:S(2)}) copy-start(bf16[128,256]{1,0:T(8,128)(2,1)} %param.8) | copy-start | bytes 196612
  110.8 7.0 %collective-permute-start.25 = (bf16[320,256]{1,0:T(8,128)(2,1)S(1)}, bf16[320,256]{1,0:T(8,128)(2,1)S(1)}, u32[]{:S(2)}, u32[]{:S(2)}) collective-permute-start(bf16[320,256]{1,0:T(8,128)(2,1)S(1)} %fusion.23), channel_id=1, source_target_pairs={{0,64},{1,65},{2,66},{3,67},{4,68},{5,69},{6,70},{7,71},{8,72},{9,... | collective-permute-start | bytes 491528 | tf_op jit(solution)/shard_map/ppermute | solution.py:26
  117.9 5.0 %collective-permute-start.32 = (bf16[2,40,256]{2,1,0:T(8,128)(2,1)S(1)}, bf16[2,40,256]{2,1,0:T(8,128)(2,1)S(1)}, u32[]{:S(2)}, u32[]{:S(2)}) collective-permute-start(bf16[2,40,256]{2,1,0:T(8,128)(2,1)S(1)} %bitcast.153), channel_id=1, source_target_pairs={{0,6},{1,7},{2,0},{3,1},{4,2},{5,3},{6,4},{7,5},{8,14},{9,15},{10,... | collective-permute-start | bytes 122888 | tf_op jit(solution)/shard_map/ppermute | solution.py:26
  118.4 6.4 %collective-permute-start.33 = (bf16[2,40,256]{2,1,0:T(8,128)(2,1)S(1)}, bf16[2,40,256]{2,1,0:T(8,128)(2,1)S(1)}, u32[]{:S(2)}, u32[]{:S(2)}) collective-permute-start(bf16[2,40,256]{2,1,0:T(8,128)(2,1)S(1)} %bitcast.151), channel_id=1, source_target_pairs={{0,4},{1,5},{2,6},{3,7},{4,0},{5,1},{6,2},{7,3},{8,12},{9,13},{10,... | collective-permute-start | bytes 122888 | tf_op jit(solution)/shard_map/ppermute | solution.py:26
  122.9 4.0 %collective-permute-start.34 = (bf16[2,40,256]{2,1,0:T(8,128)(2,1)S(1)}, bf16[2,40,256]{2,1,0:T(8,128)(2,1)S(1)}, u32[]{:S(2)}, u32[]{:S(2)}) collective-permute-start(bf16[2,40,256]{2,1,0:T(8,128)(2,1)S(1)} %bitcast.149), channel_id=1, source_target_pairs={{0,2},{1,3},{2,4},{3,5},{4,6},{5,7},{6,0},{7,1},{8,10},{9,11},{10,... | collective-permute-start | bytes 122888 | tf_op jit(solution)/shard_map/ppermute | solution.py:26
  126.9 8.4 %collective-permute-start.35 = (bf16[4,40,256]{2,1,0:T(8,128)(2,1)S(1)}, bf16[4,40,256]{2,1,0:T(8,128)(2,1)S(1)}, u32[]{:S(2)}, u32[]{:S(2)}) collective-permute-start(bf16[4,40,256]{2,1,0:T(8,128)(2,1)S(1)} %get-tuple-element.68), channel_id=1, source_target_pairs={{0,8},{1,9},{2,10},{3,11},{4,12},{5,13},{6,14},{7,15},{8,0},{9,1},... | collective-permute-start | bytes 245768 | tf_op jit(solution)/shard_map/ppermute | solution.py:26
